TPU v7x, 32 devices: a whole 2x2x4 slice. The times are simulated.
32 devices in a mesh: seq: 4 (over y, x), fsdp: 8 (over z, core).
Axes of the slice: x: 2, y: 2, z: 4, core: 2. Of those that a mesh axis runs over, the one named last changes fastest.
Arguments:
- hidden_in: bfloat16 [8, 512, 2048], P('fsdp', 'seq'), may hold values from -6 to 6
- norm_one: bfloat16 [2048], P('fsdp'), may hold values from 0.5 to 1.5
- w_qkv: bfloat16 [2048, 6144], P('fsdp'), may hold values from -0.125 to 0.125
- w_out: bfloat16 [2048, 2048], P('fsdp'), may hold values from -1 to 1
- norm_two: bfloat16 [2048], P('fsdp'), may hold values from 0.5 to 1.5
- w_gate_up: bfloat16 [2048, 16384], P('fsdp'), may hold values from -0.125 to 0.125
- w_down: bfloat16 [8192, 2048], P('fsdp'), may hold values from -0.0625 to 0.0625
- grad_out: bfloat16 [8, 512, 2048], P('fsdp', 'seq'), may hold values from -6 to 6
Outputs:
- out_hidden: bfloat16 [8, 512, 2048], P('fsdp', 'seq')
- grad_input: float32 [8, 512, 2048], P('fsdp', 'seq')
- grad_norm_one: float32 [2048], P('fsdp')
- grad_qkv: float32 [2048, 6144], P('fsdp')
- grad_out_proj: float32 [2048, 2048], P('fsdp')
- grad_norm_two: float32 [2048], P('fsdp')
- grad_gate_up: float32 [2048, 16384], P('fsdp')
- grad_down: float32 [8192, 2048], P('fsdp')
All inputs are finite; a program needn't handle non-finite values.
Results may differ from a plain program's by a relative error of at most 0.02.
Values may be sent and summed in bfloat16 or wider, within the bound.
No kernel may reach another device: no remote copies, remote signals or barrier semaphores. Data moves between devices by JAX's collectives and lax.ppermute only.
A program may use at most 576 MiB of HBM per device.

v0:
```python
import jax
import jax.numpy as jnp
from jax import lax
from jax.sharding import PartitionSpec as P

HEAD_DIM = 64


EPSILON = 1e-05
THETA = 130000.0
SCALE = 0.125


def outer_sum(left, right):
    return lax.dot_general(
        left, right, (((0,), (0,)), ((), ())), preferred_element_type=jnp.float32
    )


def back_product(grad, weight):
    return lax.dot_general(
        grad, weight, (((1,), (1,)), ((), ())), preferred_element_type=jnp.float32
    )


def rope_tables(length):
    half = HEAD_DIM // 2
    freqs = THETA ** (-(jnp.arange(half, dtype=jnp.float32) * 2.0) / HEAD_DIM)
    angles = jnp.arange(length, dtype=jnp.float32)[:, None] * freqs[None, :]
    angles = jnp.concatenate([angles, angles], axis=1)
    return (jnp.cos(angles)[:, None, :], jnp.sin(angles)[:, None, :])


def rotate(values, cosine, sine):
    half = values.shape[-1] // 2
    turned = jnp.concatenate([-values[..., half:], values[..., :half]], axis=-1)
    return values * cosine + turned * sine


def unrotate(grads, cosine, sine):
    half = grads.shape[-1] // 2
    scaled = grads * sine
    turned = jnp.concatenate([scaled[..., half:], -scaled[..., :half]], axis=-1)
    return grads * cosine + turned


def norm_forward(values, gain):
    factor = lax.rsqrt(jnp.mean(values * values, axis=-1, keepdims=True) + EPSILON)
    return (values * factor * gain, factor)


def norm_backward(values, factor, gain, grad):
    grad_gain = jnp.sum(grad * values * factor, axis=0)
    scaled = grad * gain
    grad_values = factor * scaled - values * factor**3 * jnp.mean(
        scaled * values, axis=-1, keepdims=True
    )
    return (grad_values, grad_gain)


def fetch_rows(gain, first, second):
    return (
        lax.all_gather(gain, "fsdp", axis=0, tiled=True),
        lax.all_gather(first, "fsdp", axis=0, tiled=True),
        lax.all_gather(second, "fsdp", axis=0, tiled=True),
    )


def weight_term(left, right):
    return outer_sum(left, right)


def reduce_grads(terms):
    partial_sums = (
        lax.psum_scatter(
            terms[0].astype(jnp.bfloat16), "fsdp", scatter_dimension=0, tiled=True
        ).astype(jnp.float32),
        lax.psum_scatter(
            terms[1].astype(jnp.bfloat16), "fsdp", scatter_dimension=0, tiled=True
        ).astype(jnp.float32),
    )
    return (
        lax.psum(partial_sums[0].astype(jnp.bfloat16), "seq").astype(jnp.float32),
        lax.psum(partial_sums[1].astype(jnp.bfloat16), "seq").astype(jnp.float32),
    )


def block_scores(query_block, key_rows, offset):
    scores = (
        jnp.einsum("qhd,khd->hqk", query_block, key_rows, preferred_element_type=jnp.float32)
        * SCALE
    )
    rows = offset + jnp.arange(query_block.shape[0])[:, None]
    columns = jnp.arange(key_rows.shape[0])[None, :]
    return jnp.where((columns <= rows)[None], scores, -1e30)


def on_device(hidden_in, norm_one, w_qkv, w_out, norm_two, w_gate_up, w_down, grad_out):
    inputs = hidden_in[0].astype(jnp.float32)
    tokens = inputs.shape[0]
    width = inputs.shape[1]
    gain_one, qkv_full, out_full = fetch_rows(norm_one, w_qkv, w_out)
    normed, factor_one = norm_forward(inputs, gain_one.astype(jnp.float32))
    normed_low = normed.astype(jnp.bfloat16)
    mixed = jnp.dot(normed_low, qkv_full, preferred_element_type=jnp.float32).astype(jnp.bfloat16)
    regrouped = lax.all_to_all(
        mixed.reshape(tokens, 3, width), "seq", split_axis=2, concat_axis=0, tiled=True
    )
    length = regrouped.shape[0]
    local_width = regrouped.shape[2]
    heads = local_width // HEAD_DIM
    regrouped = regrouped.reshape(length, 3, heads, HEAD_DIM)
    cosine, sine = rope_tables(length)
    query = rotate(regrouped[:, 0].astype(jnp.float32), cosine, sine).astype(jnp.bfloat16)
    keys = rotate(regrouped[:, 1].astype(jnp.float32), cosine, sine).astype(jnp.bfloat16)
    values = regrouped[:, 2]
    block = min(512, length)
    attended_parts = []
    logsums = []
    for start in range(0, length, block):
        stop = start + block
        scores = block_scores(query[start:stop], keys[:stop], start)
        highest = jnp.max(scores, axis=-1, keepdims=True)
        weights = jnp.exp(scores - highest)
        total = jnp.sum(weights, axis=-1, keepdims=True)
        probabilities = (weights / total).astype(jnp.bfloat16)
        logsums.append(highest + jnp.log(total))
        attended_parts.append(
            jnp.einsum(
                "hqk,khd->qhd", probabilities, values[:stop], preferred_element_type=jnp.float32
            )
        )
    attended = (
        jnp.concatenate(attended_parts, axis=0).reshape(length, local_width).astype(jnp.bfloat16)
    )
    back_rows = lax.all_to_all(attended, "seq", split_axis=0, concat_axis=1, tiled=True)
    middle = inputs + jnp.dot(back_rows, out_full, preferred_element_type=jnp.float32)
    gain_two, gate_up_full, down_full = fetch_rows(norm_two, w_gate_up, w_down)
    normed_two, factor_two = norm_forward(middle, gain_two.astype(jnp.float32))
    normed_two_low = normed_two.astype(jnp.bfloat16)
    gate_up = jnp.dot(normed_two_low, gate_up_full, preferred_element_type=jnp.float32)
    hidden_units = gate_up.shape[1] // 2
    gate = gate_up[:, :hidden_units]
    upward = gate_up[:, hidden_units:]
    sigmoid = jax.nn.sigmoid(gate)
    activated = gate * sigmoid
    hidden = (activated * upward).astype(jnp.bfloat16)
    output = middle + jnp.dot(hidden, down_full, preferred_element_type=jnp.float32)
    cotangent = grad_out[0]
    grad_hidden = back_product(cotangent, down_full)
    grad_gate = grad_hidden * upward * sigmoid * (1.0 + gate * (1.0 - sigmoid))
    grad_upward = grad_hidden * activated
    grad_gate_up_low = jnp.concatenate([grad_gate, grad_upward], axis=1).astype(jnp.bfloat16)
    grad_normed_two = back_product(grad_gate_up_low, gate_up_full)
    middle_part, grad_gain_two = norm_backward(
        middle, factor_two, gain_two.astype(jnp.float32), grad_normed_two
    )
    grad_middle = cotangent.astype(jnp.float32) + middle_part
    grad_gate_up_term = weight_term(normed_two_low, grad_gate_up_low)
    grad_branch = grad_middle.astype(jnp.bfloat16)
    grad_out_term = weight_term(back_rows, grad_branch)
    grad_down_term = weight_term(hidden, cotangent)
    grad_down_sum, gain_two_sum = reduce_grads((grad_down_term, grad_gain_two))
    gate_up_sum, out_proj_sum = reduce_grads((grad_gate_up_term, grad_out_term))
    gain_one, qkv_full, out_full = fetch_rows(norm_one, w_qkv, w_out)
    grad_attended = back_product(grad_branch, out_full).astype(jnp.bfloat16)
    grad_heads = lax.all_to_all(
        grad_attended, "seq", split_axis=1, concat_axis=0, tiled=True
    ).reshape(length, heads, HEAD_DIM)
    query_parts = []
    grad_keys = jnp.zeros((length, heads, HEAD_DIM), jnp.float32)
    grad_values = jnp.zeros((length, heads, HEAD_DIM), jnp.float32)
    for index, start in enumerate(range(0, length, block)):
        stop = start + block
        query_block = query[start:stop]
        grad_block = grad_heads[start:stop]
        scores = block_scores(query_block, keys[:stop], start)
        probabilities = jnp.exp(scores - logsums[index])
        grad_probabilities = jnp.einsum(
            "qhd,khd->hqk", grad_block, values[:stop], preferred_element_type=jnp.float32
        )
        inner = jnp.sum(probabilities * grad_probabilities, axis=-1, keepdims=True)
        grad_scores = (probabilities * (grad_probabilities - inner)).astype(jnp.bfloat16)
        query_parts.append(
            jnp.einsum("hqk,khd->qhd", grad_scores, keys[:stop], preferred_element_type=jnp.float32)
            * SCALE
        )
        key_term = (
            jnp.einsum("hqk,qhd->khd", grad_scores, query_block, preferred_element_type=jnp.float32)
            * SCALE
        )
        value_term = jnp.einsum(
            "hqk,qhd->khd",
            probabilities.astype(jnp.bfloat16),
            grad_block,
            preferred_element_type=jnp.float32,
        )
        grad_keys = grad_keys.at[:stop].add(key_term)
        grad_values = grad_values.at[:stop].add(value_term)
    grad_query = unrotate(jnp.concatenate(query_parts, axis=0), cosine, sine)
    grad_keys = unrotate(grad_keys, cosine, sine)
    stacked = (
        jnp.stack([grad_query, grad_keys, grad_values], axis=1)
        .astype(jnp.bfloat16)
        .reshape(length, 3, local_width)
    )
    grad_mixed = lax.all_to_all(stacked, "seq", split_axis=0, concat_axis=2, tiled=True).reshape(
        tokens, 3 * width
    )
    grad_qkv_term = weight_term(normed_low, grad_mixed)
    grad_normed_one = back_product(grad_mixed, qkv_full)
    input_part, grad_gain_one = norm_backward(
        inputs, factor_one, gain_one.astype(jnp.float32), grad_normed_one
    )
    grad_inputs = grad_middle + input_part
    qkv_sum, gain_one_sum = reduce_grads((grad_qkv_term, grad_gain_one))
    return (
        output.astype(jnp.bfloat16)[None],
        grad_inputs[None],
        gain_one_sum,
        qkv_sum,
        out_proj_sum,
        gain_two_sum,
        gate_up_sum,
        grad_down_sum,
    )


def solution(mesh):
    placed = (
        P("fsdp", "seq", None),
        P("fsdp"),
        P("fsdp", None),
        P("fsdp", None),
        P("fsdp"),
        P("fsdp", None),
        P("fsdp", None),
        P("fsdp", "seq", None),
    )
    return jax.shard_map(
        on_device,
        mesh=mesh,
        in_specs=placed,
        out_specs=(
            P("fsdp", "seq", None),
            P("fsdp", "seq", None),
            P("fsdp"),
            P("fsdp", None),
            P("fsdp", None),
            P("fsdp"),
            P("fsdp", None),
            P("fsdp", None),
        ),
        check_vma=False,
    )
```

profile of v0, /device:TPU:0, one launch (start us, length us, event | category | flops | bytes accessed | tf_op | source)
XLA Modules:
  0.0 2872.6 jit_solution(16259498665658700247)
XLA Ops:
  10.0 13.4 all-gather
  24.2 208.1 %all-gather.7.cloned.1.call-done = bf16[2048,6144]{1,0:T(8,128)(2,1)} async-done(((bf16[256,6144]{1,0:T(8,128)(2,1)}), bf16[2048,6144]{1,0:T(8,128)(2,1)}) %all-gather.7.cloned.1.call-update) | async-done | bytes 25165840 | tf_op jit(solution)/shard_map/all_gather | solution.py:64
  232.2 12.3 convolution_convert_fusion.4
  255.6 24.4 all-to-all-done
  298.0 8.7 all-gather.1
  306.7 7.5 all-gather.9.cloned.1.call-done
  314.1 4.7 multiply_reduce_fusion.3
  318.9 559.5 %all-gather.11.cloned.1.call-done = bf16[2048,16384]{1,0:T(8,128)(2,1)} async-done(((bf16[256,16384]{1,0:T(8,128)(2,1)}), bf16[2048,16384]{1,0:T(8,128)(2,1)}) %all-gather.11.cloned.1.call-update) | async-done | bytes 67108880 | tf_op jit(solution)/shard_map/all_gather | solution.py:64
  878.4 31.8 %fusion.57 = f32[128,16384]{1,0:T(8,128)} fusion(bf16[2048,16384]{1,0:T(8,128)(2,1)} %all-gather.11.cloned.1.call-done, f32[128,2048]{1,0:T(8,128)S(1)} %get-tuple-element.90, f32[2048]{0:T(1024)S(1)} %bitcast.135, f32[128]{0:T(128)S(1)} %get-tuple-element.86), kind=kOutput, calls=%fused_computation.108 | convolution fusion | flops 8590721024 | bytes 76554752 | tf_op jit(solution)/shard_map/dot_general | solution.py:141
  910.1 256.5 %all-gather.13.cloned.1.call-done = bf16[8192,2048]{1,0:T(8,128)(2,1)} async-done(((bf16[1024,2048]{1,0:T(8,128)(2,1)}), bf16[8192,2048]{1,0:T(8,128)(2,1)}) %all-gather.13.cloned.1.call-update) | async-done | bytes 33554448 | tf_op jit(solution)/shard_map/all_gather | solution.py:65
  1166.7 21.0 multiply_convert_fusion.2
  1187.7 30.0 %multiply_reduce_fusion.1 = (bf16[2048]{0:T(1024)(128)(2,1)S(1)}, f32[128]{0:T(128)S(1)}, f32[128,2048]{1,0:T(8,128)}) fusion(f32[128,2048]{1,0:T(8,128)S(1)} %get-tuple-element.90, f32[128]{0:T(128)S(1)} %get-tuple-element.86, f32[2048]{0:T(1024)S(1)} %bitcast.136, bf16[2048,16384]{1,0:T(8,128)(2,1)} %all-gather.11.cloned.1.call-done, ...), kind=kOutput, calls=%fused_computation.63 | convolution fusion | flops 8599894016 | bytes 73413632 | tf_op jit(solution)/shard_map/dot_general | solution.py:21
  1219.4 5.7 convolution_convert_fusion.3
  1225.2 6.3 convolution_convert_fusion.5
  1236.0 8.5 all-to-all-done.2
  1245.0 4.9 fusion.16
  1252.3 5.6 multiply_reduce_fusion
  1257.9 4.6 multiply_convert_fusion
  1271.5 4.8 pad_maximum_fusion.3
  1276.4 27.6 all_to_all.62
  1307.4 11.9 convolution_convert_fusion.2
  1319.4 15.9 convolution_convert_fusion.1
  1335.4 27.6 convolution_convert_fusion
  1363.1 200.4 %reduce-scatter.5.cloned.1.call-done = bf16[256,6144]{1,0:T(8,128)(2,1)} async-done(((bf16[2048,6144]{1,0:T(8,128)(2,1)}), bf16[256,6144]{1,0:T(8,128)(2,1)}) %reduce-scatter.5.cloned.1.call-update) | async-done | bytes 3145744 | tf_op jit(solution)/shard_map/reduce_scatter | solution.py:75
  1563.5 326.3 %reduce-scatter.11.cloned.1.call-done = bf16[1024,2048]{1,0:T(8,128)(2,1)} async-done(((bf16[8192,2048]{1,0:T(8,128)(2,1)}), bf16[1024,2048]{1,0:T(8,128)(2,1)}) %reduce-scatter.11.cloned.1.call-update) | async-done | bytes 4194320 | tf_op jit(solution)/shard_map/reduce_scatter | solution.py:75
  1889.8 641.0 %reduce-scatter.9.cloned.1.call-done = bf16[256,16384]{1,0:T(8,128)(2,1)} async-done(((bf16[2048,16384]{1,0:T(8,128)(2,1)}), bf16[256,16384]{1,0:T(8,128)(2,1)}) %reduce-scatter.9.cloned.1.call-update) | async-done | bytes 8388624 | tf_op jit(solution)/shard_map/reduce_scatter | solution.py:75
  2532.7 17.6 fusion.9
  2550.3 15.2 fusion.29
  2565.5 13.9 all-reduce.2
  2579.6 10.2 all-reduce.3
  2593.5 249.9 %all-reduce.7.cloned.1.call-done = (bf16[256,6144]{1,0:T(8,128)(2,1)}, bf16[256,2048]{1,0:T(8,128)(2,1)}, bf16[256,16384]{1,0:T(8,128)(2,1)}, bf16[1024,2048]{1,0:T(8,128)(2,1)}) async-done(((bf16[256,6144]{1,0:T(8,128)(2,1)}, bf16[256,2048]{1,0:T(8,128)(2,1)}, bf16[256,16384]{1,0:T(8,128)(2,1)}, bf16[1024,2048]{1,0:T(8,128)(2,1)}), (bf16[256,6144]{1,0:T(8,128)(2,1)}, bf16[256,2048]{1,0:T(8,128)(2,1)}, ...) | async-done | bytes 16777232 | tf_op jit(solution)/shard_map/psum | solution.py:83
  2854.3 11.5 convert_element_type.170
  (115 shorter events, 70.0 us)
Async XLA Ops:
  7.2 225.1 %all-gather.7.cloned.1.call-start = ((), (), s32[]{:S(2)}) async-start(), calls=%async_computation.8 | async-start | bytes 28311552 | tf_op jit(solution)/shard_map/all_gather | solution.py:64
  7.9 306.2 %all-gather.9.cloned.1.call-start = ((), (), s32[]{:S(2)}) async-start(), calls=%async_computation.9 | async-start | bytes 9437184 | tf_op jit(solution)/shard_map/all_gather | solution.py:65
  8.7 1.3 copy-start.18
  8.7 869.7 %all-gather.11.cloned.1.call-start = ((), (), s32[]{:S(2)}) async-start(), calls=%async_computation.10 | async-start | bytes 75497472 | tf_op jit(solution)/shard_map/all_gather | solution.py:64
  9.4 14.1 copy-start.1
  9.4 1157.3 %all-gather.13.cloned.1.call-start = ((), (), s32[]{:S(2)}) async-start(), calls=%async_computation.11 | async-start | bytes 37748736 | tf_op jit(solution)/shard_map/all_gather | solution.py:65
  250.3 29.7 %all-to-all-start = ((bf16[128,3,2048]{0,1,2:T(4,128)(2,1)}), bf16[128,3,2048]{0,1,2:T(4,128)(2,1)S(1)}, u32[]{:S(2)}, u32[]{:S(2)}) async-start(bf16[128,3,2048]{0,1,2:T(4,128)(2,1)} %copy.43), calls=%async_computation | async-start | bytes 4194304 | tf_op jit(solution)/shard_map/all_to_all | solution.py:106
  285.1 4.5 copy-start.4
  285.1 1.1 copy-start.12
  285.1 1.3 copy-start.13
  286.8 1.6 copy-start.5
  286.8 1.6 copy-start.7
  288.4 3.4 copy-start
  288.4 3.4 copy-start.15
  291.8 6.1 copy-start.19
  294.4 19.8 all-to-all-start.1
  297.9 1065.2 %reduce-scatter.7.cloned.1.call-start = ((), (), s32[]{:S(2)}) async-start(), calls=%async_computation.13 | async-start | bytes 9437184 | tf_op jit(solution)/shard_map/reduce_scatter | solution.py:78
  878.4 288.3 %copy-start.11 = (bf16[1,128,2048]{2,1,0:T(8,128)(2,1)S(1)}, bf16[1,128,2048]{2,1,0:T(8,128)(2,1)}, u32[]{:S(2)}) copy-start(bf16[1,128,2048]{2,1,0:T(8,128)(2,1)} %param.23) | copy-start | bytes 1572868
  1219.4 5.8 copy-start.2
  1225.2 10.8 copy-start.16
  1232.3 12.2 all-to-all-start.2
  1236.0 327.5 %reduce-scatter.5.cloned.1.call-start = ((), (), s32[]{:S(2)}) async-start(), calls=%async_computation.12 | async-start | bytes 28311552 | tf_op jit(solution)/shard_map/reduce_scatter | solution.py:75
  1257.9 4.6 copy-start.8
  1262.5 1.4 copy-start.6
  1264.8 0.9 copy-start.14
  1319.4 570.4 %reduce-scatter.11.cloned.1.call-start = ((), (), s32[]{:S(2)}) async-start(), calls=%async_computation.15 | async-start | bytes 37748736 | tf_op jit(solution)/shard_map/reduce_scatter | solution.py:75
  1335.3 1195.4 %reduce-scatter.9.cloned.1.call-start = ((), (), s32[]{:S(2)}) async-start(), calls=%async_computation.14 | async-start | bytes 75497472 | tf_op jit(solution)/shard_map/reduce_scatter | solution.py:75
  1363.0 1480.4 %all-reduce.7.cloned.1.call-start = ((), (), s32[]{:S(2)}) async-start(), calls=%async_computation.16 | async-start | bytes 33554432 | tf_op jit(solution)/shard_map/psum | solution.py:83
  2550.3 40.6 %copy-start.3 = (f32[128,2048]{1,0:T(8,128)S(1)}, f32[128,2048]{1,0:T(8,128)}, u32[]{:S(2)}) copy-start(f32[128,2048]{1,0:T(8,128)} %copy-done.2) | copy-start | bytes 3145732
  2550.3 40.6 %copy-start.17 = (f32[128]{0:T(128)S(1)}, f32[128]{0:T(128)}, u32[]{:S(2)}) copy-start(f32[128]{0:T(128)} %get-tuple-element.83) | copy-start | bytes 1540
  2843.4 2.9 copy-start.10
  2846.4 3.5 copy-start.9
  (1 other events, 0.7 us)
Sparse Core Ops, SparseCore 0:
  9.6 222.5 all-gather.6
  233.8 80.2 all-gather.8
  315.8 562.5 all-gather.10
  879.8 286.8 all-gather.12
  1225.3 87.8 reduce-scatter.6
  1319.5 243.9 reduce-scatter.4
  1565.9 323.8 reduce-scatter.10
  1892.3 638.4 reduce-scatter.8
  2534.8 308.6 all-reduce.6
where the time goes:
time: 2880 us; the launch traced here: 2870 us
  waiting for transfers between devices  2480 us (86%)
  matrix products  216 us (8%)
  blocking collectives  73.8 us (3%)
  other arithmetic  42.8 us (1%)
    reduce_scatter x3, waiting for transfers between devices, reduce_grads(): lax.psum_scatter(terms[0].astype(jnp.bfloat16), 'fsdp', scatter_dimension...  1170 us
    all_gather x2, waiting for transfers between devices, fetch_rows(): lax.all_gather(first, 'fsdp', axis=0, tiled=True)  768 us
    all_gather x2, waiting for transfers between devices, fetch_rows(): lax.all_gather(second, 'fsdp', axis=0, tiled=True)  264 us
    psum x1, waiting for transfers between devices, reduce_grads(): lax.psum(partial_sums[0].astype(jnp.bfloat16), 'seq').astype(jnp.float32)  250 us
    dot_general x4, matrix products, back_product(): lax.dot_general(grad, weight, (((1,), (1,)), ((), ())), preferred_element...  72.5 us
    dot_general x4, matrix products, outer_sum(): lax.dot_general(left, right, (((0,), (0,)), ((), ())), preferred_element_...  61.2 us
  transfers between devices with their start and end apart: 12, of which 10 were waited for; matrix products, arithmetic and copies ran while one was open for 7% of the time, Pallas kernels for 0%

commit v1 on v0

--- a/solution.py
+++ b/solution.py
@@ -1,6 +1,10 @@
+import functools
+
 import jax
 import jax.numpy as jnp
 from jax import lax
+from jax.experimental import pallas as pl
+from jax.experimental.pallas import tpu as pltpu
 from jax.sharding import PartitionSpec as P
 
 HEAD_DIM = 64
@@ -9,6 +13,7 @@
 EPSILON = 1e-05
 THETA = 130000.0
 SCALE = 0.125
+LANES = 128
 
 
 def outer_sum(left, right):
@@ -95,7 +100,7 @@
     return jnp.where((columns <= rows)[None], scores, -1e30)
 
 
-def on_device(hidden_in, norm_one, w_qkv, w_out, norm_two, w_gate_up, w_down, grad_out):
+def gathered_plan(hidden_in, norm_one, w_qkv, w_out, norm_two, w_gate_up, w_down, grad_out):
     inputs = hidden_in[0].astype(jnp.float32)
     tokens = inputs.shape[0]
     width = inputs.shape[1]
@@ -226,7 +231,412 @@
     )
 
 
+def xor_pairs(size, offset):
+    return [(i, i ^ offset) for i in range(size)]
+
+
+def swap_cores(values, fsdp):
+    return lax.ppermute(values, "fsdp", xor_pairs(fsdp, 1))
+
+
+def gather_tokens(block, seq, fsdp):
+    row = jnp.stack(
+        [block] + [lax.ppermute(block, "seq", xor_pairs(seq, k)) for k in range(1, seq)]
+    )
+    return jnp.stack([row, swap_cores(row, fsdp)])
+
+
+def reduce_tokens(partial, seq, fsdp):
+    other = swap_cores(partial[1], fsdp)
+    row = (partial[0].astype(jnp.float32) + other.astype(jnp.float32)).astype(jnp.bfloat16)
+    total = row[0].astype(jnp.float32)
+    for k in range(1, seq):
+        total = total + lax.ppermute(row[k], "seq", xor_pairs(seq, k)).astype(jnp.float32)
+    return total
+
+
+def rows_groups(fsdp):
+    return [[i for i in range(core, fsdp, 2)] for core in range(2)]
+
+
+def gather_rows(block, fsdp):
+    return lax.all_gather(block, "fsdp", axis=0, tiled=True, axis_index_groups=rows_groups(fsdp))
+
+
+def scatter_rows(term, fsdp):
+    return lax.psum_scatter(
+        term, "fsdp", scatter_dimension=0, tiled=True, axis_index_groups=rows_groups(fsdp)
+    )
+
+
+def lane_mask(rows):
+    return lax.broadcasted_iota(jnp.int32, (rows, LANES), 1) < LANES // 2
+
+
+def slice_wide(weight, gain, place, groups, chunk, seq):
+    rows = weight.shape[0]
+
+    def body(place_ref, weight_ref, gain_ref, out_ref):
+        out_ref[0] = (weight_ref[...].astype(jnp.float32) * gain_ref[...]).astype(jnp.bfloat16)
+
+    return pl.pallas_call(
+        body,
+        grid_spec=pltpu.PrefetchScalarGridSpec(
+            num_scalar_prefetch=1,
+            grid=(2, groups),
+            in_specs=[
+                pl.BlockSpec(
+                    (rows, chunk), lambda j, k, p: (0, (k * 2 + (p[1] ^ j)) * seq + p[0])
+                ),
+                pl.BlockSpec((rows, 1), lambda j, k, p: (0, 0)),
+            ],
+            out_specs=pl.BlockSpec((1, rows, chunk), lambda j, k, p: (j, 0, k)),
+        ),
+        out_shape=jax.ShapeDtypeStruct((2, rows, groups * chunk), jnp.bfloat16),
+        name="slice_wide",
+    )(place, weight, gain)
+
+
+def slice_heads(weight, gain, place, heads, seq):
+    rows = weight.shape[0]
+    part = weight.shape[1] // 3
+
+    def body(place_ref, weight_ref, gain_ref, out_ref):
+        own_seq, own_core = place_ref[0], place_ref[1]
+        odd = (own_seq % 2) == 1
+        low = lane_mask(rows)
+        for core in range(2):
+            for pair in range(heads // 2):
+                tiles = []
+                for head in (2 * pair, 2 * pair + 1):
+                    start = (head * 2 + (own_core ^ core)) * (seq * HEAD_DIM) + (
+                        own_seq // 2
+                    ) * LANES
+                    tile = weight_ref[:, pl.ds(pl.multiple_of(start, LANES), LANES)]
+                    tiles.append(tile.astype(jnp.float32) * gain_ref[...])
+                turned = [pltpu.roll(tile, LANES // 2, axis=1) for tile in tiles]
+                first = jnp.where(odd, turned[0], tiles[0])
+                second = jnp.where(odd, tiles[1], turned[1])
+                out_ref[core, :, pair * LANES : (pair + 1) * LANES] = jnp.where(
+                    low, first, second
+                ).astype(jnp.bfloat16)
+
+    return pl.pallas_call(
+        body,
+        grid_spec=pltpu.PrefetchScalarGridSpec(
+            num_scalar_prefetch=1,
+            grid=(3,),
+            in_specs=[
+                pl.BlockSpec((rows, part), lambda k, p: (0, k)),
+                pl.BlockSpec((rows, 1), lambda k, p: (0, 0)),
+            ],
+            out_specs=pl.BlockSpec((2, rows, heads * HEAD_DIM), lambda k, p: (0, 0, k)),
+        ),
+        out_shape=jax.ShapeDtypeStruct((2, rows, 3 * heads * HEAD_DIM), jnp.bfloat16),
+        name="slice_heads",
+    )(place, weight, gain)
+
+
+def fold(products):
+    total = products[:, :LANES]
+    for k in range(1, products.shape[1] // LANES):
+        total = total + products[:, k * LANES : (k + 1) * LANES]
+    return total
+
+
+def merge_wide(pieces, weight, gain, place, groups, chunk):
+    seq = len(pieces)
+    rows = weight.shape[0]
+    width = seq * chunk
+
+    def body(place_ref, *refs):
+        weight_ref, gain_ref = refs[seq : seq + 2]
+        out_ref, sum_ref = refs[seq + 2 :]
+
+        @pl.when((pl.program_id(0) == 0) & (pl.program_id(1) == 0))
+        def _():
+            sum_ref[...] = jnp.zeros_like(sum_ref)
+
+        for r in range(seq):
+            start = pl.multiple_of((place_ref[0] ^ r) * chunk, LANES)
+            term = refs[r][0].astype(jnp.float32)
+            out_ref[:, pl.ds(start, chunk)] = term * gain_ref[...]
+            sum_ref[place_ref[0] ^ r] += fold(
+                term * weight_ref[:, pl.ds(start, chunk)].astype(jnp.float32)
+            )
+
+    wide = pl.BlockSpec((rows, width), lambda j, k, p: (0, k * 2 + (p[1] ^ j)))
+    return pl.pallas_call(
+        body,
+        grid_spec=pltpu.PrefetchScalarGridSpec(
+            num_scalar_prefetch=1,
+            grid=(2, groups),
+            in_specs=[pl.BlockSpec((1, rows, chunk), lambda j, k, p: (j, 0, k))] * seq
+            + [wide, pl.BlockSpec((rows, 1), lambda j, k, p: (0, 0))],
+            out_specs=[wide, pl.BlockSpec((seq, rows, LANES), lambda j, k, p: (0, 0, 0))],
+        ),
+        out_shape=[
+            jax.ShapeDtypeStruct(weight.shape, jnp.float32),
+            jax.ShapeDtypeStruct((seq, rows, LANES), jnp.float32),
+        ],
+        name="merge_wide",
+    )(place, *pieces, weight, gain)
+
+
+def merge_heads(pieces, weight, gain, place, heads):
+    seq = len(pieces)
+    rows = weight.shape[0]
+    part = weight.shape[1] // 3
+
+    def body(place_ref, *refs):
+        weight_ref, gain_ref = refs[seq : seq + 2]
+        out_ref, sum_ref = refs[seq + 2 :]
+        own_seq, own_core = place_ref[0], place_ref[1]
+        odd = (own_seq % 2) == 1
+        low = lane_mask(rows)
+
+        @pl.when(pl.program_id(0) == 0)
+        def _():
+            sum_ref[...] = jnp.zeros_like(sum_ref)
+
+        for core in range(2):
+            for pair in range(heads // 2):
+                for couple in range(seq // 2):
+                    first, second = (
+                        refs[2 * couple + k][core, :, pair * LANES : (pair + 1) * LANES].astype(
+                            jnp.float32
+                        )
+                        for k in range(2)
+                    )
+                    turned_first = pltpu.roll(first, LANES // 2, axis=1)
+                    turned_second = pltpu.roll(second, LANES // 2, axis=1)
+                    for head, even_tile, odd_tile in (
+                        (
+                            2 * pair,
+                            jnp.where(low, first, turned_second),
+                            jnp.where(low, second, turned_first),
+                        ),
+                        (
+                            2 * pair + 1,
+                            jnp.where(low, turned_first, second),
+                            jnp.where(low, turned_second, first),
+                        ),
+                    ):
+                        tile = jnp.where(odd, odd_tile, even_tile)
+                        start = (head * 2 + (own_core ^ core)) * (seq * HEAD_DIM) + (
+                            (own_seq // 2) ^ couple
+                        ) * LANES
+                        columns = pl.ds(pl.multiple_of(start, LANES), LANES)
+                        out_ref[:, columns] = tile * gain_ref[...]
+                        sum_ref[(own_seq // 2) ^ couple] += tile * weight_ref[:, columns].astype(
+                            jnp.float32
+                        )
+
+    wide = pl.BlockSpec((rows, part), lambda k, p: (0, k))
+    return pl.pallas_call(
+        body,
+        grid_spec=pltpu.PrefetchScalarGridSpec(
+            num_scalar_prefetch=1,
+            grid=(3,),
+            in_specs=[pl.BlockSpec((2, rows, heads * HEAD_DIM), lambda k, p: (0, 0, k))] * seq
+            + [wide, pl.BlockSpec((rows, 1), lambda k, p: (0, 0))],
+            out_specs=[wide, pl.BlockSpec((seq // 2, rows, LANES), lambda k, p: (0, 0, 0))],
+        ),
+        out_shape=[
+            jax.ShapeDtypeStruct(weight.shape, jnp.float32),
+            jax.ShapeDtypeStruct((seq // 2, rows, LANES), jnp.float32),
+        ],
+        name="merge_heads",
+    )(place, *pieces, weight, gain)
+
+
+def share_rows(piece, seq):
+    return [piece] + [lax.ppermute(piece, "seq", xor_pairs(seq, k)) for k in range(1, seq)]
+
+
+def place_rows(pieces, own_seq):
+    rows, width = pieces[0].shape
+    out = jnp.zeros((rows * len(pieces), width), jnp.float32)
+    for k, piece in enumerate(pieces):
+        out = lax.dynamic_update_slice(out, piece.astype(jnp.float32), ((own_seq ^ k) * rows, 0))
+    return out
+
+
+def both_halves(mine, other, own_core):
+    return jnp.concatenate(
+        [jnp.where(own_core == 0, mine, other), jnp.where(own_core == 0, other, mine)]
+    )
+
+
+def own_halves(rows, own_core, fsdp):
+    half = rows.shape[0] // 2
+    mine = lax.dynamic_slice_in_dim(rows, own_core * half, half)
+    other = swap_cores(lax.dynamic_slice_in_dim(rows, (1 - own_core) * half, half), fsdp)
+    return jnp.stack([mine, other])
+
+
+def sliced_plan(
+    seq, fsdp, hidden_in, norm_one, w_qkv, w_out, norm_two, w_gate_up, w_down, grad_out
+):
+    own_seq = lax.axis_index("seq")
+    own_core = lax.axis_index("fsdp") % 2
+    place = jnp.stack([own_seq, own_core]).astype(jnp.int32)
+    chips = fsdp // 2
+    inputs = hidden_in[0].astype(jnp.float32)
+    cotangent = grad_out[0]
+    tokens, width = inputs.shape
+    length = tokens * seq
+    hidden_units = w_down.shape[0] * fsdp
+    chunk = hidden_units // (fsdp * seq)
+    heads = width // HEAD_DIM // (2 * seq)
+    gain_one = norm_one.astype(jnp.float32)[:, None]
+    gain_two = norm_two.astype(jnp.float32)[:, None]
+
+    qkv_parts = slice_heads(w_qkv, gain_one, place, heads, seq)
+    qkv_chip = both_halves(qkv_parts[0], swap_cores(qkv_parts[1], fsdp), own_core)
+    qkv = gather_rows(qkv_chip, fsdp)
+    out_rows = w_out.shape[0] // seq
+    out_proj = gather_rows(lax.dynamic_slice_in_dim(w_out, own_seq * out_rows, out_rows), fsdp)
+    gate_up_parts = slice_wide(w_gate_up, gain_two, place, 2 * chips, chunk, seq)
+    gate_up_chip = both_halves(gate_up_parts[0], swap_cores(gate_up_parts[1], fsdp), own_core)
+    gate_up_w = gather_rows(gate_up_chip, fsdp)
+    down = gather_rows(lax.dynamic_slice_in_dim(w_down, own_seq * chunk, chunk), fsdp)
+
+    factor_one = lax.rsqrt(jnp.mean(inputs * inputs, axis=-1, keepdims=True) + EPSILON)
+    normed = (inputs * factor_one).astype(jnp.bfloat16)
+    group = 2 * seq * tokens
+    normed_all = gather_tokens(normed, seq, fsdp).reshape(group, width)
+    mixed = jnp.dot(normed_all, qkv, preferred_element_type=jnp.float32).astype(jnp.bfloat16)
+    mixed = mixed.reshape(2, length, 3, heads, HEAD_DIM)
+    block_starts = (own_seq ^ jnp.arange(seq)) * tokens
+    positions = (block_starts[:, None] + jnp.arange(tokens)[None]).reshape(length)
+    half = HEAD_DIM // 2
+    freqs = THETA ** (-(jnp.arange(half, dtype=jnp.float32) * 2.0) / HEAD_DIM)
+    angles = positions.astype(jnp.float32)[:, None] * freqs[None, :]
+    angles = jnp.concatenate([angles, angles], axis=1)
+    cosine, sine = jnp.cos(angles)[:, None, :], jnp.sin(angles)[:, None, :]
+    query = rotate(mixed[:, :, 0].astype(jnp.float32), cosine, sine).astype(jnp.bfloat16)
+    keys = rotate(mixed[:, :, 1].astype(jnp.float32), cosine, sine).astype(jnp.bfloat16)
+    values = mixed[:, :, 2]
+    visible = positions[None, :] <= positions[:, None]
+    scores = (
+        jnp.einsum("bqhd,bkhd->bhqk", query, keys, preferred_element_type=jnp.float32) * SCALE
+    )
+    scores = jnp.where(visible, scores, -1e30)
+    highest = jnp.max(scores, axis=-1, keepdims=True)
+    weights = jnp.exp(scores - highest)
+    total = jnp.sum(weights, axis=-1, keepdims=True)
+    probabilities = weights / total
+    attended = jnp.einsum(
+        "bhqk,bkhd->bqhd",
+        probabilities.astype(jnp.bfloat16),
+        values,
+        preferred_element_type=jnp.float32,
+    ).astype(jnp.bfloat16)
+    attended = attended.reshape(group, heads * HEAD_DIM)
+    branch = jnp.dot(attended, out_proj, preferred_element_type=jnp.float32).astype(jnp.bfloat16)
+    middle = inputs + reduce_tokens(branch.reshape(2, seq, tokens, width), seq, fsdp)
+
+    factor_two = lax.rsqrt(jnp.mean(middle * middle, axis=-1, keepdims=True) + EPSILON)
+    normed_two = (middle * factor_two).astype(jnp.bfloat16)
+    cotangent_all = gather_tokens(cotangent, seq, fsdp).reshape(group, width)
+    normed_two_all = gather_tokens(normed_two, seq, fsdp).reshape(group, width)
+    gate_up = jnp.dot(normed_two_all, gate_up_w, preferred_element_type=jnp.float32)
+    units = gate_up.shape[1] // 2
+    gate, upward = gate_up[:, :units], gate_up[:, units:]
+    sigmoid = jax.nn.sigmoid(gate)
+    activated = gate * sigmoid
+    hidden = (activated * upward).astype(jnp.bfloat16)
+    grad_down_rows = scatter_rows(outer_sum(hidden, cotangent_all).astype(jnp.bfloat16), fsdp)
+    grad_hidden = back_product(cotangent_all, down)
+    grad_gate = grad_hidden * upward * sigmoid * (1.0 + gate * (1.0 - sigmoid))
+    grad_upward = grad_hidden * activated
+    grad_low = jnp.concatenate([grad_gate, grad_upward], axis=1).astype(jnp.bfloat16)
+    back = back_product(grad_low, gate_up_w).astype(jnp.bfloat16)
+    scaled_two = reduce_tokens(back.reshape(2, seq, tokens, width), seq, fsdp)
+    grad_gate_up_rows = scatter_rows(outer_sum(normed_two_all, grad_low).astype(jnp.bfloat16), fsdp)
+    grad_middle = (
+        cotangent.astype(jnp.float32)
+        + factor_two * scaled_two
+        - middle * factor_two**3 * jnp.mean(scaled_two * middle, axis=-1, keepdims=True)
+    )
+    grad_branch = gather_tokens(grad_middle.astype(jnp.bfloat16), seq, fsdp).reshape(group, width)
+    forward = jnp.dot(hidden, down, preferred_element_type=jnp.float32).astype(jnp.bfloat16)
+    output = middle + reduce_tokens(forward.reshape(2, seq, tokens, width), seq, fsdp)
+
+    grad_out_rows = scatter_rows(outer_sum(attended, grad_branch).astype(jnp.bfloat16), fsdp)
+    grad_heads = back_product(grad_branch, out_proj).astype(jnp.bfloat16)
+    grad_heads = grad_heads.reshape(2, length, heads, HEAD_DIM)
+    grad_probabilities = jnp.einsum(
+        "bqhd,bkhd->bhqk", grad_heads, values, preferred_element_type=jnp.float32
+    )
+    inner = jnp.sum(probabilities * grad_probabilities, axis=-1, keepdims=True)
+    grad_scores = (probabilities * (grad_probabilities - inner)).astype(jnp.bfloat16)
+    grad_query = (
+        jnp.einsum("bhqk,bkhd->bqhd", grad_scores, keys, preferred_element_type=jnp.float32) * SCALE
+    )
+    grad_keys = (
+        jnp.einsum("bhqk,bqhd->bkhd", grad_scores, query, preferred_element_type=jnp.float32)
+        * SCALE
+    )
+    grad_values = jnp.einsum(
+        "bhqk,bqhd->bkhd",
+        probabilities.astype(jnp.bfloat16),
+        grad_heads,
+        preferred_element_type=jnp.float32,
+    )
+    grad_mixed = jnp.stack(
+        [unrotate(grad_query, cosine, sine), unrotate(grad_keys, cosine, sine), grad_values], axis=2
+    )
+    grad_mixed = grad_mixed.astype(jnp.bfloat16).reshape(group, 3 * heads * HEAD_DIM)
+    grad_qkv_rows = scatter_rows(outer_sum(normed_all, grad_mixed).astype(jnp.bfloat16), fsdp)
+    back = back_product(grad_mixed, qkv).astype(jnp.bfloat16)
+    scaled_one = reduce_tokens(back.reshape(2, seq, tokens, width), seq, fsdp)
+    grad_inputs = (
+        grad_middle
+        + factor_one * scaled_one
+        - inputs * factor_one**3 * jnp.mean(scaled_one * inputs, axis=-1, keepdims=True)
+    )
+
+    grad_down = place_rows(share_rows(grad_down_rows, seq), own_seq)
+    grad_out_proj = place_rows(share_rows(grad_out_rows, seq), own_seq)
+    grad_gate_up, gain_two_sums = merge_wide(
+        share_rows(own_halves(grad_gate_up_rows, own_core, fsdp), seq),
+        w_gate_up,
+        gain_two,
+        place,
+        2 * chips,
+        chunk,
+    )
+    grad_qkv, gain_one_sums = merge_heads(
+        share_rows(own_halves(grad_qkv_rows, own_core, fsdp), seq), w_qkv, gain_one, place, heads
+    )
+    return (
+        output.astype(jnp.bfloat16)[None],
+        grad_inputs[None],
+        jnp.sum(gain_one_sums, axis=(0, 2)),
+        grad_qkv,
+        grad_out_proj,
+        jnp.sum(gain_two_sums, axis=(0, 2)),
+        grad_gate_up,
+        grad_down,
+    )
+
+
 def solution(mesh):
+    seq, fsdp = mesh.shape["seq"], mesh.shape["fsdp"]
+
+    def on_device(hidden_in, norm_one, w_qkv, w_out, norm_two, w_gate_up, w_down, grad_out):
+        arrays = (hidden_in, norm_one, w_qkv, w_out, norm_two, w_gate_up, w_down, grad_out)
+        if (
+            w_out.shape[0] == seq * HEAD_DIM
+            and (fsdp // 2) % 2 == 0
+            and seq & (seq - 1) == 0
+            and (w_down.shape[0] // seq) % LANES == 0
+        ):
+            return sliced_plan(seq, fsdp, *arrays)
+        return gathered_plan(*arrays)
+
     placed = (
         P("fsdp", "seq", None),
         P("fsdp"),

time: 2880 us -> 984 us (0.34)
  waiting for transfers between devices: 2480 us -> 646 us
  matrix products: 216 us -> 111 us
  blocking collectives: 73.8 us -> 0 us
  Pallas kernels: 0 us -> 44.9 us
  starting transfers between devices: 11.6 us -> 49.2 us
    reduce_scatter x4, waiting for transfers between devices: 1170 us -> 194 us  [scatter_rows(): lax.psum_scatter(term, 'fsdp', scatter_dimension=0, tiled=True, axis_inde...]
    all_gather x4, waiting for transfers between devices: 1030 us -> 142 us  [gather_rows(): lax.all_gather(block, 'fsdp', axis=0, tiled=True, axis_index_groups=rows_...]
    ppermute x0 -> x48, waiting for transfers between devices: none -> 310 us  [the longest x12 154 us: share_rows(): lax.ppermute(piece, 'seq', xor_pairs(seq, k))]
    psum x1 -> x0, waiting for transfers between devices: 250 us -> none  [reduce_grads(): lax.psum(partial_sums[0].astype(jnp.bfloat16), 'seq').astype(jnp.float32)]
    ppermute x0 -> x48, starting transfers between devices: none -> 48.9 us  [the longest x12 16.8 us: gather_tokens(): lax.ppermute(block, 'seq', xor_pairs(seq, k))]
    pallas_call x0 -> x4, Pallas kernels: none -> 44.9 us  [the longest x1 19.8 us: merge_wide(): pl.pallas_call(body, grid_spec=pltpu.PrefetchScalarGridSpec(num_scalar_pr...]
    dot_general x10 -> x9, matrix products: 82.2 us -> 41.8 us  [the longest x1 14.9 us: sliced_plan(): jnp.dot(normed_two_all, gate_up_w, preferred_element_type=jnp.float32)]
    dot_general x4, matrix products: 72.5 us -> 33.8 us  [back_product(): lax.dot_general(grad, weight, (((1,), (1,)), ((), ())), preferred_element...]
  transfers between devices with their start and end apart: 12 -> 56, of which waited for: 10 -> 38; matrix products, arithmetic and copies ran while one was open for 7% -> 17% of each run, Pallas kernels for 0% -> 2%
where the time goes in v1:
time: 984 us; the launch traced here: 977 us
  waiting for transfers between devices  646 us (66%)
  matrix products  111 us (11%)
  other arithmetic  62.3 us (6%)
  starting transfers between devices  49.2 us (5%)
  local copies, waits for them, and re-layouts  48.3 us (5%)
  Pallas kernels  44.9 us (5%)
  between operations  15.4 us (2%)
    reduce_scatter x4, waiting for transfers between devices, scatter_rows(): lax.psum_scatter(term, 'fsdp', scatter_dimension=0, tiled=True, axis_inde...  194 us
    ppermute x12, waiting for transfers between devices, share_rows(): lax.ppermute(piece, 'seq', xor_pairs(seq, k))  154 us
    all_gather x4, waiting for transfers between devices, gather_rows(): lax.all_gather(block, 'fsdp', axis=0, tiled=True, axis_index_groups=rows_...  142 us
    ppermute x12, waiting for transfers between devices, gather_tokens(): lax.ppermute(block, 'seq', xor_pairs(seq, k))  80.6 us
    ppermute x12, waiting for transfers between devices, reduce_tokens(): lax.ppermute(row[k], 'seq', xor_pairs(seq, k)).astype(jnp.float32)  56.5 us
    dot_general x4, matrix products, back_product(): lax.dot_general(grad, weight, (((1,), (1,)), ((), ())), preferred_element...  33.8 us
    dot_general x4, matrix products, outer_sum(): lax.dot_general(left, right, (((0,), (0,)), ((), ())), preferred_element_...  29.2 us
    pallas_call x1, Pallas kernels, merge_wide(): pl.pallas_call(body, grid_spec=pltpu.PrefetchScalarGridSpec(num_scalar_pr...  19.8 us
  transfers between devices with their start and end apart: 56, of which 38 were waited for; matrix products, arithmetic and copies ran while one was open for 17% of the time, Pallas kernels for 2%

profile of v1, /device:TPU:0, one launch (start us, length us, event | category | flops | bytes accessed | tf_op | source)
XLA Modules:
  0.0 977.4 jit_solution(11945061559430590525)
XLA Ops:
  20.3 10.8 %slice_wide.1 = bf16[2,256,2048]{2,1,0:T(8,128)(2,1)} custom-call(s32[2]{0:T(128)} %pad_add_fusion.place_ref, bf16[256,16384]{1,0:T(8,128)(2,1)} %refs_4_.3, f32[256,1]{1,0:T(8,128)} %copy.34.gain_ref.refs_5_), custom_call_target="tpu_custom_call" | custom-call | tf_op jit(solution)/shard_map/slice_wide/pallas_call | solution.py:282
  43.7 12.0 %collective-permute-done.2 = bf16[128,2048]{1,0:T(8,128)(2,1)S(1)} collective-permute-done((bf16[128,2048]{1,0:T(8,128)(2,1)S(1)}, bf16[128,2048]{1,0:T(8,128)(2,1)S(1)}, u32[]{:S(2)}, u32[]{:S(2)}) %collective-permute-start.2) | collective-permute-done | bytes 524320 | tf_op jit(solution)/shard_map/ppermute | solution.py:244
  55.7 10.7 %collective-permute-done.1 = bf16[128,2048]{1,0:T(8,128)(2,1)S(1)} collective-permute-done((bf16[128,2048]{1,0:T(8,128)(2,1)S(1)}, bf16[128,2048]{1,0:T(8,128)(2,1)S(1)}, u32[]{:S(2)}, u32[]{:S(2)}) %collective-permute-start.1) | collective-permute-done | bytes 524320 | tf_op jit(solution)/shard_map/ppermute | solution.py:244
  73.6 12.1 %all-gather.5.cloned.1.call-done = bf16[2048,768]{1,0:T(8,128)(2,1)} async-done(((bf16[512,768]{1,0:T(8,128)(2,1)}), bf16[2048,768]{1,0:T(8,128)(2,1)}) %all-gather.5.cloned.1.call-update) | async-done | bytes 3145744 | tf_op jit(solution)/shard_map/all_gather | solution.py:263
  133.3 7.1 collective-permute-done.8
  141.9 9.8 %collective-permute-done.7 = bf16[128,2048]{1,0:T(8,128)(2,1)S(1)} collective-permute-done((bf16[128,2048]{1,0:T(8,128)(2,1)}, bf16[128,2048]{1,0:T(8,128)(2,1)S(1)}, u32[]{:S(2)}, u32[]{:S(2)}) %collective-permute-start.7) | collective-permute-done | bytes 524320 | tf_op jit(solution)/shard_map/ppermute | solution.py:254
  164.4 9.9 %collective-permute-done.19 = bf16[128,2048]{1,0:T(8,128)(2,1)} collective-permute-done((bf16[128,2048]{1,0:T(8,128)(2,1)S(1)}, bf16[128,2048]{1,0:T(8,128)(2,1)}, u32[]{:S(2)}, u32[]{:S(2)}) %collective-permute-start.19) | collective-permute-done | bytes 524320 | tf_op jit(solution)/shard_map/ppermute | solution.py:244
  175.9 9.6 collective-permute-done.11
  185.5 10.3 %collective-permute-done.10 = bf16[128,2048]{1,0:T(8,128)(2,1)S(1)} collective-permute-done((bf16[128,2048]{1,0:T(8,128)(2,1)S(1)}, bf16[128,2048]{1,0:T(8,128)(2,1)S(1)}, u32[]{:S(2)}, u32[]{:S(2)}) %collective-permute-start.10) | collective-permute-done | bytes 524320 | tf_op jit(solution)/shard_map/ppermute | solution.py:244
  202.8 62.4 %all-gather.9.cloned.1.call-done = bf16[2048,2048]{1,0:T(8,128)(2,1)} async-done(((bf16[512,2048]{1,0:T(8,128)(2,1)}), bf16[2048,2048]{1,0:T(8,128)(2,1)}) %all-gather.9.cloned.1.call-update) | async-done | bytes 8388624 | tf_op jit(solution)/shard_map/all_gather | solution.py:263
  265.2 14.9 %fusion.98 = f32[1024,2048]{1,0:T(8,128)} fusion(bf16[1024,2048]{1,0:T(8,128)(2,1)} %bitcast.242, bf16[2048,2048]{1,0:T(8,128)(2,1)} %all-gather.9.cloned.1.call-done), kind=kOutput, calls=%fused_computation.191 | convolution fusion | flops 8589934592 | bytes 20971520 | tf_op jit(solution)/shard_map/dot_general | solution.py:544
  280.1 66.2 %all-gather.11.cloned.1.call-done = bf16[1024,2048]{1,0:T(8,128)(2,1)} async-done(((bf16[256,2048]{1,0:T(8,128)(2,1)}), bf16[1024,2048]{1,0:T(8,128)(2,1)}) %all-gather.11.cloned.1.call-update) | async-done | bytes 4194320 | tf_op jit(solution)/shard_map/all_gather | solution.py:263
  346.2 13.1 %multiply_convert_fusion.2 = (bf16[1024,1024]{1,0:T(8,128)(2,1)S(1)}, bf16[1024,1024]{1,0:T(8,128)(2,1)S(1)}, bf16[1024,1024]{1,0:T(8,128)(2,1)}) fusion(f32[1024,2048]{1,0:T(8,128)} %fusion.98, bf16[1024,2048]{1,0:T(8,128)(2,1)} %bitcast.240, bf16[1024,2048]{1,0:T(8,128)(2,1)} %all-gather.11.cloned.1.call-done), kind=kOutput, calls=%fused_computation.21 | convolution fusion | flops 4310695936 | bytes 23068672 | tf_op jit(solution)/shard_map/dot_general | solution.py:26
  361.4 11.3 %convolution_convert_fusion.1 = bf16[1024,2048]{1,0:T(8,128)(2,1)S(1)} fusion(bf16[2048,2048]{1,0:T(8,128)(2,1)} %all-gather.9.cloned.1.call-done, bf16[1024,1024]{1,0:T(8,128)(2,1)S(1)} %get-tuple-element.21, bf16[1024,1024]{1,0:T(8,128)(2,1)S(1)} %get-tuple-element.20), kind=kOutput, calls=%fused_computation.29 | convolution fusion | flops 8600420352 | bytes 16777216 | tf_op jit(solution)/shard_map/dot_general | solution.py:26
  389.6 8.2 collective-permute-done.25
  399.3 9.8 collective-permute-done.24
  409.6 10.7 %collective-permute-done.17 = bf16[128,2048]{1,0:T(8,128)(2,1)S(1)} collective-permute-done((bf16[128,2048]{1,0:T(8,128)(2,1)S(1)}, bf16[128,2048]{1,0:T(8,128)(2,1)S(1)}, u32[]{:S(2)}, u32[]{:S(2)}) %collective-permute-start.17) | collective-permute-done | bytes 524320 | tf_op jit(solution)/shard_map/ppermute | solution.py:254
  420.3 10.7 %collective-permute-done.16 = bf16[128,2048]{1,0:T(8,128)(2,1)S(1)} collective-permute-done((bf16[128,2048]{1,0:T(8,128)(2,1)S(1)}, bf16[128,2048]{1,0:T(8,128)(2,1)S(1)}, u32[]{:S(2)}, u32[]{:S(2)}) %collective-permute-start.16) | collective-permute-done | bytes 524320 | tf_op jit(solution)/shard_map/ppermute | solution.py:254
  436.9 12.3 %collective-permute-done.28 = bf16[128,2048]{1,0:T(8,128)(2,1)S(1)} collective-permute-done((bf16[128,2048]{1,0:T(8,128)(2,1)S(1)}, bf16[128,2048]{1,0:T(8,128)(2,1)S(1)}, u32[]{:S(2)}, u32[]{:S(2)}) %collective-permute-start.28) | collective-permute-done | bytes 524320 | tf_op jit(solution)/shard_map/ppermute | solution.py:244
  449.1 10.1 %collective-permute-done.27 = bf16[128,2048]{1,0:T(8,128)(2,1)S(1)} collective-permute-done((bf16[128,2048]{1,0:T(8,128)(2,1)S(1)}, bf16[128,2048]{1,0:T(8,128)(2,1)S(1)}, u32[]{:S(2)}, u32[]{:S(2)}) %collective-permute-start.27) | collective-permute-done | bytes 524320 | tf_op jit(solution)/shard_map/ppermute | solution.py:244
  468.8 13.8 %convolution_convert_fusion = bf16[2048,2048]{1,0:T(8,128)(2,1)} fusion(bf16[1024,2048]{1,0:T(8,128)(2,1)} %bitcast.243, bf16[1024,1024]{1,0:T(8,128)(2,1)} %copy-done.35, bf16[1024,1024]{1,0:T(8,128)(2,1)S(1)} %copy-done.34), kind=kOutput, calls=%fused_computation.5 | convolution fusion | flops 8602517504 | bytes 16777216 | tf_op jit(solution)/shard_map/dot_general | solution.py:20
  484.2 8.3 convolution_convert_fusion.4
  548.7 23.1 %collective-permute-done.38 = bf16[64,2048]{1,0:T(8,128)(2,1)S(1)} collective-permute-done((bf16[64,2048]{1,0:T(8,128)(2,1)}, bf16[64,2048]{1,0:T(8,128)(2,1)S(1)}, u32[]{:S(2)}, u32[]{:S(2)}) %collective-permute-start.38) | collective-permute-done | bytes 262176 | tf_op jit(solution)/shard_map/ppermute | solution.py:454
  581.3 58.3 %reduce-scatter.9.cloned.1.call-done = bf16[512,2048]{1,0:T(8,128)(2,1)} async-done(((bf16[2048,2048]{1,0:T(8,128)(2,1)}), bf16[512,2048]{1,0:T(8,128)(2,1)}) %reduce-scatter.9.cloned.1.call-update) | async-done | bytes 2097168 | tf_op jit(solution)/shard_map/reduce_scatter | solution.py:267
  644.4 75.1 %reduce-scatter.11.cloned.1.call-done = bf16[256,2048]{1,0:T(8,128)(2,1)} async-done(((bf16[1024,2048]{1,0:T(8,128)(2,1)}), bf16[256,2048]{1,0:T(8,128)(2,1)}) %reduce-scatter.11.cloned.1.call-update) | async-done | bytes 1048592 | tf_op jit(solution)/shard_map/reduce_scatter | solution.py:267
  722.5 60.7 %reduce-scatter.5.cloned.1.call-done = bf16[512,768]{1,0:T(8,128)(2,1)} async-done(((bf16[2048,768]{1,0:T(8,128)(2,1)}), bf16[512,768]{1,0:T(8,128)(2,1)}) %reduce-scatter.5.cloned.1.call-update) | async-done | bytes 786448 | tf_op jit(solution)/shard_map/reduce_scatter | solution.py:267
  804.5 10.0 %collective-permute-done.47 = bf16[256,2048]{1,0:T(8,128)(2,1)S(1)} collective-permute-done((bf16[256,2048]{1,0:T(8,128)(2,1)S(1)}, bf16[256,2048]{1,0:T(8,128)(2,1)S(1)}, u32[]{:S(2)}, u32[]{:S(2)}) %collective-permute-start.47) | collective-permute-done | bytes 1048608 | tf_op jit(solution)/shard_map/ppermute | solution.py:454
  816.0 15.4 %collective-permute-done.35.refs_1_ = bf16[2,256,768]{2,1,0:T(8,128)(2,1)S(1)} collective-permute-done((bf16[2,256,768]{2,1,0:T(8,128)(2,1)S(1)}, bf16[2,256,768]{2,1,0:T(8,128)(2,1)S(1)}, u32[]{:S(2)}, u32[]{:S(2)}) %collective-permute-start.35) | collective-permute-done | bytes 786464 | tf_op jit(solution)/shard_map/ppermute | solution.py:454
  837.2 39.0 %collective-permute-done.36.refs_2_ = bf16[2,256,768]{2,1,0:T(8,128)(2,1)S(1)} collective-permute-done((bf16[2,256,768]{2,1,0:T(8,128)(2,1)S(1)}, bf16[2,256,768]{2,1,0:T(8,128)(2,1)S(1)}, u32[]{:S(2)}, u32[]{:S(2)}) %collective-permute-start.36) | collective-permute-done | bytes 786464 | tf_op jit(solution)/shard_map/ppermute | solution.py:454
  877.1 60.7 %collective-permute-done.37.refs_3_ = bf16[2,256,768]{2,1,0:T(8,128)(2,1)} collective-permute-done((bf16[2,256,768]{2,1,0:T(8,128)(2,1)S(1)}, bf16[2,256,768]{2,1,0:T(8,128)(2,1)}, u32[]{:S(2)}, u32[]{:S(2)}) %collective-permute-start.37) | collective-permute-done | bytes 786464 | tf_op jit(solution)/shard_map/ppermute | solution.py:454
  937.8 9.1 merge_heads.1
  948.5 19.8 %merge_wide.1 = (f32[256,16384]{1,0:T(8,128)}, f32[4,256,128]{2,1,0:T(8,128)}) custom-call(s32[2]{0:T(128)} %pad_add_fusion.place_ref, bf16[2,256,2048]{2,1,0:T(8,128)(2,1)} %copy-done.4, bf16[2,256,2048]{2,1,0:T(8,128)(2,1)} %collective-permute-done.42.refs_1_, bf16[2,256,2048]{2,1,0:T(8,128)(2,1)} %collective-permute-done.43.refs_2_, ...), custom_call_target="tpu_custom_call" | custom-call | tf_op jit(solution)/shard_map/merge_wide/pallas_call | solution.py:369
  (272 shorter events, 246.7 us)
Async XLA Ops:
  7.2 78.6 %all-gather.5.cloned.1.call-start = ((), (), s32[]{:S(2)}) async-start(), calls=%async_computation.4 | async-start | bytes 3932160 | tf_op jit(solution)/shard_map/all_gather | solution.py:263
  19.4 94.5 %all-gather.7.cloned.1.call-start = ((), (), s32[]{:S(2)}) async-start(), calls=%async_computation.5 | async-start | bytes 1310720 | tf_op jit(solution)/shard_map/all_gather | solution.py:263
  33.7 231.5 %all-gather.9.cloned.1.call-start = ((), (), s32[]{:S(2)}) async-start(), calls=%async_computation.6 | async-start | bytes 10485760 | tf_op jit(solution)/shard_map/all_gather | solution.py:263
  38.2 308.0 %all-gather.11.cloned.1.call-start = ((), (), s32[]{:S(2)}) async-start(), calls=%async_computation.7 | async-start | bytes 5242880 | tf_op jit(solution)/shard_map/all_gather | solution.py:263
  128.0 34.9 %collective-permute-start.20 = (bf16[128,2048]{1,0:T(8,128)(2,1)S(1)}, bf16[128,2048]{1,0:T(8,128)(2,1)S(1)}, u32[]{:S(2)}, u32[]{:S(2)}) collective-permute-start(bf16[128,2048]{1,0:T(8,128)(2,1)S(1)} %bitcast.248), channel_id=1, source_target_pairs={{0,24},{8,16},{16,8},{24,0},{1,25},{9,17},{17,9},{25,1},{2,26},{10... | collective-permute-start | bytes 1572872 | tf_op jit(solution)/shard_map/ppermute | solution.py:244
  130.4 43.9 %collective-permute-start.19 = (bf16[128,2048]{1,0:T(8,128)(2,1)S(1)}, bf16[128,2048]{1,0:T(8,128)(2,1)}, u32[]{:S(2)}, u32[]{:S(2)}) collective-permute-start(bf16[128,2048]{1,0:T(8,128)(2,1)S(1)} %bitcast.249), channel_id=1, source_target_pairs={{0,16},{8,24},{16,0},{24,8},{1,17},{9,25},{17,1},{25,9},{2,18},{10... | collective-permute-start | bytes 1572872 | tf_op jit(solution)/shard_map/ppermute | solution.py:244
  133.3 410.5 %reduce-scatter.7.cloned.1.call-start = ((), (), s32[]{:S(2)}) async-start(), calls=%async_computation.9 | async-start | bytes 1310720 | tf_op jit(solution)/shard_map/reduce_scatter | solution.py:267
  140.4 33.9 %collective-permute-start.18 = (bf16[128,2048]{1,0:T(8,128)(2,1)S(1)}, bf16[128,2048]{1,0:T(8,128)(2,1)S(1)}, u32[]{:S(2)}, u32[]{:S(2)}) collective-permute-start(bf16[128,2048]{1,0:T(8,128)(2,1)S(1)} %bitcast.250), channel_id=1, source_target_pairs={{0,8},{8,0},{16,24},{24,16},{1,9},{9,1},{17,25},{25,17},{2,10},{10... | collective-permute-start | bytes 1572872 | tf_op jit(solution)/shard_map/ppermute | solution.py:244
  154.7 30.8 %collective-permute-start.11 = (bf16[128,2048]{1,0:T(8,128)(2,1)S(1)}, bf16[128,2048]{1,0:T(8,128)(2,1)S(1)}, u32[]{:S(2)}, u32[]{:S(2)}) collective-permute-start(bf16[128,2048]{1,0:T(8,128)(2,1)S(1)} %multiply_convert_fusion.4), channel_id=1, source_target_pairs={{0,24},{8,16},{16,8},{24,0},{1,25},{9,17},{17,9},{25,1},{2,26},{10... | collective-permute-start | bytes 1572872 | tf_op jit(solution)/shard_map/ppermute | solution.py:244
  157.2 38.6 %collective-permute-start.10 = (bf16[128,2048]{1,0:T(8,128)(2,1)S(1)}, bf16[128,2048]{1,0:T(8,128)(2,1)S(1)}, u32[]{:S(2)}, u32[]{:S(2)}) collective-permute-start(bf16[128,2048]{1,0:T(8,128)(2,1)S(1)} %multiply_convert_fusion.4), channel_id=1, source_target_pairs={{0,16},{8,24},{16,0},{24,8},{1,17},{9,25},{17,1},{25,9},{2,18},{10... | collective-permute-start | bytes 1572872 | tf_op jit(solution)/shard_map/ppermute | solution.py:244
  162.9 33.0 %collective-permute-start.9 = (bf16[128,2048]{1,0:T(8,128)(2,1)S(1)}, bf16[128,2048]{1,0:T(8,128)(2,1)S(1)}, u32[]{:S(2)}, u32[]{:S(2)}) collective-permute-start(bf16[128,2048]{1,0:T(8,128)(2,1)S(1)} %multiply_convert_fusion.4), channel_id=1, source_target_pairs={{0,8},{8,0},{16,24},{24,16},{1,9},{9,1},{17,25},{25,17},{2,10},{10... | collective-permute-start | bytes 1572872 | tf_op jit(solution)/shard_map/ppermute | solution.py:244
  386.6 33.7 %collective-permute-start.17 = (bf16[128,2048]{1,0:T(8,128)(2,1)S(1)}, bf16[128,2048]{1,0:T(8,128)(2,1)S(1)}, u32[]{:S(2)}, u32[]{:S(2)}) collective-permute-start(bf16[128,2048]{1,0:T(8,128)(2,1)S(1)} %get-tuple-element.46), channel_id=1, source_target_pairs={{0,24},{8,16},{16,8},{24,0},{1,25},{9,17},{17,9},{25,1},{2,26},{10... | collective-permute-start | bytes 1572872 | tf_op jit(solution)/shard_map/ppermute | solution.py:254
  389.1 42.0 %collective-permute-start.16 = (bf16[128,2048]{1,0:T(8,128)(2,1)S(1)}, bf16[128,2048]{1,0:T(8,128)(2,1)S(1)}, u32[]{:S(2)}, u32[]{:S(2)}) collective-permute-start(bf16[128,2048]{1,0:T(8,128)(2,1)S(1)} %get-tuple-element.47), channel_id=1, source_target_pairs={{0,16},{8,24},{16,0},{24,8},{1,17},{9,25},{17,1},{25,9},{2,18},{10... | collective-permute-start | bytes 1572872 | tf_op jit(solution)/shard_map/ppermute | solution.py:254
  397.8 33.4 %collective-permute-start.15 = (bf16[128,2048]{1,0:T(8,128)(2,1)S(1)}, bf16[128,2048]{1,0:T(8,128)(2,1)S(1)}, u32[]{:S(2)}, u32[]{:S(2)}) collective-permute-start(bf16[128,2048]{1,0:T(8,128)(2,1)S(1)} %get-tuple-element.45), channel_id=1, source_target_pairs={{0,8},{8,0},{16,24},{24,16},{1,9},{9,1},{17,25},{25,17},{2,10},{10... | collective-permute-start | bytes 1572872 | tf_op jit(solution)/shard_map/ppermute | solution.py:254
  468.8 170.9 %reduce-scatter.9.cloned.1.call-start = ((), (), s32[]{:S(2)}) async-start(), calls=%async_computation.10 | async-start | bytes 10485760 | tf_op jit(solution)/shard_map/reduce_scatter | solution.py:267
  482.6 237.0 %reduce-scatter.11.cloned.1.call-start = ((), (), s32[]{:S(2)}) async-start(), calls=%async_computation.11 | async-start | bytes 5242880 | tf_op jit(solution)/shard_map/reduce_scatter | solution.py:267
  492.5 290.7 %reduce-scatter.5.cloned.1.call-start = ((), (), s32[]{:S(2)}) async-start(), calls=%async_computation.8 | async-start | bytes 3932160 | tf_op jit(solution)/shard_map/reduce_scatter | solution.py:267
  540.2 102.6 %collective-permute-start.33 = (bf16[128,2048]{1,0:T(8,128)(2,1)}, bf16[128,2048]{1,0:T(8,128)(2,1)S(1)}, u32[]{:S(2)}, u32[]{:S(2)}) collective-permute-start(bf16[128,2048]{1,0:T(8,128)(2,1)} %get-tuple-element.36), channel_id=1, source_target_pairs={{0,24},{8,16},{16,8},{24,0},{1,25},{9,17},{17,9},{25,1},{2,26},{10... | collective-permute-start | bytes 1572872 | tf_op jit(solution)/shard_map/ppermute | solution.py:254
  541.2 101.6 %collective-permute-start.32 = (bf16[128,2048]{1,0:T(8,128)(2,1)}, bf16[128,2048]{1,0:T(8,128)(2,1)}, u32[]{:S(2)}, u32[]{:S(2)}) collective-permute-start(bf16[128,2048]{1,0:T(8,128)(2,1)} %get-tuple-element.37), channel_id=1, source_target_pairs={{0,16},{8,24},{16,0},{24,8},{1,17},{9,25},{17,1},{25,9},{2,18},{10... | collective-permute-start | bytes 1572872 | tf_op jit(solution)/shard_map/ppermute | solution.py:254
  542.8 100.0 %collective-permute-start.31 = (bf16[128,2048]{1,0:T(8,128)(2,1)}, bf16[128,2048]{1,0:T(8,128)(2,1)}, u32[]{:S(2)}, u32[]{:S(2)}) collective-permute-start(bf16[128,2048]{1,0:T(8,128)(2,1)} %get-tuple-element.35), channel_id=1, source_target_pairs={{0,8},{8,0},{16,24},{24,16},{1,9},{9,1},{17,25},{25,17},{2,10},{10... | collective-permute-start | bytes 1572872 | tf_op jit(solution)/shard_map/ppermute | solution.py:254
  543.7 28.1 %collective-permute-start.38 = (bf16[64,2048]{1,0:T(8,128)(2,1)}, bf16[64,2048]{1,0:T(8,128)(2,1)S(1)}, u32[]{:S(2)}, u32[]{:S(2)}) collective-permute-start(bf16[64,2048]{1,0:T(8,128)(2,1)} %reduce-scatter.7.cloned.1.call-done), channel_id=1, source_target_pairs={{0,8},{8,0},{16,24},{24,16},{1,9},{9,1},{17,25},{25,17},{2,10},{10... | collective-permute-start | bytes 786440 | tf_op jit(solution)/shard_map/ppermute | solution.py:454
  544.8 29.3 %collective-permute-start.39 = (bf16[64,2048]{1,0:T(8,128)(2,1)}, bf16[64,2048]{1,0:T(8,128)(2,1)S(1)}, u32[]{:S(2)}, u32[]{:S(2)}) collective-permute-start(bf16[64,2048]{1,0:T(8,128)(2,1)} %reduce-scatter.7.cloned.1.call-done), channel_id=1, source_target_pairs={{0,16},{8,24},{16,0},{24,8},{1,17},{9,25},{17,1},{25,9},{2,18},{10... | collective-permute-start | bytes 786440 | tf_op jit(solution)/shard_map/ppermute | solution.py:454
  642.8 147.9 %collective-permute-start.41 = (bf16[256,2048]{1,0:T(8,128)(2,1)}, bf16[256,2048]{1,0:T(8,128)(2,1)}, u32[]{:S(2)}, u32[]{:S(2)}) collective-permute-start(bf16[256,2048]{1,0:T(8,128)(2,1)} %get-tuple-element.34), channel_id=1, source_target_pairs={{0,1},{1,0},{2,3},{3,2},{4,5},{5,4},{6,7},{7,6},{8,9},{9,8},{10,11... | collective-permute-start | bytes 3145736 | tf_op jit(solution)/shard_map/ppermute | solution.py:239
  719.6 74.1 %collective-permute-start.45 = (bf16[256,2048]{1,0:T(8,128)(2,1)}, bf16[256,2048]{1,0:T(8,128)(2,1)}, u32[]{:S(2)}, u32[]{:S(2)}) collective-permute-start(bf16[256,2048]{1,0:T(8,128)(2,1)} %reduce-scatter.11.cloned.1.call-done), channel_id=1, source_target_pairs={{0,8},{8,0},{16,24},{24,16},{1,9},{9,1},{17,25},{25,17},{2,10},{10... | collective-permute-start | bytes 3145736 | tf_op jit(solution)/shard_map/ppermute | solution.py:454
  721.0 73.2 %collective-permute-start.46 = (bf16[256,2048]{1,0:T(8,128)(2,1)}, bf16[256,2048]{1,0:T(8,128)(2,1)}, u32[]{:S(2)}, u32[]{:S(2)}) collective-permute-start(bf16[256,2048]{1,0:T(8,128)(2,1)} %reduce-scatter.11.cloned.1.call-done), channel_id=1, source_target_pairs={{0,16},{8,24},{16,0},{24,8},{1,17},{9,25},{17,1},{25,9},{2,18},{10... | collective-permute-start | bytes 3145736 | tf_op jit(solution)/shard_map/ppermute | solution.py:454
  787.6 26.9 %collective-permute-start.47 = (bf16[256,2048]{1,0:T(8,128)(2,1)S(1)}, bf16[256,2048]{1,0:T(8,128)(2,1)S(1)}, u32[]{:S(2)}, u32[]{:S(2)}) collective-permute-start(bf16[256,2048]{1,0:T(8,128)(2,1)S(1)} %copy-done.17), channel_id=1, source_target_pairs={{0,24},{8,16},{16,8},{24,0},{1,25},{9,17},{17,9},{25,1},{2,26},{10... | collective-permute-start | bytes 3145736 | tf_op jit(solution)/shard_map/ppermute | solution.py:454
  790.1 41.3 %collective-permute-start.35 = (bf16[2,256,768]{2,1,0:T(8,128)(2,1)S(1)}, bf16[2,256,768]{2,1,0:T(8,128)(2,1)S(1)}, u32[]{:S(2)}, u32[]{:S(2)}) collective-permute-start(bf16[2,256,768]{2,1,0:T(8,128)(2,1)S(1)} %pad_maximum_fusion.14.refs_0_), channel_id=1, source_target_pairs={{0,8},{8,0},{16,24},{24,16},{1,9},{9,1},{17,25},{25,17},{2,10},{10... | collective-permute-start | bytes 2359304 | tf_op jit(solution)/shard_map/ppermute | solution.py:454
  792.2 156.4 %collective-permute-start.42 = (bf16[2,256,2048]{2,1,0:T(8,128)(2,1)S(1)}, bf16[2,256,2048]{2,1,0:T(8,128)(2,1)}, u32[]{:S(2)}, u32[]{:S(2)}) collective-permute-start(bf16[2,256,2048]{2,1,0:T(8,128)(2,1)S(1)} %pad_maximum_fusion.12.refs_0_), channel_id=1, source_target_pairs={{0,8},{8,0},{16,24},{24,16},{1,9},{9,1},{17,25},{25,17},{2,10},{10... | collective-permute-start | bytes 6291464 | tf_op jit(solution)/shard_map/ppermute | solution.py:454
  793.7 154.8 %collective-permute-start.43 = (bf16[2,256,2048]{2,1,0:T(8,128)(2,1)S(1)}, bf16[2,256,2048]{2,1,0:T(8,128)(2,1)}, u32[]{:S(2)}, u32[]{:S(2)}) collective-permute-start(bf16[2,256,2048]{2,1,0:T(8,128)(2,1)S(1)} %pad_maximum_fusion.12.refs_0_), channel_id=1, source_target_pairs={{0,16},{8,24},{16,0},{24,8},{1,17},{9,25},{17,1},{25,9},{2,18},{10... | collective-permute-start | bytes 6291464 | tf_op jit(solution)/shard_map/ppermute | solution.py:454
  794.3 154.3 %collective-permute-start.44 = (bf16[2,256,2048]{2,1,0:T(8,128)(2,1)S(1)}, bf16[2,256,2048]{2,1,0:T(8,128)(2,1)}, u32[]{:S(2)}, u32[]{:S(2)}) collective-permute-start(bf16[2,256,2048]{2,1,0:T(8,128)(2,1)S(1)} %pad_maximum_fusion.12.refs_0_), channel_id=1, source_target_pairs={{0,24},{8,16},{16,8},{24,0},{1,25},{9,17},{17,9},{25,1},{2,26},{10... | collective-permute-start | bytes 6291464 | tf_op jit(solution)/shard_map/ppermute | solution.py:454
  814.5 61.7 %collective-permute-start.36 = (bf16[2,256,768]{2,1,0:T(8,128)(2,1)S(1)}, bf16[2,256,768]{2,1,0:T(8,128)(2,1)S(1)}, u32[]{:S(2)}, u32[]{:S(2)}) collective-permute-start(bf16[2,256,768]{2,1,0:T(8,128)(2,1)S(1)} %pad_maximum_fusion.14.refs_0_), channel_id=1, source_target_pairs={{0,16},{8,24},{16,0},{24,8},{1,17},{9,25},{17,1},{25,9},{2,18},{10... | collective-permute-start | bytes 2359304 | tf_op jit(solution)/shard_map/ppermute | solution.py:454
  831.4 106.4 %collective-permute-start.37 = (bf16[2,256,768]{2,1,0:T(8,128)(2,1)S(1)}, bf16[2,256,768]{2,1,0:T(8,128)(2,1)}, u32[]{:S(2)}, u32[]{:S(2)}) collective-permute-start(bf16[2,256,768]{2,1,0:T(8,128)(2,1)S(1)} %pad_maximum_fusion.14.refs_0_), channel_id=1, source_target_pairs={{0,24},{8,16},{16,8},{24,0},{1,25},{9,17},{17,9},{25,1},{2,26},{10... | collective-permute-start | bytes 2359304 | tf_op jit(solution)/shard_map/ppermute | solution.py:454
  (62 other events, 1107.0 us)
Sparse Core Ops, SparseCore 0:
  19.6 66.1 all-gather.4
  87.3 26.5 all-gather.6
  116.0 149.1 all-gather.8
  267.2 78.9 all-gather.10
  468.9 24.6 reduce-scatter.6
  496.5 143.1 reduce-scatter.8
  642.1 77.4 reduce-scatter.10
  722.4 60.7 reduce-scatter.4

commit v2 on v0

--- a/solution.py
+++ b/solution.py
@@ -1,6 +1,10 @@
+import functools
+
 import jax
 import jax.numpy as jnp
 from jax import lax
+from jax.experimental import pallas as pl
+from jax.experimental.pallas import tpu as pltpu
 from jax.sharding import PartitionSpec as P
 
 HEAD_DIM = 64
@@ -9,6 +13,7 @@
 EPSILON = 1e-05
 THETA = 130000.0
 SCALE = 0.125
+LANES = 128
 
 
 def outer_sum(left, right):
@@ -95,7 +100,7 @@
     return jnp.where((columns <= rows)[None], scores, -1e30)
 
 
-def on_device(hidden_in, norm_one, w_qkv, w_out, norm_two, w_gate_up, w_down, grad_out):
+def gathered_plan(hidden_in, norm_one, w_qkv, w_out, norm_two, w_gate_up, w_down, grad_out):
     inputs = hidden_in[0].astype(jnp.float32)
     tokens = inputs.shape[0]
     width = inputs.shape[1]
@@ -226,7 +231,825 @@
     )
 
 
+def xor_pairs(size, offset):
+    return [(i, i ^ offset) for i in range(size)]
+
+
+def swap_cores(values):
+    return lax.ppermute(values, "fsdp", xor_pairs(8, 1))
+
+
+def swap_rows(values, offset):
+    return lax.ppermute(values, "fsdp", xor_pairs(8, 2 * offset))
+
+
+def swap_seq(values, offset):
+    return lax.ppermute(values, "seq", xor_pairs(4, offset))
+
+
+def fence(*values):
+    return lax.optimization_barrier(values)
+
+
+def window(needed, work):
+    outs = jax.eval_shape(work)
+    return lax.cond(
+        needed,
+        work,
+        lambda: jax.tree.map(lambda out: jnp.zeros(out.shape, out.dtype), outs),
+    )
+
+
+def halves(block):
+    half = block.shape[0] // 2
+    return block[:half], block[half:]
+
+
+def gather_one(block):
+    first, second = halves(block)
+    return swap_seq(first, 1), swap_seq(second, 2), swap_rows(block, 2)
+
+
+def gather_two(block, first_more, second_more, next_row):
+    first, second = halves(block)
+    first = jnp.concatenate([first, first_more])
+    second = jnp.concatenate([second, second_more])
+    next_first, next_second = halves(next_row)
+    return (first, second, next_first, next_second), (
+        swap_seq(first, 2),
+        swap_seq(second, 1),
+        swap_seq(next_first, 1),
+        swap_seq(next_second, 2),
+    )
+
+
+def gather_three(held, arrived):
+    first, second, next_first, next_second = held
+    first_more, second_more, next_first_more, next_second_more = arrived
+    own = jnp.concatenate([first, first_more, second, second_more])
+    next_first = jnp.concatenate([next_first, next_first_more])
+    next_second = jnp.concatenate([next_second, next_second_more])
+    return (own, next_first, next_second), (
+        swap_cores(own),
+        swap_seq(next_first, 2),
+        swap_seq(next_second, 1),
+    )
+
+
+def gather_four(held, arrived):
+    own, next_first, next_second = held
+    other, next_first_more, next_second_more = arrived
+    next_own = jnp.concatenate([next_first, next_first_more, next_second, next_second_more])
+    return (own, other, next_own), swap_cores(next_own)
+
+
+def row_one(block):
+    first, second = halves(block)
+    return swap_seq(first, 1), swap_seq(second, 2)
+
+
+def row_two(block, first_more, second_more):
+    first, second = halves(block)
+    first = jnp.concatenate([first, first_more])
+    second = jnp.concatenate([second, second_more])
+    return (first, second), (swap_seq(first, 2), swap_seq(second, 1))
+
+
+def row_three(held, arrived):
+    own = jnp.concatenate([held[0], arrived[0], held[1], arrived[1]])
+    return own, swap_cores(own)
+
+
+def send_quarters(partial):
+    quarter = partial.shape[0] // 4
+    return swap_seq(partial[quarter : 2 * quarter], 2), swap_seq(partial[3 * quarter :], 1)
+
+
+def add_quarters(partial, first, second):
+    quarter = partial.shape[0] // 4
+    return (
+        partial[:quarter].astype(jnp.float32) + first.astype(jnp.float32),
+        partial[2 * quarter : 3 * quarter].astype(jnp.float32) + second.astype(jnp.float32),
+    )
+
+
+def send_eighths(first, second):
+    half = first.shape[0] // 2
+    return (
+        swap_seq(first[half:].astype(jnp.bfloat16), 1),
+        swap_seq(second[half:].astype(jnp.bfloat16), 2),
+    )
+
+
+def add_eighths(first, second, first_more, second_more):
+    half = first.shape[0] // 2
+    return jnp.concatenate(
+        [
+            first[:half] + first_more.astype(jnp.float32),
+            second[:half] + second_more.astype(jnp.float32),
+        ]
+    )
+
+
+def add(first, second):
+    return (first.astype(jnp.float32) + second.astype(jnp.float32)).astype(jnp.bfloat16)
+
+
+def share_one(first, second):
+    return swap_seq(first, 1), swap_seq(second, 2)
+
+
+def share_two(first, second, first_more, second_more):
+    first = jnp.concatenate([first, first_more])
+    second = jnp.concatenate([second, second_more])
+    return (first, second), (swap_seq(first, 2), swap_seq(second, 1))
+
+
+def shared(held, arrived):
+    return held[0], arrived[0], held[1], arrived[1]
+
+
+ROWS = [[0, 2, 4, 6], [1, 3, 5, 7]]
+ROW_PAIRS = [[0, 2], [4, 6], [1, 3], [5, 7]]
+ROW_ORDER = (0, 2, 1, 3)
+
+
+def gather_rows(block, groups):
+    return lax.all_gather(block, "fsdp", axis=0, tiled=True, axis_index_groups=groups)
+
+
+def scatter_rows(term, groups):
+    return lax.psum_scatter(
+        term.astype(jnp.bfloat16),
+        "fsdp",
+        scatter_dimension=0,
+        tiled=True,
+        axis_index_groups=groups,
+    )
+
+
+def lane_mask(rows):
+    return lax.broadcasted_iota(jnp.int32, (rows, LANES), 1) < LANES // 2
+
+
+def mixed_row(k):
+    return (k & 4) | ((k & 1) << 1) | ((k & 2) >> 1)
+
+
+def slice_wide(weight, gain, place, groups, chunk):
+    rows = weight.shape[0]
+
+    def body(place_ref, own_ref, other_ref, gain_ref, *out_refs):
+        for weight_ref, out_ref in zip((own_ref, other_ref), out_refs):
+            for step in range(2):
+                start = pl.multiple_of((place_ref[2] ^ step) * chunk, LANES)
+                columns = weight_ref[:, pl.ds(start, chunk)].astype(jnp.float32)
+                out_ref[step] = (columns * gain_ref[...]).astype(jnp.bfloat16)
+
+    def columns_of(core):
+        return pl.BlockSpec(
+            (rows, 2 * chunk), lambda k, p: (0, (mixed_row(k) * 2 + (p[1] ^ core)) * 4 + p[0])
+        )
+
+    out = jax.ShapeDtypeStruct((2, rows, groups * chunk), jnp.bfloat16)
+    return pl.pallas_call(
+        body,
+        grid_spec=pltpu.PrefetchScalarGridSpec(
+            num_scalar_prefetch=1,
+            grid=(groups,),
+            in_specs=[columns_of(0), columns_of(1), pl.BlockSpec((rows, 1), lambda k, p: (0, 0))],
+            out_specs=[pl.BlockSpec((2, rows, chunk), lambda k, p: (0, 0, k))] * 2,
+        ),
+        out_shape=[out, out],
+        name="slice_wide",
+    )(place, weight, weight, gain)
+
+
+def slice_heads(weight, gain, place, heads):
+    rows = weight.shape[0]
+    part = weight.shape[1] // 3
+
+    def body(place_ref, weight_ref, gain_ref, *out_refs):
+        own_seq, own_core = place_ref[0], place_ref[1]
+        odd = (own_seq % 2) == 1
+        low = lane_mask(rows)
+        for core in range(2):
+            for pair in range(heads // 2):
+                tiles = []
+                for head in (2 * pair, 2 * pair + 1):
+                    start = (head * 2 + (own_core ^ core)) * (4 * HEAD_DIM) + (
+                        own_seq // 2
+                    ) * LANES
+                    tile = weight_ref[:, pl.ds(pl.multiple_of(start, LANES), LANES)]
+                    tiles.append(tile.astype(jnp.float32) * gain_ref[...])
+                turned = [pltpu.roll(tile, LANES // 2, axis=1) for tile in tiles]
+                first = jnp.where(odd, turned[0], tiles[0])
+                second = jnp.where(odd, tiles[1], turned[1])
+                out_refs[core][:, pair * LANES : (pair + 1) * LANES] = jnp.where(
+                    low, first, second
+                ).astype(jnp.bfloat16)
+
+    out = jax.ShapeDtypeStruct((rows, 3 * heads * HEAD_DIM), jnp.bfloat16)
+    return pl.pallas_call(
+        body,
+        grid_spec=pltpu.PrefetchScalarGridSpec(
+            num_scalar_prefetch=1,
+            grid=(3,),
+            in_specs=[
+                pl.BlockSpec((rows, part), lambda k, p: (0, k)),
+                pl.BlockSpec((rows, 1), lambda k, p: (0, 0)),
+            ],
+            out_specs=[pl.BlockSpec((rows, heads * HEAD_DIM), lambda k, p: (0, k))] * 2,
+        ),
+        out_shape=[out, out],
+        name="slice_heads",
+    )(place, weight, gain)
+
+
+def fold(products):
+    total = products[:, :LANES]
+    for k in range(1, products.shape[1] // LANES):
+        total = total + products[:, k * LANES : (k + 1) * LANES]
+    return total
+
+
+PIECES = (((0, 0), (0, 2), (1, 0), (1, 2)), ((2, 0), (3, 0), (2, 2), (3, 2)))
+
+
+def merge_wide(pieces, weight, gain, place, groups, chunk):
+    rows = weight.shape[0]
+    width = 16 * chunk
+
+    def body(place_ref, *refs):
+        weight_ref, gain_ref = refs[4:6]
+        out_ref, sum_ref = refs[6:]
+
+        @pl.when(pl.program_id(0) == 0)
+        def _():
+            sum_ref[...] = jnp.zeros_like(sum_ref)
+
+        for r in range(4):
+            for k in range(4):
+                block = ((place_ref[1] ^ (k // 2)) * 4 + (place_ref[0] ^ r)) * 2 + (
+                    place_ref[2] ^ (k % 2)
+                )
+                columns = pl.ds(pl.multiple_of(block * chunk, LANES), chunk)
+                term = refs[PIECES[k // 2][r][0]][PIECES[k // 2][r][1] + k % 2].astype(jnp.float32)
+                out_ref[:, columns] = term * gain_ref[...]
+                sum_ref[place_ref[0] ^ r] += fold(
+                    term * weight_ref[:, columns].astype(jnp.float32)
+                )
+
+    wide = pl.BlockSpec((rows, width), lambda k, p: (0, mixed_row(k)))
+    return pl.pallas_call(
+        body,
+        grid_spec=pltpu.PrefetchScalarGridSpec(
+            num_scalar_prefetch=1,
+            grid=(groups,),
+            in_specs=[pl.BlockSpec((4, rows, chunk), lambda k, p: (0, 0, k))] * 4
+            + [wide, pl.BlockSpec((rows, 1), lambda k, p: (0, 0))],
+            out_specs=[wide, pl.BlockSpec((4, rows, LANES), lambda k, p: (0, 0, 0))],
+        ),
+        out_shape=[
+            jax.ShapeDtypeStruct(weight.shape, jnp.float32),
+            jax.ShapeDtypeStruct((4, rows, LANES), jnp.float32),
+        ],
+        compiler_params=pltpu.CompilerParams(vmem_limit_bytes=32 * 1024 * 1024),
+        name="merge_wide",
+    )(place, *pieces, weight, gain)
+
+
+def merge_heads(pieces, weight, gain, place, heads):
+    rows = weight.shape[0]
+    part = weight.shape[1] // 3
+
+    def body(place_ref, *refs):
+        weight_ref, gain_ref = refs[4:6]
+        out_ref, sum_ref = refs[6:]
+        own_seq, own_core = place_ref[0], place_ref[1]
+        odd = (own_seq % 2) == 1
+        low = lane_mask(rows)
+
+        @pl.when(pl.program_id(0) == 0)
+        def _():
+            sum_ref[...] = jnp.zeros_like(sum_ref)
+
+        for core in range(2):
+            for pair in range(heads // 2):
+                for couple in range(2):
+                    first, second = (
+                        refs[at][block // 2, :, pair * LANES : (pair + 1) * LANES].astype(
+                            jnp.float32
+                        )
+                        for at, block in PIECES[core][2 * couple : 2 * couple + 2]
+                    )
+                    turned_first = pltpu.roll(first, LANES // 2, axis=1)
+                    turned_second = pltpu.roll(second, LANES // 2, axis=1)
+                    for head, even_tile, odd_tile in (
+                        (
+                            2 * pair,
+                            jnp.where(low, first, turned_second),
+                            jnp.where(low, second, turned_first),
+                        ),
+                        (
+                            2 * pair + 1,
+                            jnp.where(low, turned_first, second),
+                            jnp.where(low, turned_second, first),
+                        ),
+                    ):
+                        tile = jnp.where(odd, odd_tile, even_tile)
+                        start = (head * 2 + (own_core ^ core)) * (4 * HEAD_DIM) + (
+                            (own_seq // 2) ^ couple
+                        ) * LANES
+                        columns = pl.ds(pl.multiple_of(start, LANES), LANES)
+                        out_ref[:, columns] = tile * gain_ref[...]
+                        sum_ref[(own_seq // 2) ^ couple] += tile * weight_ref[:, columns].astype(
+                            jnp.float32
+                        )
+
+    wide = pl.BlockSpec((rows, part), lambda k, p: (0, k))
+    return pl.pallas_call(
+        body,
+        grid_spec=pltpu.PrefetchScalarGridSpec(
+            num_scalar_prefetch=1,
+            grid=(3,),
+            in_specs=[pl.BlockSpec((2, rows, heads * HEAD_DIM), lambda k, p: (0, 0, k))] * 4
+            + [wide, pl.BlockSpec((rows, 1), lambda k, p: (0, 0))],
+            out_specs=[wide, pl.BlockSpec((2, rows, LANES), lambda k, p: (0, 0, 0))],
+        ),
+        out_shape=[
+            jax.ShapeDtypeStruct(weight.shape, jnp.float32),
+            jax.ShapeDtypeStruct((2, rows, LANES), jnp.float32),
+        ],
+        name="merge_heads",
+    )(place, *pieces, weight, gain)
+
+
+def dot_rows(left, right):
+    return lax.dot_general(
+        left, right, (((1,), (1,)), ((), ())), preferred_element_type=jnp.float32
+    )
+
+
+def swap_head_halves(values):
+    lanes = lax.broadcasted_iota(jnp.int32, values.shape, 1) % HEAD_DIM
+    half = HEAD_DIM // 2
+    return jnp.where(
+        lanes < half,
+        pltpu.roll(values, LANES - half, axis=1),
+        pltpu.roll(values, half, axis=1),
+    )
+
+
+def softmax_of(query, keys, visible):
+    scores = jnp.where(visible, dot_rows(query, keys) * SCALE, -1e30)
+    weights = jnp.exp(scores - jnp.max(scores, axis=1, keepdims=True))
+    return weights / jnp.sum(weights, axis=1, keepdims=True)
+
+
+def attend(mixed, cosine, sine, rows_at, columns_at):
+    length = cosine.shape[0]
+    total, columns = mixed.shape
+    part = columns // 3
+
+    def body(mixed_ref, cosine_ref, sine_ref, rows_ref, columns_ref, out_ref, turned_ref):
+        visible = columns_ref[...] <= rows_ref[...]
+        low = lane_mask(length)
+        for k in range(2 * part // LANES):
+            lanes = slice(k * LANES, (k + 1) * LANES)
+            heads = mixed_ref[:, lanes].astype(jnp.float32)
+            turned_ref[:, lanes] = (
+                heads * cosine_ref[...] + swap_head_halves(heads) * sine_ref[...]
+            ).astype(jnp.bfloat16)
+        for k in range(part // LANES):
+            query = turned_ref[:, k * LANES : (k + 1) * LANES]
+            keys = turned_ref[:, part + k * LANES : part + (k + 1) * LANES]
+            values = mixed_ref[:, 2 * part + k * LANES : 2 * part + (k + 1) * LANES]
+            zero = jnp.zeros_like(query)
+            outs = []
+            for own in (low, ~low):
+                probabilities = softmax_of(jnp.where(own, query, zero), keys, visible)
+                outs.append(
+                    jnp.dot(
+                        probabilities.astype(jnp.bfloat16),
+                        values,
+                        preferred_element_type=jnp.float32,
+                    )
+                )
+            out_ref[:, k * LANES : (k + 1) * LANES] = jnp.where(low, outs[0], outs[1]).astype(
+                jnp.bfloat16
+            )
+
+    def whole(shape):
+        return pl.BlockSpec(shape, lambda i: (0, 0))
+
+    return pl.pallas_call(
+        body,
+        grid=(total // length,),
+        in_specs=[
+            pl.BlockSpec((length, columns), lambda i: (i, 0)),
+            whole((length, LANES)),
+            whole((length, LANES)),
+            whole((length, 1)),
+            whole((1, length)),
+        ],
+        out_specs=[
+            pl.BlockSpec((length, part), lambda i: (i, 0)),
+            pl.BlockSpec((length, 2 * part), lambda i: (i, 0)),
+        ],
+        out_shape=[
+            jax.ShapeDtypeStruct((total, part), jnp.bfloat16),
+            jax.ShapeDtypeStruct((total, 2 * part), jnp.bfloat16),
+        ],
+        compiler_params=pltpu.CompilerParams(vmem_limit_bytes=40 * 1024 * 1024),
+        cost_estimate=pl.CostEstimate(
+            flops=8 * total * length * part,
+            bytes_accessed=12 * total * part,
+            transcendentals=total * length * part // HEAD_DIM,
+        ),
+        name="attend",
+    )(mixed, cosine, sine, rows_at, columns_at)
+
+
+def attend_back(turned, mixed, grad_heads, cosine, sine, rows_at, columns_at):
+    length = cosine.shape[0]
+    total, columns = mixed.shape
+    part = columns // 3
+
+    def body(
+        turned_ref, values_ref, grad_ref, cosine_ref, sine_ref, rows_ref, columns_ref, out_ref
+    ):
+        visible = columns_ref[...] <= rows_ref[...]
+        low = lane_mask(length)
+        for k in range(part // LANES):
+            lanes = slice(k * LANES, (k + 1) * LANES)
+            query = turned_ref[:, lanes]
+            keys = turned_ref[:, part + k * LANES : part + (k + 1) * LANES]
+            values = values_ref[:, lanes]
+            grad = grad_ref[:, lanes]
+            zero = jnp.zeros_like(query)
+            grads = []
+            for own in (low, ~low):
+                probabilities = softmax_of(jnp.where(own, query, zero), keys, visible)
+                grad_probabilities = dot_rows(jnp.where(own, grad, zero), values)
+                inner = jnp.sum(probabilities * grad_probabilities, axis=1, keepdims=True)
+                grad_scores = (probabilities * (grad_probabilities - inner)).astype(jnp.bfloat16)
+                grads.append(
+                    (
+                        jnp.dot(grad_scores, keys, preferred_element_type=jnp.float32) * SCALE,
+                        outer_sum(grad_scores, query) * SCALE,
+                        outer_sum(probabilities.astype(jnp.bfloat16), grad),
+                    )
+                )
+            for which in range(3):
+                heads = jnp.where(low, grads[0][which], grads[1][which])
+                if which < 2:
+                    heads = heads * cosine_ref[...] - swap_head_halves(heads) * sine_ref[...]
+                start = which * part + k * LANES
+                out_ref[:, start : start + LANES] = heads.astype(jnp.bfloat16)
+
+    def whole(shape):
+        return pl.BlockSpec(shape, lambda i: (0, 0))
+
+    return pl.pallas_call(
+        body,
+        grid=(total // length,),
+        in_specs=[
+            pl.BlockSpec((length, 2 * part), lambda i: (i, 0)),
+            pl.BlockSpec((length, part), lambda i: (i, 2)),
+            pl.BlockSpec((length, part), lambda i: (i, 0)),
+            whole((length, LANES)),
+            whole((length, LANES)),
+            whole((length, 1)),
+            whole((1, length)),
+        ],
+        out_specs=pl.BlockSpec((length, columns), lambda i: (i, 0)),
+        out_shape=jax.ShapeDtypeStruct((total, columns), jnp.bfloat16),
+        compiler_params=pltpu.CompilerParams(vmem_limit_bytes=48 * 1024 * 1024),
+        cost_estimate=pl.CostEstimate(
+            flops=20 * total * length * part,
+            bytes_accessed=16 * total * part,
+            transcendentals=total * length * part // HEAD_DIM,
+        ),
+        name="attend_back",
+    )(turned, mixed, grad_heads, cosine, sine, rows_at, columns_at)
+
+
+def place_rows(pieces, own_seq):
+    rows = pieces[0].shape[0] // 2
+    width = pieces[0].shape[1]
+    out = jnp.zeros((8 * rows, width), jnp.float32)
+    for half in range(2):
+        for k in range(4):
+            at, block = PIECES[half][k]
+            block = pieces[at][block // 2 * rows :][:rows].astype(jnp.float32)
+            out = lax.dynamic_update_slice(out, block, (((own_seq ^ k) * 2 + half) * rows, 0))
+    return out
+
+
+def mix_blocks(values):
+    blocks = jnp.split(values, 4, axis=1)
+    return jnp.concatenate([blocks[k] for k in ROW_ORDER], axis=1)
+
+
+def in_order(own, other, place):
+    return jnp.concatenate([jnp.where(place == 0, own, other), jnp.where(place == 0, other, own)])
+
+
+def sliced_plan(hidden_in, norm_one, w_qkv, w_out, norm_two, w_gate_up, w_down, grad_out):
+    own_seq = lax.axis_index("seq")
+    own_core = lax.axis_index("fsdp") % 2
+    row = lax.axis_index("fsdp") // 2
+    step = row // 2
+    place = jnp.stack([own_seq, own_core, step]).astype(jnp.int32)
+    inputs = hidden_in[0].astype(jnp.float32)
+    cotangent = grad_out[0]
+    tokens, width = inputs.shape
+    length = tokens * 4
+    chunk = w_down.shape[0] // 8
+    chip_rows = width // 4
+    gain_one = norm_one.astype(jnp.float32)[:, None]
+    gain_two = norm_two.astype(jnp.float32)[:, None]
+
+    needed = own_seq < 4
+    heads = 4
+
+    def project(rows, weight):
+        return jnp.dot(rows, weight, preferred_element_type=jnp.float32).astype(jnp.bfloat16)
+
+    def token_part(rows, k):
+        return rows[k * length : (k + 1) * length]
+
+    def backward(grad, weight):
+        return [
+            back_product(token_part(grad, k), weight).astype(jnp.bfloat16)
+            for k in range(grad.shape[0] // length)
+        ]
+
+    def own_rows(pair, rows):
+        return (
+            lax.dynamic_slice_in_dim(pair, step * rows, rows),
+            lax.dynamic_slice_in_dim(pair, (1 - step) * rows, rows),
+        )
+
+    def halves_of_chip(*chips):
+        half_rows = chip_rows // 2
+        mine = [lax.dynamic_slice_in_dim(c, own_core * half_rows, half_rows) for c in chips]
+        other = [lax.dynamic_slice_in_dim(c, (1 - own_core) * half_rows, half_rows) for c in chips]
+        return jnp.stack(mine), swap_cores(jnp.stack(other))
+
+    factor_one = lax.rsqrt(jnp.mean(inputs * inputs, axis=-1, keepdims=True) + EPSILON)
+    normed, qkv_own, qkv_other = fence(
+        (inputs * factor_one).astype(jnp.bfloat16), *slice_heads(w_qkv, gain_one, place, heads)
+    )
+    normed, qkv_chip, w_out, w_down = fence(
+        normed, in_order(qkv_own, swap_cores(qkv_other), own_core), w_out, w_down
+    )
+    qkv = gather_rows(qkv_chip, ROWS)
+    out_proj = gather_rows(lax.dynamic_slice_in_dim(w_out, own_seq * HEAD_DIM, HEAD_DIM), ROWS)
+
+    def gather_inputs():
+        flight = fence(*row_one(normed))
+        held, flight = row_two(normed, *flight)
+        wide_own, wide_other = slice_wide(w_gate_up, gain_two, place, 8, chunk)
+        *flight, wide_own, wide_other = fence(*flight, wide_own, wide_other)
+        own, other = row_three(held, flight)
+        other, *flight, wide_swapped = fence(other, *row_one(cotangent), swap_cores(wide_other))
+        held, flight = row_two(cotangent, *flight)
+        flight = fence(*flight)
+        cotangent_own, cotangent_other = row_three(held, flight)
+        return (
+            jnp.concatenate([own, other]),
+            [in_order(wide_own[k], wide_swapped[k], own_core) for k in range(2)],
+            cotangent_own,
+            *fence(cotangent_other),
+        )
+
+    normed_all, wide_chips, cotangent_own, cotangent_other = window(needed, gather_inputs)
+
+    half_block = tokens // 2
+    starts = jnp.concatenate(
+        [
+            (own_seq ^ jnp.array([0, 1, 2, 3])) * tokens,
+            (own_seq ^ jnp.array([0, 2, 1, 3])) * tokens + half_block,
+        ]
+    )
+    positions = (starts[:, None] + jnp.arange(half_block)[None]).reshape(length)
+    half = HEAD_DIM // 2
+    freqs = THETA ** (-(jnp.arange(half, dtype=jnp.float32) * 2.0) / HEAD_DIM)
+    angles = positions.astype(jnp.float32)[:, None] * freqs[None, :]
+    cosine = jnp.tile(jnp.cos(angles), (1, 4))
+    sine = jnp.tile(jnp.concatenate([-jnp.sin(angles), jnp.sin(angles)], axis=1), (1, 2))
+    tables = (cosine, sine, positions[:, None], positions[None, :])
+
+    def norm_two_of(middle):
+        factor = lax.rsqrt(jnp.mean(middle * middle, axis=-1, keepdims=True) + EPSILON)
+        return mix_blocks((middle * factor).astype(jnp.bfloat16)), factor
+
+    def attention():
+        mixed = project(normed_all, qkv)
+        return mixed, *attend(mixed, *tables)
+
+    mixed, attended, turned = window(needed, attention)
+    attended, out_proj, wide_send, cotangent_send, w_down = fence(
+        attended, out_proj, wide_chips[1], cotangent, w_down
+    )
+    cotangent_next = swap_rows(cotangent_send, 2)
+    wide_more = swap_rows(wide_send, 2)
+    down_rows = [
+        lax.dynamic_slice_in_dim(w_down, own_seq * 2 * chunk + (step ^ k) * chunk, chunk)
+        for k in range(2)
+    ]
+
+    def attention_out():
+        other = project(token_part(attended, 1), out_proj)
+        own = project(token_part(attended, 0), out_proj)
+        swapped, own = fence(swap_cores(other), own)
+        own = add(own, swapped)
+        flight = fence(*send_quarters(own))
+        own = add_quarters(own, *flight)
+        flight = fence(*send_eighths(*own))
+        middle = inputs + add_eighths(*own, *flight)
+        return middle, norm_two_of(middle)[0]
+
+    middle, normed_two = window(needed, attention_out)
+    wide_more, cotangent_next, normed_two = fence(wide_more, cotangent_next, normed_two)
+    gate_up_w = gather_rows(in_order(wide_chips[0], wide_more, step), ROW_PAIRS)
+
+    def gather_middle():
+        *flight, first, second = fence(*gather_one(normed_two), *row_one(cotangent_next))
+        cotangent_held, cotangent_flight = row_two(cotangent_next, first, second)
+        held, flight = gather_two(normed_two, *flight)
+        *flight, down_more = fence(*flight, swap_rows(down_rows[1], 2))
+        held, flight = gather_three(held, flight)
+        *flight, first, second = fence(*flight, *cotangent_flight)
+        held, last = gather_four(held, flight)
+        next_own, next_other = row_three(cotangent_held, (first, second))
+        last, next_other = fence(last, next_other)
+        return (
+            jnp.concatenate([*held, last]),
+            in_order(down_rows[0], down_more, step),
+            next_own,
+            next_other,
+        )
+
+    normed_two_all, down_pair, *cotangent_parts = window(needed, gather_middle)
+    down = gather_rows(down_pair, ROW_PAIRS)
+
+    _, factor_two = norm_two_of(middle)
+    cotangent_all = jnp.concatenate([cotangent_own, cotangent_other, *cotangent_parts])
+    gate_up = jnp.dot(normed_two_all, gate_up_w, preferred_element_type=jnp.float32)
+    units = gate_up.shape[1] // 2
+    gate, upward = gate_up[:, :units], gate_up[:, units:]
+    sigmoid = jax.nn.sigmoid(gate)
+    activated = gate * sigmoid
+    hidden = (activated * upward).astype(jnp.bfloat16)
+    hidden, cotangent_all = fence(hidden, cotangent_all)
+    forward_far, forward_other = project(token_part(hidden, 2), down), project(
+        token_part(hidden, 3), down
+    )
+    forward_far, forward_other = fence(forward_far, forward_other)
+    grad_hidden = back_product(cotangent_all, down)
+    grad_gate = grad_hidden * upward * sigmoid * (1.0 + gate * (1.0 - sigmoid))
+    grad_upward = grad_hidden * activated
+    grad_low = jnp.concatenate([grad_gate, grad_upward], axis=1).astype(jnp.bfloat16)
+    grad_low, swapped = fence(grad_low, swap_cores(forward_other))
+    forward_far = add(forward_far, swapped)
+    forward_near, forward_other = project(token_part(hidden, 0), down), project(
+        token_part(hidden, 1), down
+    )
+
+    def backward_part(grad, weight, k):
+        return back_product(token_part(grad, k), weight).astype(jnp.bfloat16)
+
+    far, far_other, forward_near, forward_other, *flight = fence(
+        backward_part(grad_low, gate_up_w, 2),
+        backward_part(grad_low, gate_up_w, 3),
+        forward_near,
+        forward_other,
+        *send_quarters(forward_far),
+    )
+    forward_far = add_quarters(forward_far, *flight)
+    grad_down_term = outer_sum(hidden, cotangent_all).astype(jnp.bfloat16)
+    swapped, far, near, near_other, grad_down_term, forward_swapped, *flight = fence(
+        swap_cores(far_other),
+        far,
+        backward_part(grad_low, gate_up_w, 0),
+        backward_part(grad_low, gate_up_w, 1),
+        grad_down_term,
+        swap_cores(forward_other),
+        *send_eighths(*forward_far),
+    )
+    far = add(far, swapped)
+    forward_near = add(forward_near, forward_swapped)
+    forward_far = add_eighths(*forward_far, *flight).astype(jnp.bfloat16)
+    grad_down_pair = scatter_rows(grad_down_term, ROW_PAIRS)
+    grad_gate_up_term = outer_sum(normed_two_all, grad_low).astype(jnp.bfloat16)
+    *flight, swapped, grad_gate_up_term = fence(
+        *send_quarters(far), swap_cores(near_other), grad_gate_up_term
+    )
+    far = add_quarters(far, *flight)
+    near = add(near, swapped)
+    grad_gate_up_pair = scatter_rows(grad_gate_up_term, ROW_PAIRS)
+
+    def feed_forward_back():
+        *flight, first, second = fence(*send_eighths(*far), *send_quarters(near))
+        next_row = add_eighths(*far, *flight).astype(jnp.bfloat16)
+        quarters = add_quarters(near, first, second)
+        next_row, first, second, *flight = fence(
+            swap_rows(next_row, 2), *send_eighths(*quarters), *send_quarters(forward_near)
+        )
+        scaled = mix_blocks(add_eighths(*quarters, first, second) + next_row.astype(jnp.float32))
+        forward_quarters = add_quarters(forward_near, *flight)
+        grad_middle = (
+            cotangent.astype(jnp.float32)
+            + factor_two * scaled
+            - middle * factor_two**3 * jnp.mean(scaled * middle, axis=-1, keepdims=True)
+        )
+        block = grad_middle.astype(jnp.bfloat16)
+        down_own, down_send = own_rows(grad_down_pair, chunk)
+        *flight, first, second, forward_next = fence(
+            *row_one(block), *send_eighths(*forward_quarters), swap_rows(forward_far, 2)
+        )
+        output = middle + forward_next.astype(jnp.float32)
+        output = output + add_eighths(*forward_quarters, first, second)
+        held, flight = row_two(block, *flight)
+        *flight, down_more = fence(*flight, swap_rows(down_send, 2))
+        own, other = row_three(held, flight)
+        down_halves = halves(in_order(down_own, down_more, step))
+        return jnp.concatenate([own, *fence(other)]), grad_middle, output, down_halves
+
+    grad_branch, grad_middle, output, down_halves = window(needed, feed_forward_back)
+
+    wide_own, wide_send = own_rows(grad_gate_up_pair, chip_rows)
+    grad_branch, wide_send = fence(grad_branch, wide_send)
+    wide_more = swap_rows(wide_send, 2)
+
+    def attention_back():
+        grad_heads = back_product(grad_branch, out_proj).astype(jnp.bfloat16)
+        grad_mixed = attend_back(turned, mixed, grad_heads, *tables)
+        grad_mixed, *flight = fence(grad_mixed, *share_one(*down_halves))
+        held, flight = share_two(*down_halves, *flight)
+        grad_qkv_term = outer_sum(normed_all, grad_mixed).astype(jnp.bfloat16)
+        return grad_mixed, grad_qkv_term, shared(held, fence(*flight))
+
+    grad_mixed, grad_qkv_term, down_pieces = window(needed, attention_back)
+    grad_qkv_term, wide_more = fence(grad_qkv_term, wide_more)
+    grad_qkv_rows = scatter_rows(grad_qkv_term, ROWS)
+    grad_out_rows = scatter_rows(outer_sum(attended, grad_branch), ROWS)
+
+    def inputs_back():
+        back = backward(grad_mixed, qkv)
+        mine, swapped = halves_of_chip(wide_own, wide_more)
+        swapped, row_swapped, near = fence(swapped, swap_cores(back[1]), back[0])
+        near = add(near, row_swapped)
+        wide_halves = mine, swapped
+        *row_flight, first, second = fence(*send_quarters(near), *share_one(*wide_halves))
+        near = add_quarters(near, *row_flight)
+        scaled = add_eighths(*near, *fence(*send_eighths(*near)))
+        grad_inputs = (
+            grad_middle
+            + factor_one * scaled
+            - inputs * factor_one**3 * jnp.mean(scaled * inputs, axis=-1, keepdims=True)
+        )
+        return grad_inputs, wide_halves, (first, second)
+
+    grad_inputs, wide_halves, wide_flight = window(needed, inputs_back)
+
+    wide_held, wide_flight = share_two(*wide_halves, *wide_flight)
+    grad_qkv_rows, grad_inputs = fence(grad_qkv_rows, grad_inputs)
+    qkv_halves = fence(*halves_of_chip(grad_qkv_rows))
+    out_halves = halves(grad_out_rows)
+    *qkv_flight, first, second = fence(*share_one(*qkv_halves), *share_one(*out_halves))
+    qkv_held, qkv_flight = share_two(*qkv_halves, *qkv_flight)
+    out_held, out_flight = share_two(*out_halves, first, second)
+    grad_gate_up, gain_two_sums = merge_wide(
+        shared(wide_held, wide_flight), w_gate_up, gain_two, place, 8, chunk
+    )
+    grad_qkv, gain_one_sums = merge_heads(
+        shared(qkv_held, qkv_flight), w_qkv, gain_one, place, heads
+    )
+    return (
+        output.astype(jnp.bfloat16)[None],
+        grad_inputs[None],
+        jnp.sum(gain_one_sums, axis=(0, 2)),
+        grad_qkv,
+        place_rows(shared(out_held, out_flight), own_seq),
+        jnp.sum(gain_two_sums, axis=(0, 2)),
+        grad_gate_up,
+        place_rows(down_pieces, own_seq),
+    )
+
+
 def solution(mesh):
+    seq, fsdp = mesh.shape["seq"], mesh.shape["fsdp"]
+
+    def on_device(hidden_in, norm_one, w_qkv, w_out, norm_two, w_gate_up, w_down, grad_out):
+        arrays = (hidden_in, norm_one, w_qkv, w_out, norm_two, w_gate_up, w_down, grad_out)
+        if seq == 4 and fsdp == 8 and w_out.shape[0] == 4 * HEAD_DIM and w_down.shape[0] % 1024 == 0:
+            return sliced_plan(*arrays)
+        return gathered_plan(*arrays)
+
     placed = (
         P("fsdp", "seq", None),
         P("fsdp"),

time: 2880 us -> 794 us (0.28)
  waiting for transfers between devices: 2480 us -> 331 us
  matrix products: 216 us -> 108 us
  starting transfers between devices: 11.6 us -> 86.1 us
  blocking collectives: 73.8 us -> 0 us
  local copies, waits for them, and re-layouts: 28.5 us -> 102 us
  Pallas kernels: 0 us -> 58 us
  other arithmetic: 42.8 us -> 87.9 us
    reduce_scatter x4, waiting for transfers between devices: 1170 us -> 2.14 us  [scatter_rows(): lax.psum_scatter(term.astype(jnp.bfloat16), 'fsdp', scatter_dimension=0,...]
    all_gather x4, waiting for transfers between devices: 1030 us -> 15.4 us  [gather_rows(): lax.all_gather(block, 'fsdp', axis=0, tiled=True, axis_index_groups=groups)]
    ppermute x0 -> x88, waiting for transfers between devices: none -> 313 us  [the longest x64 213 us: swap_seq(): return lax.ppermute(values, 'seq', xor_pairs(4, offset))]
    psum x1 -> x0, waiting for transfers between devices: 250 us -> none  [reduce_grads(): lax.psum(partial_sums[0].astype(jnp.bfloat16), 'seq').astype(jnp.float32)]
    ppermute x0 -> x88, starting transfers between devices: none -> 85.2 us  [the longest x64 69.3 us: swap_seq(): return lax.ppermute(values, 'seq', xor_pairs(4, offset))]
    pallas_call x0 -> x6, Pallas kernels: none -> 58 us  [the longest x1 15.9 us: merge_wide(): pl.pallas_call(body, grid_spec=pltpu.PrefetchScalarGridSpec(num_scalar_pr...]
    dot_general x10 -> x8, matrix products: 82.2 us -> 36.3 us  [the longest x7 22.9 us: project(): jnp.dot(rows, weight, preferred_element_type=jnp.float32)]
    cond x0 -> x104, local copies, waits for them, and re-layouts: none -> 38.2 us
  transfers between devices with their start and end apart: 12 -> 96, of which waited for: 10 -> 53; matrix products, arithmetic and copies ran while one was open for 7% -> 34% of each run, Pallas kernels for 0% -> 6%
where the time goes in v2:
time: 794 us; the launch traced here: 789 us
  waiting for transfers between devices  331 us (42%)
  matrix products  108 us (14%)
  local copies, waits for them, and re-layouts  102 us (13%)
  other arithmetic  87.9 us (11%)
  starting transfers between devices  86.1 us (11%)
  Pallas kernels  58 us (7%)
  between operations  15.2 us (2%)
    ppermute x64, waiting for transfers between devices, swap_seq(): return lax.ppermute(values, 'seq', xor_pairs(4, offset))  213 us
    ppermute x8, waiting for transfers between devices, swap_rows(): return lax.ppermute(values, 'fsdp', xor_pairs(8, 2 * offset))  92.8 us
    ppermute x64, starting transfers between devices, swap_seq(): return lax.ppermute(values, 'seq', xor_pairs(4, offset))  69.3 us
    dot_general x8, matrix products, back_product(): lax.dot_general(grad, weight, (((1,), (1,)), ((), ())), preferred_element...  40.2 us
    cond x104, local copies, waits for them, and re-layouts  38.2 us
    dot_general x4, matrix products, outer_sum(): lax.dot_general(left, right, (((0,), (0,)), ((), ())), preferred_element_...  31 us
    dot_general x7, matrix products, project(): jnp.dot(rows, weight, preferred_element_type=jnp.float32)  22.9 us
    dynamic_update_slice x16, other arithmetic, place_rows(): lax.dynamic_update_slice(out, block, (((own_seq ^ k) * 2 + half) * rows, 0))  18.1 us
  transfers between devices with their start and end apart: 96, of which 53 were waited for; matrix products, arithmetic and copies ran while one was open for 34% of the time, Pallas kernels for 6%

profile of v2, /device:TPU:0, one launch (start us, length us, event | category | flops | bytes accessed | tf_op | source)
XLA Modules:
  0.0 789.0 jit_solution(8546375917411860386)
XLA Ops:
  22.4 64.5 %conditional.7 = (bf16[1024,2048]{1,0:T(8,128)(2,1)}, bf16[512,1024]{1,0:T(8,128)(2,1)S(1)}, bf16[512,1024]{1,0:T(8,128)(2,1)S(1)}, bf16[512,2048]{1,0:T(8,128)(2,1)}, bf16[512,2048]{1,0:T(8,128)(2,1)}) conditional(s32[]{:T(128)} %convert_element_type.338, () %tuple.109, (bf16[128,2048]{1,0:T(8,128)(2,1)S(1)}, s32[3]{0:T(128)S(1)}, ...), branch_computations={%region_1.2_spmd, %region_2.3_spmd} | conditional | flops 9437185 | bytes 88869488 | solution.py:256
  67.7 10.0 %collective-permute-done.8 = bf16[128,2048]{1,0:T(8,128)(2,1)S(1)} collective-permute-done((bf16[128,2048]{1,0:T(8,128)(2,1)S(1)}, bf16[128,2048]{1,0:T(8,128)(2,1)S(1)}, u32[]{:S(2)}, u32[]{:S(2)}) %collective-permute-start.8) | collective-permute-done | bytes 524320 | tf_op jit(solution)/shard_map/cond/branch_1_fun/ppermute | solution.py:247
  88.6 18.4 %conditional.8 = (bf16[1024,768]{1,0:T(8,128)(2,1)}, bf16[1024,256]{1,0:T(8,128)(2,1)}, bf16[1024,512]{1,0:T(8,128)(2,1)}) conditional(s32[]{:T(128)} %convert_element_type.338, () %tuple.108, (bf16[1024,2048]{1,0:T(8,128)(2,1)}, bf16[2048,768]{1,0:T(8,128)(2,1)}, f32[512,128]{0,1:T(8,128)}, f32[512,128]{0,1:T(8,128)}, s32[512,1]{0,1:T(1,128)S(1)}, ...), branch_computations={%region_3.4_spmd, %region_4.5_spmd} | conditional | flops 4295753728 | bytes 13111320 | solution.py:256
  98.6 8.3 %attend.1 = (bf16[1024,256]{1,0:T(8,128)(2,1)}, bf16[1024,512]{1,0:T(8,128)(2,1)}) custom-call(bf16[1024,768]{1,0:T(8,128)(2,1)} %convolution_convert_fusion.mixed_ref, f32[512,128]{1,0:T(8,128)S(1)} %copy.22.cosine_ref, f32[512,128]{1,0:T(8,128)S(1)} %copy.23.sine_ref, s32[512,1]{1,0:T(8,128)S(1)} %copy.24.rows_ref, s32[1,512]{1,0:T(1,128)S(1)} %get-tuple-element.191.columns_ref), custom_call_target="tpu_custom_call" | custom-call | flops 1073741824 | bytes 3145728 | tf_op jit(solution)/shard_map/cond/branch_1_fun/attend/pallas_call | solution.py:646
  106.9 8.2 %all-gather.7.cloned.1.call-done = bf16[256,2048]{1,0:T(8,128)(2,1)} async-done(((bf16[64,2048]{1,0:T(8,128)(2,1)}), bf16[256,2048]{1,0:T(8,128)(2,1)}) %all-gather.7.cloned.1.call-update) | async-done | bytes 1048592 | tf_op jit(solution)/shard_map/all_gather | solution.py:378
  119.2 36.5 %conditional.9 = (f32[128,2048]{1,0:T(8,128)}, bf16[128,2048]{1,0:T(8,128)(2,1)S(1)}, f32[128,1]{0,1:T(1,128)}) conditional(s32[]{:T(128)} %convert_element_type.338, () %tuple.107, (bf16[1024,256]{1,0:T(8,128)(2,1)}, bf16[256,2048]{1,0:T(8,128)(2,1)}, f32[128,2048]{1,0:T(8,128)}) %tuple.115), branch_computations={%region_5.6_spmd, %region_6.8_spmd} | conditional | flops 1085800576 | bytes 48761084 | solution.py:256
  129.5 11.0 %collective-permute-done.47 = bf16[128,2048]{1,0:T(8,128)(2,1)S(1)} collective-permute-done((bf16[128,2048]{1,0:T(8,128)(2,1)S(1)}, bf16[128,2048]{1,0:T(8,128)(2,1)S(1)}, u32[]{:S(2)}, u32[]{:S(2)}) %collective-permute-start.47) | collective-permute-done | bytes 524320 | tf_op jit(solution)/shard_map/cond/branch_1_fun/ppermute | solution.py:247
  155.7 30.3 %collective-permute-done.65 = bf16[128,2048]{1,0:T(8,128)(2,1)S(1)} collective-permute-done((bf16[128,2048]{1,0:T(8,128)(2,1)S(1)}, bf16[128,2048]{1,0:T(8,128)(2,1)S(1)}, u32[]{:S(2)}, u32[]{:S(2)}) %collective-permute-start.65) | collective-permute-done | bytes 524320 | tf_op jit(solution)/shard_map/ppermute | solution.py:243
  189.1 108.3 %conditional.10 = (bf16[2048,2048]{1,0:T(8,128)(2,1)}, bf16[256,2048]{1,0:T(8,128)(2,1)S(1)}, bf16[512,2048]{1,0:T(8,128)(2,1)S(1)}, bf16[512,2048]{1,0:T(8,128)(2,1)}) conditional(s32[]{:T(128)} %convert_element_type.338, () %tuple.116, (bf16[128,2048]{1,0:T(8,128)(2,1)S(1)}, bf16[128,2048]{1,0:T(8,128)(2,1)S(1)}, s32[]{:T(128)}, s32[]{:T(128)}, ...), branch_computations={%region_8.9_spmd, %region_9.10_spmd} | conditional | flops 8912908 | bytes 123470896 | solution.py:256
  204.6 19.4 %collective-permute-done.13 = bf16[128,2048]{1,0:T(8,128)(2,1)S(1)} collective-permute-done((bf16[128,2048]{1,0:T(8,128)(2,1)S(1)}, bf16[128,2048]{1,0:T(8,128)(2,1)S(1)}, u32[]{:S(2)}, u32[]{:S(2)}) %collective-permute-start.13) | collective-permute-done | bytes 524320 | tf_op jit(solution)/shard_map/cond/branch_1_fun/ppermute | solution.py:243
  236.0 11.0 %collective-permute-done.18 = bf16[64,2048]{1,0:T(8,128)(2,1)S(1)} collective-permute-done((bf16[64,2048]{1,0:T(8,128)(2,1)S(1)}, bf16[64,2048]{1,0:T(8,128)(2,1)S(1)}, u32[]{:S(2)}, u32[]{:S(2)}) %collective-permute-start.18) | collective-permute-done | bytes 262176 | tf_op jit(solution)/shard_map/cond/branch_1_fun/ppermute | solution.py:247
  259.9 8.6 %collective-permute-done.24 = bf16[128,2048]{1,0:T(8,128)(2,1)S(1)} collective-permute-done((bf16[128,2048]{1,0:T(8,128)(2,1)S(1)}, bf16[128,2048]{1,0:T(8,128)(2,1)S(1)}, u32[]{:S(2)}, u32[]{:S(2)}) %collective-permute-start.24) | collective-permute-done | bytes 524320 | tf_op jit(solution)/shard_map/cond/branch_1_fun/ppermute | solution.py:247
  270.0 9.4 %collective-permute-done.22 = bf16[128,2048]{1,0:T(8,128)(2,1)S(1)} collective-permute-done((bf16[128,2048]{1,0:T(8,128)(2,1)S(1)}, bf16[128,2048]{1,0:T(8,128)(2,1)S(1)}, u32[]{:S(2)}, u32[]{:S(2)}) %collective-permute-start.22) | collective-permute-done | bytes 524320 | tf_op jit(solution)/shard_map/cond/branch_1_fun/ppermute | solution.py:247
  305.1 13.5 %fusion.36 = f32[2048,1024]{0,1:T(8,128)S(1)} fusion(bf16[2048,2048]{1,0:T(8,128)(2,1)} %get-tuple-element.407, bf16[2048,1024]{1,0:T(8,128)(2,1)} %all-gather.9.cloned.1.call-done), kind=kOutput, calls=%fused_computation.273 | convolution fusion | flops 8589934592 | bytes 20971520 | tf_op jit(solution)/shard_map/dot_general | solution.py:901
  336.6 9.6 %multiply_convert_fusion.2 = (bf16[2048,512]{0,1:T(8,128)(2,1)S(1)}, bf16[2048,512]{0,1:T(8,128)(2,1)S(1)}) fusion(f32[2048,1024]{0,1:T(8,128)S(1)} %copy-done.3, bf16[2048,2048]{1,0:T(8,128)(2,1)} %pad_maximum_fusion.21, bf16[512,2048]{1,0:T(8,128)(2,1)S(1)} %copy-done.78), kind=kOutput, calls=%fused_computation.179 | convolution fusion | flops 4308598784 | bytes 23068672 | tf_op jit(solution)/shard_map/dot_general | solution.py:26
  399.7 12.6 %convolution_convert_fusion.7 = bf16[2048,1024]{1,0:T(8,128)(2,1)} fusion(bf16[2048,2048]{1,0:T(8,128)(2,1)} %get-tuple-element.407, bf16[2048,1024]{0,1:T(8,128)(2,1)S(1)} %copy-done.13), kind=kOutput, calls=%fused_computation.183 | convolution fusion | flops 8592031744 | bytes 16777216 | tf_op jit(solution)/shard_map/dot_general | solution.py:20
  424.4 109.4 %conditional.11 = (bf16[1024,2048]{1,0:T(8,128)(2,1)}, f32[128,2048]{1,0:T(8,128)S(1)}, bf16[128,2048]{1,0:T(8,128)(2,1)}, bf16[128,2048]{1,0:T(8,128)(2,1)}, bf16[1,128,2048]{2,1,0:T(8,128)(2,1)}) conditional(s32[]{:T(128)} %convert_element_type.338, () %tuple.106, (bf16[128,2048]{1,0:T(8,128)(2,1)}, f32[128,1]{0,1:T(1,128)}, ...), branch_computations={%region_11.12_spmd, %region_12.14_spmd} | conditional | flops 15729162 | bytes 147331296 | solution.py:256
  434.0 12.3 %collective-permute-done.28 = bf16[64,2048]{1,0:T(8,128)(2,1)S(1)} collective-permute-done((bf16[64,2048]{1,0:T(8,128)(2,1)S(1)}, bf16[64,2048]{1,0:T(8,128)(2,1)S(1)}, u32[]{:S(2)}, u32[]{:S(2)}) %collective-permute-start.28) | collective-permute-done | bytes 262176 | tf_op jit(solution)/shard_map/cond/branch_1_fun/ppermute | solution.py:247
  464.5 10.6 %collective-permute-done.32 = bf16[128,2048]{1,0:T(8,128)(2,1)S(1)} collective-permute-done((bf16[128,2048]{1,0:T(8,128)(2,1)S(1)}, bf16[128,2048]{1,0:T(8,128)(2,1)S(1)}, u32[]{:S(2)}, u32[]{:S(2)}) %collective-permute-start.32) | collective-permute-done | bytes 524320 | tf_op jit(solution)/shard_map/cond/branch_1_fun/ppermute | solution.py:243
  485.7 10.0 %collective-permute-done.41 = bf16[128,2048]{1,0:T(8,128)(2,1)} collective-permute-done((bf16[128,2048]{1,0:T(8,128)(2,1)}, bf16[128,2048]{1,0:T(8,128)(2,1)}, u32[]{:S(2)}, u32[]{:S(2)}) %collective-permute-start.41) | collective-permute-done | bytes 524320 | tf_op jit(solution)/shard_map/cond/branch_1_fun/ppermute | solution.py:243
  501.4 18.6 %collective-permute-done.44 = bf16[128,2048]{1,0:T(8,128)(2,1)S(1)} collective-permute-done((bf16[128,2048]{1,0:T(8,128)(2,1)S(1)}, bf16[128,2048]{1,0:T(8,128)(2,1)S(1)}, u32[]{:S(2)}, u32[]{:S(2)}) %collective-permute-start.44) | collective-permute-done | bytes 524320 | tf_op jit(solution)/shard_map/cond/branch_1_fun/ppermute | solution.py:243
  535.7 53.3 %conditional.12 = (bf16[1024,768]{1,0:T(8,128)(2,1)}, bf16[2048,768]{0,1:T(8,128)(2,1)}, bf16[256,2048]{1,0:T(8,128)(2,1)}, bf16[256,2048]{1,0:T(8,128)(2,1)}, b...) conditional(s32[]{:T(128)} %convert_element_type.338, () %tuple.126, (bf16[1024,2048]{1,0:T(8,128)(2,1)}, ...), branch_computations={%region_15.16_spmd, %region_16.17_spmd} | conditional | flops 6981156864 | bytes 36704464 | solution.py:256
  546.4 12.6 %attend_back.1 = bf16[1024,768]{1,0:T(8,128)(2,1)} custom-call(bf16[1024,512]{1,0:T(8,128)(2,1)} %get-tuple-element.255.turned_ref, bf16[1024,768]{1,0:T(8,128)(2,1)} %get-tuple-element.256.values_ref, bf16[1024,256]{1,0:T(8,128)(2,1)S(1)} %convolution_convert_fusion.4.grad_ref, f32[512,128]{1,0:T(8,128)S(1)} %copy.25.cosine_ref, ...), custom_call_target="tpu_custom_call" | custom-call | flops 2684354560 | bytes 4194304 | tf_op jit(solution)/shard_map/cond/branch_1_fun/attend_back/pallas_call | solution.py:714
  565.8 7.8 fusion.8
  573.6 12.2 %collective-permute-done.53 = bf16[256,2048]{1,0:T(8,128)(2,1)} collective-permute-done((bf16[256,2048]{1,0:T(8,128)(2,1)}, bf16[256,2048]{1,0:T(8,128)(2,1)}, u32[]{:S(2)}, u32[]{:S(2)}) %collective-permute-start.53) | collective-permute-done | bytes 1048608 | tf_op jit(solution)/shard_map/cond/branch_1_fun/ppermute | solution.py:247
  609.7 63.7 %conditional.13 = (f32[128,2048]{1,0:T(8,128)}, bf16[2,256,1024]{2,1,0:T(8,128)(2,1)S(1)}, bf16[2,256,1024]{2,1,0:T(8,128)(2,1)}, bf16[2,256,1024]{2,1,0:T(8,128)(2,1)}, bf16[2,256,1024]{2,1,0:T(8,128)(2,1)}) conditional(s32[]{:T(128)} %convert_element_type.338, () %tuple.130, (f32[128]{0:T(128)S(1)}, f32[128,1]{0,1:T(1,128)S(1)}, s32[]{:T(128)}, ...), branch_computations={%region_18.19_spmd, %region_19.21_spmd} | conditional | flops 3233022464 | bytes 91231912 | solution.py:256
  628.2 15.9 %collective-permute-done.59 = bf16[2,256,1024]{2,1,0:T(8,128)(2,1)} collective-permute-done((bf16[2,256,1024]{2,1,0:T(8,128)(2,1)S(1)}, bf16[2,256,1024]{2,1,0:T(8,128)(2,1)}, u32[]{:S(2)}, u32[]{:S(2)}) %collective-permute-start.59) | collective-permute-done | bytes 1048608 | tf_op jit(solution)/shard_map/cond/branch_1_fun/ppermute | solution.py:247
  644.0 15.4 %collective-permute-done.57 = bf16[128,2048]{1,0:T(8,128)(2,1)S(1)} collective-permute-done((bf16[128,2048]{1,0:T(8,128)(2,1)S(1)}, bf16[128,2048]{1,0:T(8,128)(2,1)S(1)}, u32[]{:S(2)}, u32[]{:S(2)}) %collective-permute-start.57) | collective-permute-done | bytes 524320 | tf_op jit(solution)/shard_map/cond/branch_1_fun/ppermute | solution.py:247
  695.7 30.2 %collective-permute-done.87.refs_3_ = bf16[4,256,1024]{2,1,0:T(8,128)(2,1)} collective-permute-done((bf16[4,256,1024]{2,1,0:T(8,128)(2,1)S(1)}, bf16[4,256,1024]{2,1,0:T(8,128)(2,1)}, u32[]{:S(2)}, u32[]{:S(2)}) %collective-permute-start.87) | collective-permute-done | bytes 2097184 | tf_op jit(solution)/shard_map/ppermute | solution.py:247
  729.7 15.9 %merge_wide.1 = (f32[256,16384]{1,0:T(8,128)}, f32[4,256,128]{2,1,0:T(8,128)S(1)}) custom-call(s32[3]{0:T(128)S(1)} %copy-done.67, bf16[4,256,1024]{2,1,0:T(8,128)(2,1)} %constant_dynamic-update-slice_fusion.72.refs_0_, bf16[4,256,1024]{2,1,0:T(8,128)(2,1)} %collective-permute-done.86.refs_1_, ...), custom_call_target="tpu_custom_call" | custom-call | tf_op jit(solution)/shard_map/merge_wide/pallas_call | solution.py:504
  761.7 7.8 collective-permute-done.83.refs_3_
  771.3 9.0 %merge_heads.1 = (f32[256,6144]{1,0:T(8,128)}, f32[2,256,128]{2,1,0:T(8,128)}) custom-call(s32[3]{0:T(128)S(1)} %copy-done.67, bf16[2,256,768]{2,1,0:T(8,128)(2,1)} %copy-done.39, bf16[2,256,768]{2,1,0:T(8,128)(2,1)} %collective-permute-done.82.refs_1_, bf16[2,256,768]{2,1,0:T(8,128)(2,1)} %copy-done.40, bf16[2,256,768]{2,1,0:T(8,128)(2,1)} %copy-done.50, ...), custom_call_target="tpu_custom_call" | custom-call | tf_op jit(solution)/shard_map/merge_heads/pallas_call | solution.py:571
  (575 shorter events, 442.9 us)
Async XLA Ops:
  7.2 79.8 %all-gather.5.cloned.1.call-start = ((), (), s32[]{:S(2)}) async-start(), calls=%async_computation.4 | async-start | bytes 3932160 | tf_op jit(solution)/shard_map/all_gather | solution.py:378
  20.7 94.5 %all-gather.7.cloned.1.call-start = ((), (), s32[]{:S(2)}) async-start(), calls=%async_computation.5 | async-start | bytes 1310720 | tf_op jit(solution)/shard_map/all_gather | solution.py:378
  21.5 283.6 %all-gather.9.cloned.1.call-start = ((), (), s32[]{:S(2)}) async-start(), calls=%async_computation.6 | async-start | bytes 6291456 | tf_op jit(solution)/shard_map/all_gather | solution.py:378
  115.1 70.8 %collective-permute-start.64 = (bf16[512,1024]{1,0:T(8,128)(2,1)}, bf16[512,1024]{1,0:T(8,128)(2,1)}, u32[]{:S(2)}, u32[]{:S(2)}) collective-permute-start(bf16[512,1024]{1,0:T(8,128)(2,1)} %copy-done.46), channel_id=1, source_target_pairs={{0,4},{1,5},{2,6},{3,7},{4,0},{5,1},{6,2},{7,3},{8,12},{9,13},{10,... | collective-permute-start | bytes 3145736 | tf_op jit(solution)/shard_map/ppermute | solution.py:243
  117.1 68.9 %collective-permute-start.65 = (bf16[128,2048]{1,0:T(8,128)(2,1)S(1)}, bf16[128,2048]{1,0:T(8,128)(2,1)S(1)}, u32[]{:S(2)}, u32[]{:S(2)}) collective-permute-start(bf16[128,2048]{1,0:T(8,128)(2,1)S(1)} %bitcast.85), channel_id=1, source_target_pairs={{0,4},{1,5},{2,6},{3,7},{4,0},{5,1},{6,2},{7,3},{8,12},{9,13},{10,... | collective-permute-start | bytes 1572872 | tf_op jit(solution)/shard_map/ppermute | solution.py:243
  188.8 141.6 %all-gather.11.cloned.1.call-start = ((), (), s32[]{:S(2)}) async-start(), calls=%async_computation.7 | async-start | bytes 3145728 | tf_op jit(solution)/shard_map/all_gather | solution.py:378
  189.1 34.9 %collective-permute-start.13 = (bf16[128,2048]{1,0:T(8,128)(2,1)S(1)}, bf16[128,2048]{1,0:T(8,128)(2,1)S(1)}, u32[]{:S(2)}, u32[]{:S(2)}) collective-permute-start(bf16[128,2048]{1,0:T(8,128)(2,1)S(1)} %get-tuple-element.203), channel_id=1, source_target_pairs={{0,4},{1,5},{2,6},{3,7},{4,0},{5,1},{6,2},{7,3},{8,12},{9,13},{10,... | collective-permute-start | bytes 1572872 | tf_op jit(solution)/shard_map/cond/branch_1_fun/ppermute | solution.py:243
  199.0 37.0 %collective-permute-start.20 = (bf16[128,2048]{1,0:T(8,128)(2,1)S(1)}, bf16[128,2048]{1,0:T(8,128)(2,1)S(1)}, u32[]{:S(2)}, u32[]{:S(2)}) collective-permute-start(bf16[128,2048]{1,0:T(8,128)(2,1)S(1)} %constant_dynamic-slice_fusion), channel_id=1, source_target_pairs={{0,4},{1,5},{2,6},{3,7},{4,0},{5,1},{6,2},{7,3},{8,12},{9,13},{10,... | collective-permute-start | bytes 1572872 | tf_op jit(solution)/shard_map/cond/branch_1_fun/ppermute | solution.py:243
  252.7 27.9 %collective-permute-start.21 = (bf16[512,2048]{1,0:T(8,128)(2,1)S(1)}, bf16[512,2048]{1,0:T(8,128)(2,1)S(1)}, u32[]{:S(2)}, u32[]{:S(2)}) collective-permute-start(bf16[512,2048]{1,0:T(8,128)(2,1)S(1)} %get-tuple-element.531), channel_id=1, source_target_pairs={{0,1},{1,0},{2,3},{3,2},{4,5},{5,4},{6,7},{7,6},{8,9},{9,8},{10,11... | collective-permute-start | bytes 6291464 | tf_op jit(solution)/shard_map/cond/branch_1_fun/ppermute | solution.py:239
  298.3 126.0 %reduce-scatter.5.cloned.1.call-start = ((), (), s32[]{:S(2)}) async-start(), calls=%async_computation.8 | async-start | bytes 3145728 | tf_op jit(solution)/shard_map/reduce_scatter | solution.py:382
  368.4 25.2 %collective-permute-start.69 = (bf16[512,2048]{1,0:T(8,128)(2,1)}, bf16[512,2048]{1,0:T(8,128)(2,1)}, u32[]{:S(2)}, u32[]{:S(2)}) collective-permute-start(bf16[512,2048]{1,0:T(8,128)(2,1)} %convolution_convert_fusion.10), channel_id=1, source_target_pairs={{0,1},{1,0},{2,3},{3,2},{4,5},{5,4},{6,7},{7,6},{8,9},{9,8},{10,11... | collective-permute-start | bytes 6291464 | tf_op jit(solution)/shard_map/ppermute | solution.py:239
  369.2 24.5 %collective-permute-start.70 = (bf16[512,2048]{1,0:T(8,128)(2,1)}, bf16[512,2048]{1,0:T(8,128)(2,1)}, u32[]{:S(2)}, u32[]{:S(2)}) collective-permute-start(bf16[512,2048]{1,0:T(8,128)(2,1)} %convolution_convert_fusion.13), channel_id=1, source_target_pairs={{0,1},{1,0},{2,3},{3,2},{4,5},{5,4},{6,7},{7,6},{8,9},{9,8},{10,11... | collective-permute-start | bytes 6291464 | tf_op jit(solution)/shard_map/ppermute | solution.py:239
  393.7 140.1 %reduce-scatter.7.cloned.1.call-start = ((), (), s32[]{:S(2)}) async-start(), calls=%async_computation.9 | async-start | bytes 6291456 | tf_op jit(solution)/shard_map/reduce_scatter | solution.py:382
  413.1 274.4 %reduce-scatter.9.cloned.1.call-start = ((), (), s32[]{:S(2)}) async-start(), calls=%async_computation.10 | async-start | bytes 3932160 | tf_op jit(solution)/shard_map/reduce_scatter | solution.py:382
  432.5 25.0 %collective-permute-start.35 = (bf16[128,2048]{1,0:T(8,128)(2,1)S(1)}, bf16[128,2048]{1,0:T(8,128)(2,1)S(1)}, u32[]{:S(2)}, u32[]{:S(2)}) collective-permute-start(bf16[128,2048]{1,0:T(8,128)(2,1)S(1)} %get-tuple-element.569), channel_id=1, source_target_pairs={{0,16},{8,24},{16,0},{24,8},{1,17},{9,25},{17,1},{25,9},{2,18},{10... | collective-permute-start | bytes 1572872 | tf_op jit(solution)/shard_map/cond/branch_1_fun/ppermute | solution.py:247
  447.9 27.1 %collective-permute-start.32 = (bf16[128,2048]{1,0:T(8,128)(2,1)S(1)}, bf16[128,2048]{1,0:T(8,128)(2,1)S(1)}, u32[]{:S(2)}, u32[]{:S(2)}) collective-permute-start(bf16[128,2048]{1,0:T(8,128)(2,1)S(1)} %pad_maximum_fusion.15), channel_id=1, source_target_pairs={{0,4},{1,5},{2,6},{3,7},{4,0},{5,1},{6,2},{7,3},{8,12},{9,13},{10,... | collective-permute-start | bytes 1572872 | tf_op jit(solution)/shard_map/cond/branch_1_fun/ppermute | solution.py:243
  457.5 38.2 %collective-permute-start.41 = (bf16[128,2048]{1,0:T(8,128)(2,1)}, bf16[128,2048]{1,0:T(8,128)(2,1)}, u32[]{:S(2)}, u32[]{:S(2)}) collective-permute-start(bf16[128,2048]{1,0:T(8,128)(2,1)} %get-tuple-element.244), channel_id=1, source_target_pairs={{0,4},{1,5},{2,6},{3,7},{4,0},{5,1},{6,2},{7,3},{8,12},{9,13},{10,... | collective-permute-start | bytes 1572872 | tf_op jit(solution)/shard_map/cond/branch_1_fun/ppermute | solution.py:243
  475.4 23.6 %collective-permute-start.39 = (bf16[64,2048]{1,0:T(8,128)(2,1)S(1)}, bf16[64,2048]{1,0:T(8,128)(2,1)S(1)}, u32[]{:S(2)}, u32[]{:S(2)}) collective-permute-start(bf16[64,2048]{1,0:T(8,128)(2,1)S(1)} %slice.505), channel_id=1, source_target_pairs={{0,8},{8,0},{16,24},{24,16},{1,9},{9,1},{17,25},{25,17},{2,10},{10... | collective-permute-start | bytes 786440 | tf_op jit(solution)/shard_map/cond/branch_1_fun/ppermute | solution.py:247
  495.7 24.3 %collective-permute-start.44 = (bf16[128,2048]{1,0:T(8,128)(2,1)S(1)}, bf16[128,2048]{1,0:T(8,128)(2,1)S(1)}, u32[]{:S(2)}, u32[]{:S(2)}) collective-permute-start(bf16[128,2048]{1,0:T(8,128)(2,1)S(1)} %constant_dynamic-slice_fusion.1), channel_id=1, source_target_pairs={{0,4},{1,5},{2,6},{3,7},{4,0},{5,1},{6,2},{7,3},{8,12},{9,13},{10,... | collective-permute-start | bytes 1572872 | tf_op jit(solution)/shard_map/cond/branch_1_fun/ppermute | solution.py:243
  535.5 53.5 %collective-permute-start.76 = (bf16[512,1024]{1,0:T(8,128)(2,1)S(1)}, bf16[512,1024]{1,0:T(8,128)(2,1)}, u32[]{:S(2)}, u32[]{:S(2)}) collective-permute-start(bf16[512,1024]{1,0:T(8,128)(2,1)S(1)} %constant_dynamic-slice_fusion.4), channel_id=1, source_target_pairs={{0,4},{1,5},{2,6},{3,7},{4,0},{5,1},{6,2},{7,3},{8,12},{9,13},{10,... | collective-permute-start | bytes 3145736 | tf_op jit(solution)/shard_map/ppermute | solution.py:243
  560.9 25.0 %collective-permute-start.53 = (bf16[256,2048]{1,0:T(8,128)(2,1)}, bf16[256,2048]{1,0:T(8,128)(2,1)}, u32[]{:S(2)}, u32[]{:S(2)}) collective-permute-start(bf16[256,2048]{1,0:T(8,128)(2,1)} %constant_dynamic-update-slice_fusion.64), channel_id=1, source_target_pairs={{0,16},{8,24},{16,0},{24,8},{1,17},{9,25},{17,1},{25,9},{2,18},{10... | collective-permute-start | bytes 3145736 | tf_op jit(solution)/shard_map/cond/branch_1_fun/ppermute | solution.py:247
  564.4 24.7 %collective-permute-start.54 = (bf16[256,2048]{1,0:T(8,128)(2,1)}, bf16[256,2048]{1,0:T(8,128)(2,1)}, u32[]{:S(2)}, u32[]{:S(2)}) collective-permute-start(bf16[256,2048]{1,0:T(8,128)(2,1)} %constant_dynamic-update-slice_fusion.66), channel_id=1, source_target_pairs={{0,8},{8,0},{16,24},{24,16},{1,9},{9,1},{17,25},{25,17},{2,10},{10... | collective-permute-start | bytes 3145736 | tf_op jit(solution)/shard_map/cond/branch_1_fun/ppermute | solution.py:247
  589.1 100.5 %reduce-scatter.11.cloned.1.call-start = ((), (), s32[]{:S(2)}) async-start(), calls=%async_computation.11 | async-start | bytes 1310720 | tf_op jit(solution)/shard_map/reduce_scatter | solution.py:382
  617.8 26.2 %collective-permute-start.59 = (bf16[2,256,1024]{2,1,0:T(8,128)(2,1)S(1)}, bf16[2,256,1024]{2,1,0:T(8,128)(2,1)}, u32[]{:S(2)}, u32[]{:S(2)}) collective-permute-start(bf16[2,256,1024]{2,1,0:T(8,128)(2,1)S(1)} %pad_maximum_fusion.19), channel_id=1, source_target_pairs={{0,8},{8,0},{16,24},{24,16},{1,9},{9,1},{17,25},{25,17},{2,10},{10... | collective-permute-start | bytes 3145736 | tf_op jit(solution)/shard_map/cond/branch_1_fun/ppermute | solution.py:247
  622.4 37.0 %collective-permute-start.60 = (bf16[2,256,1024]{2,1,0:T(8,128)(2,1)}, bf16[2,256,1024]{2,1,0:T(8,128)(2,1)}, u32[]{:S(2)}, u32[]{:S(2)}) collective-permute-start(bf16[2,256,1024]{2,1,0:T(8,128)(2,1)} %collective-permute-done.55), channel_id=1, source_target_pairs={{0,16},{8,24},{16,0},{24,8},{1,17},{9,25},{17,1},{25,9},{2,18},{10... | collective-permute-start | bytes 3145736 | tf_op jit(solution)/shard_map/cond/branch_1_fun/ppermute | solution.py:247
  625.3 34.1 %collective-permute-start.57 = (bf16[128,2048]{1,0:T(8,128)(2,1)S(1)}, bf16[128,2048]{1,0:T(8,128)(2,1)S(1)}, u32[]{:S(2)}, u32[]{:S(2)}) collective-permute-start(bf16[128,2048]{1,0:T(8,128)(2,1)S(1)} %get-tuple-element.549), channel_id=1, source_target_pairs={{0,16},{8,24},{16,0},{24,8},{1,17},{9,25},{17,1},{25,9},{2,18},{10... | collective-permute-start | bytes 1572872 | tf_op jit(solution)/shard_map/cond/branch_1_fun/ppermute | solution.py:247
  627.0 32.4 %collective-permute-start.58 = (bf16[128,2048]{1,0:T(8,128)(2,1)S(1)}, bf16[128,2048]{1,0:T(8,128)(2,1)S(1)}, u32[]{:S(2)}, u32[]{:S(2)}) collective-permute-start(bf16[128,2048]{1,0:T(8,128)(2,1)S(1)} %get-tuple-element.548), channel_id=1, source_target_pairs={{0,8},{8,0},{16,24},{24,16},{1,9},{9,1},{17,25},{25,17},{2,10},{10... | collective-permute-start | bytes 1572872 | tf_op jit(solution)/shard_map/cond/branch_1_fun/ppermute | solution.py:247
  677.1 48.7 %collective-permute-start.87 = (bf16[4,256,1024]{2,1,0:T(8,128)(2,1)S(1)}, bf16[4,256,1024]{2,1,0:T(8,128)(2,1)}, u32[]{:S(2)}, u32[]{:S(2)}) collective-permute-start(bf16[4,256,1024]{2,1,0:T(8,128)(2,1)S(1)} %constant_dynamic-update-slice_fusion.74.refs_2_), channel_id=1, source_target_pairs={{0,8},{8,0},{16,24},{24,16},{1,9},{9,1},{17,25},{25,17},{2,10},{10... | collective-permute-start | bytes 6291464 | tf_op jit(solution)/shard_map/ppermute | solution.py:247
  680.9 48.9 %collective-permute-start.86 = (bf16[4,256,1024]{2,1,0:T(8,128)(2,1)}, bf16[4,256,1024]{2,1,0:T(8,128)(2,1)}, u32[]{:S(2)}, u32[]{:S(2)}) collective-permute-start(bf16[4,256,1024]{2,1,0:T(8,128)(2,1)} %constant_dynamic-update-slice_fusion.72.refs_0_), channel_id=1, source_target_pairs={{0,16},{8,24},{16,0},{24,8},{1,17},{9,25},{17,1},{25,9},{2,18},{10... | collective-permute-start | bytes 6291464 | tf_op jit(solution)/shard_map/ppermute | solution.py:247
  691.3 56.2 %collective-permute-start.80 = (bf16[32,2048]{1,0:T(8,128)(2,1)}, bf16[32,2048]{1,0:T(8,128)(2,1)S(1)}, u32[]{:S(2)}, u32[]{:S(2)}) collective-permute-start(bf16[32,2048]{1,0:T(8,128)(2,1)} %get-tuple-element.610), channel_id=1, source_target_pairs={{0,8},{8,0},{16,24},{24,16},{1,9},{9,1},{17,25},{25,17},{2,10},{10... | collective-permute-start | bytes 393224 | tf_op jit(solution)/shard_map/ppermute | solution.py:247
  693.2 54.3 %collective-permute-start.78 = (bf16[1,256,768]{2,1,0:T(8,128)(2,1)S(1)}, bf16[1,256,768]{2,1,0:T(8,128)(2,1)}, u32[]{:S(2)}, u32[]{:S(2)}) collective-permute-start(bf16[1,256,768]{2,1,0:T(8,128)(2,1)S(1)} %bitcast.86), channel_id=1, source_target_pairs={{0,8},{8,0},{16,24},{24,16},{1,9},{9,1},{17,25},{25,17},{2,10},{10... | collective-permute-start | bytes 1179656 | tf_op jit(solution)/shard_map/ppermute | solution.py:247
  693.6 54.0 %collective-permute-start.79 = (bf16[1,256,768]{2,1,0:T(8,128)(2,1)}, bf16[1,256,768]{2,1,0:T(8,128)(2,1)}, u32[]{:S(2)}, u32[]{:S(2)}) collective-permute-start(bf16[1,256,768]{2,1,0:T(8,128)(2,1)} %collective-permute-done.77), channel_id=1, source_target_pairs={{0,16},{8,24},{16,0},{24,8},{1,17},{9,25},{17,1},{25,9},{2,18},{10... | collective-permute-start | bytes 1179656 | tf_op jit(solution)/shard_map/ppermute | solution.py:247
  (147 other events, 1561.1 us)
Sparse Core Ops, SparseCore 0:
  20.8 66.1 all-gather.4
  88.5 26.5 all-gather.6
  189.0 78.9 all-gather.8
  298.5 31.9 all-gather.10
  393.8 30.5 reduce-scatter.4
  427.2 83.0 reduce-scatter.6
  589.2 59.4 reduce-scatter.8
  651.0 27.1 reduce-scatter.10

commit v3 on v2

--- a/solution.py
+++ b/solution.py
@@ -735,16 +735,31 @@
     )(turned, mixed, grad_heads, cosine, sine, rows_at, columns_at)
 
 
-def place_rows(pieces, own_seq):
+def place_rows(pieces, place):
     rows = pieces[0].shape[0] // 2
     width = pieces[0].shape[1]
-    out = jnp.zeros((8 * rows, width), jnp.float32)
-    for half in range(2):
-        for k in range(4):
-            at, block = PIECES[half][k]
-            block = pieces[at][block // 2 * rows :][:rows].astype(jnp.float32)
-            out = lax.dynamic_update_slice(out, block, (((own_seq ^ k) * 2 + half) * rows, 0))
-    return out
+
+    def body(place_ref, *refs):
+        for half in range(2):
+            for k in range(4):
+                at, block = PIECES[half][k]
+
+                @pl.when(pl.program_id(0) == half * 4 + k)
+                def _(at=at, start=block // 2 * rows):
+                    refs[4][...] = refs[at][start : start + rows, :].astype(jnp.float32)
+
+    return pl.pallas_call(
+        body,
+        grid_spec=pltpu.PrefetchScalarGridSpec(
+            num_scalar_prefetch=1,
+            grid=(8,),
+            in_specs=[pl.BlockSpec((2 * rows, width), lambda i, p: (0, 0))] * 4,
+            out_specs=pl.BlockSpec((rows, width), lambda i, p: ((p[0] ^ (i % 4)) * 2 + i // 4, 0)),
+        ),
+        out_shape=jax.ShapeDtypeStruct((8 * rows, width), jnp.float32),
+        compiler_params=pltpu.CompilerParams(vmem_limit_bytes=32 * 1024 * 1024),
+        name="place_rows",
+    )(place, *pieces)
 
 
 def mix_blocks(values):
@@ -794,9 +809,16 @@
 
     def halves_of_chip(*chips):
         half_rows = chip_rows // 2
-        mine = [lax.dynamic_slice_in_dim(c, own_core * half_rows, half_rows) for c in chips]
-        other = [lax.dynamic_slice_in_dim(c, (1 - own_core) * half_rows, half_rows) for c in chips]
-        return jnp.stack(mine), swap_cores(jnp.stack(other))
+
+        def of_core(core):
+            return jnp.stack(
+                [
+                    lax.dynamic_slice_in_dim(rows, start + core * half_rows, half_rows)
+                    for rows, start in chips
+                ]
+            )
+
+        return of_core(own_core), swap_cores(of_core(1 - own_core))
 
     factor_one = lax.rsqrt(jnp.mean(inputs * inputs, axis=-1, keepdims=True) + EPSILON)
     normed, qkv_own, qkv_other = fence(
@@ -851,10 +873,7 @@
         return mixed, *attend(mixed, *tables)
 
     mixed, attended, turned = window(needed, attention)
-    attended, out_proj, wide_send, cotangent_send, w_down = fence(
-        attended, out_proj, wide_chips[1], cotangent, w_down
-    )
-    cotangent_next = swap_rows(cotangent_send, 2)
+    attended, out_proj, wide_send, w_down = fence(attended, out_proj, wide_chips[1], w_down)
     wide_more = swap_rows(wide_send, 2)
     down_rows = [
         lax.dynamic_slice_in_dim(w_down, own_seq * 2 * chunk + (step ^ k) * chunk, chunk)
@@ -872,172 +891,181 @@
         middle = inputs + add_eighths(*own, *flight)
         return middle, norm_two_of(middle)[0]
 
+    def row_gather(block):
+        held, flight = row_two(block, *fence(*row_one(block)))
+        own, other = row_three(held, fence(*flight))
+        return own, *fence(other)
+
     middle, normed_two = window(needed, attention_out)
-    wide_more, cotangent_next, normed_two = fence(wide_more, cotangent_next, normed_two)
+    normed_two_next = swap_rows(normed_two, 2)
+    normed_two_row = window(needed, lambda: row_gather(normed_two))
+    wide_more, normed_two_next, down_send, cotangent_send, *normed_two_row = fence(
+        wide_more, normed_two_next, down_rows[1], cotangent, *normed_two_row
+    )
     gate_up_w = gather_rows(in_order(wide_chips[0], wide_more, step), ROW_PAIRS)
-
-    def gather_middle():
-        *flight, first, second = fence(*gather_one(normed_two), *row_one(cotangent_next))
-        cotangent_held, cotangent_flight = row_two(cotangent_next, first, second)
-        held, flight = gather_two(normed_two, *flight)
-        *flight, down_more = fence(*flight, swap_rows(down_rows[1], 2))
-        held, flight = gather_three(held, flight)
-        *flight, first, second = fence(*flight, *cotangent_flight)
-        held, last = gather_four(held, flight)
-        next_own, next_other = row_three(cotangent_held, (first, second))
-        last, next_other = fence(last, next_other)
-        return (
-            jnp.concatenate([*held, last]),
-            in_order(down_rows[0], down_more, step),
-            next_own,
-            next_other,
-        )
-
-    normed_two_all, down_pair, *cotangent_parts = window(needed, gather_middle)
-    down = gather_rows(down_pair, ROW_PAIRS)
+    cotangent_next = swap_rows(cotangent_send, 2)
+    down_more = swap_rows(down_send, 2)
+    normed_two_all = window(
+        needed, lambda: jnp.concatenate([*normed_two_row, *row_gather(normed_two_next)])
+    )
+    normed_two_all, cotangent_next = fence(normed_two_all, cotangent_next)
+    cotangent_all = window(
+        needed,
+        lambda: jnp.concatenate([cotangent_own, cotangent_other, *row_gather(cotangent_next)]),
+    )
+    down_more, cotangent_all = fence(down_more, cotangent_all)
+    down = gather_rows(in_order(down_rows[0], down_more, step), ROW_PAIRS)
 
     _, factor_two = norm_two_of(middle)
-    cotangent_all = jnp.concatenate([cotangent_own, cotangent_other, *cotangent_parts])
     gate_up = jnp.dot(normed_two_all, gate_up_w, preferred_element_type=jnp.float32)
     units = gate_up.shape[1] // 2
     gate, upward = gate_up[:, :units], gate_up[:, units:]
     sigmoid = jax.nn.sigmoid(gate)
     activated = gate * sigmoid
     hidden = (activated * upward).astype(jnp.bfloat16)
-    hidden, cotangent_all = fence(hidden, cotangent_all)
-    forward_far, forward_other = project(token_part(hidden, 2), down), project(
-        token_part(hidden, 3), down
-    )
-    forward_far, forward_other = fence(forward_far, forward_other)
+    grad_down_term = outer_sum(hidden, cotangent_all).astype(jnp.bfloat16)
+    grad_down_pair = scatter_rows(grad_down_term, ROW_PAIRS)
+    cotangent_all, grad_down_term = fence(cotangent_all, grad_down_term)
     grad_hidden = back_product(cotangent_all, down)
     grad_gate = grad_hidden * upward * sigmoid * (1.0 + gate * (1.0 - sigmoid))
     grad_upward = grad_hidden * activated
     grad_low = jnp.concatenate([grad_gate, grad_upward], axis=1).astype(jnp.bfloat16)
-    grad_low, swapped = fence(grad_low, swap_cores(forward_other))
-    forward_far = add(forward_far, swapped)
-    forward_near, forward_other = project(token_part(hidden, 0), down), project(
-        token_part(hidden, 1), down
-    )
 
     def backward_part(grad, weight, k):
         return back_product(token_part(grad, k), weight).astype(jnp.bfloat16)
 
-    far, far_other, forward_near, forward_other, *flight = fence(
-        backward_part(grad_low, gate_up_w, 2),
-        backward_part(grad_low, gate_up_w, 3),
-        forward_near,
-        forward_other,
-        *send_quarters(forward_far),
-    )
-    forward_far = add_quarters(forward_far, *flight)
-    grad_down_term = outer_sum(hidden, cotangent_all).astype(jnp.bfloat16)
-    swapped, far, near, near_other, grad_down_term, forward_swapped, *flight = fence(
-        swap_cores(far_other),
-        far,
+    far, far_other = fence(
+        backward_part(grad_low, gate_up_w, 2), backward_part(grad_low, gate_up_w, 3)
+    )
+    grad_gate_up_term = outer_sum(normed_two_all, grad_low).astype(jnp.bfloat16)
+    swapped, far, grad_gate_up_term, grad_low, grad_down_pair, hidden = fence(
+        swap_cores(far_other), far, grad_gate_up_term, grad_low, grad_down_pair, hidden
+    )
+    grad_gate_up_pair = scatter_rows(grad_gate_up_term, ROW_PAIRS)
+    far = add(far, swapped)
+    *flight, near, near_other, forward_far, forward_other = fence(
+        *send_quarters(far),
         backward_part(grad_low, gate_up_w, 0),
         backward_part(grad_low, gate_up_w, 1),
-        grad_down_term,
-        swap_cores(forward_other),
-        *send_eighths(*forward_far),
-    )
-    far = add(far, swapped)
-    forward_near = add(forward_near, forward_swapped)
-    forward_far = add_eighths(*forward_far, *flight).astype(jnp.bfloat16)
-    grad_down_pair = scatter_rows(grad_down_term, ROW_PAIRS)
-    grad_gate_up_term = outer_sum(normed_two_all, grad_low).astype(jnp.bfloat16)
-    *flight, swapped, grad_gate_up_term = fence(
-        *send_quarters(far), swap_cores(near_other), grad_gate_up_term
+        project(token_part(hidden, 2), down),
+        project(token_part(hidden, 3), down),
     )
     far = add_quarters(far, *flight)
-    near = add(near, swapped)
-    grad_gate_up_pair = scatter_rows(grad_gate_up_term, ROW_PAIRS)
 
     def feed_forward_back():
-        *flight, first, second = fence(*send_eighths(*far), *send_quarters(near))
+        *flight, swapped, forward_swapped = fence(
+            *send_eighths(*far), swap_cores(near_other), swap_cores(forward_other)
+        )
         next_row = add_eighths(*far, *flight).astype(jnp.bfloat16)
-        quarters = add_quarters(near, first, second)
+        near_sum = add(near, swapped)
+        forward_sum = add(forward_far, forward_swapped)
         next_row, first, second, *flight = fence(
-            swap_rows(next_row, 2), *send_eighths(*quarters), *send_quarters(forward_near)
+            swap_rows(next_row, 2), *send_quarters(near_sum), *send_quarters(forward_sum)
+        )
+        quarters = add_quarters(near_sum, first, second)
+        forward_quarters = add_quarters(forward_sum, *flight)
+        first, second, *flight = fence(
+            *send_eighths(*quarters), *send_eighths(*forward_quarters)
         )
         scaled = mix_blocks(add_eighths(*quarters, first, second) + next_row.astype(jnp.float32))
-        forward_quarters = add_quarters(forward_near, *flight)
         grad_middle = (
             cotangent.astype(jnp.float32)
             + factor_two * scaled
             - middle * factor_two**3 * jnp.mean(scaled * middle, axis=-1, keepdims=True)
         )
+        return grad_middle, add_eighths(*forward_quarters, *flight).astype(jnp.bfloat16)
+
+    grad_middle, forward_far = window(needed, feed_forward_back)
+    wide_send = lax.dynamic_slice_in_dim(grad_gate_up_pair, (1 - step) * chip_rows, chip_rows)
+    grad_middle, wide_send = fence(grad_middle, wide_send)
+    wide_more = swap_rows(wide_send, 2)
+
+    def gather_branch():
         block = grad_middle.astype(jnp.bfloat16)
-        down_own, down_send = own_rows(grad_down_pair, chunk)
-        *flight, first, second, forward_next = fence(
-            *row_one(block), *send_eighths(*forward_quarters), swap_rows(forward_far, 2)
-        )
-        output = middle + forward_next.astype(jnp.float32)
-        output = output + add_eighths(*forward_quarters, first, second)
+        forward = [project(token_part(hidden, k), down) for k in range(2)]
+        *flight, swapped = fence(*row_one(block), swap_cores(forward[1]))
         held, flight = row_two(block, *flight)
-        *flight, down_more = fence(*flight, swap_rows(down_send, 2))
+        flight = fence(*flight)
         own, other = row_three(held, flight)
-        down_halves = halves(in_order(down_own, down_more, step))
-        return jnp.concatenate([own, *fence(other)]), grad_middle, output, down_halves
-
-    grad_branch, grad_middle, output, down_halves = window(needed, feed_forward_back)
-
-    wide_own, wide_send = own_rows(grad_gate_up_pair, chip_rows)
-    grad_branch, wide_send = fence(grad_branch, wide_send)
-    wide_more = swap_rows(wide_send, 2)
+        forward_sum = add(forward[0], swapped)
+        other, *flight = fence(other, *send_quarters(forward_sum))
+        return jnp.concatenate([own, other]), add_quarters(forward_sum, *flight)
+
+    grad_branch, forward_near = window(needed, gather_branch)
+
+    down_own, down_send = own_rows(grad_down_pair, chunk)
+    grad_branch, wide_more, down_send = fence(grad_branch, wide_more, down_send)
 
     def attention_back():
         grad_heads = back_product(grad_branch, out_proj).astype(jnp.bfloat16)
+        grad_heads, *wide_halves = fence(
+            grad_heads, *halves_of_chip((grad_gate_up_pair, step * chip_rows), (wide_more, 0))
+        )
+        flight = share_one(*wide_halves)
+        down_more = swap_rows(down_send, 2)
         grad_mixed = attend_back(turned, mixed, grad_heads, *tables)
-        grad_mixed, *flight = fence(grad_mixed, *share_one(*down_halves))
-        held, flight = share_two(*down_halves, *flight)
+        grad_mixed, *near = fence(grad_mixed, *forward_near)
         grad_qkv_term = outer_sum(normed_all, grad_mixed).astype(jnp.bfloat16)
-        return grad_mixed, grad_qkv_term, shared(held, fence(*flight))
-
-    grad_mixed, grad_qkv_term, down_pieces = window(needed, attention_back)
-    grad_qkv_term, wide_more = fence(grad_qkv_term, wide_more)
+        arrived = fence(grad_qkv_term, down_more, *send_eighths(*near), *flight)
+        return grad_mixed, wide_halves, arrived
+
+    grad_mixed, wide_halves, arrived = window(needed, attention_back)
+    grad_qkv_term, down_more, forward_first, forward_second, *wide_flight = arrived
     grad_qkv_rows = scatter_rows(grad_qkv_term, ROWS)
-    grad_out_rows = scatter_rows(outer_sum(attended, grad_branch), ROWS)
+    wide_held, wide_flight = share_two(*wide_halves, *wide_flight)
 
     def inputs_back():
         back = backward(grad_mixed, qkv)
-        mine, swapped = halves_of_chip(wide_own, wide_more)
-        swapped, row_swapped, near = fence(swapped, swap_cores(back[1]), back[0])
-        near = add(near, row_swapped)
-        wide_halves = mine, swapped
-        *row_flight, first, second = fence(*send_quarters(near), *share_one(*wide_halves))
-        near = add_quarters(near, *row_flight)
+        swapped, near = fence(swap_cores(back[1]), back[0])
+        near = add(near, swapped)
+        near = add_quarters(near, *fence(*send_quarters(near)))
         scaled = add_eighths(*near, *fence(*send_eighths(*near)))
-        grad_inputs = (
+        return (
             grad_middle
             + factor_one * scaled
             - inputs * factor_one**3 * jnp.mean(scaled * inputs, axis=-1, keepdims=True)
         )
-        return grad_inputs, wide_halves, (first, second)
-
-    grad_inputs, wide_halves, wide_flight = window(needed, inputs_back)
-
-    wide_held, wide_flight = share_two(*wide_halves, *wide_flight)
-    grad_qkv_rows, grad_inputs = fence(grad_qkv_rows, grad_inputs)
-    qkv_halves = fence(*halves_of_chip(grad_qkv_rows))
-    out_halves = halves(grad_out_rows)
-    *qkv_flight, first, second = fence(*share_one(*qkv_halves), *share_one(*out_halves))
-    qkv_held, qkv_flight = share_two(*qkv_halves, *qkv_flight)
-    out_held, out_flight = share_two(*out_halves, first, second)
+
+    grad_inputs = window(needed, inputs_back)
+
+    grad_qkv_rows, grad_inputs, attended, forward_far, w_gate_up, down_own, down_more = fence(
+        grad_qkv_rows, grad_inputs, attended, forward_far, w_gate_up, down_own, down_more
+    )
+    down_halves = halves(in_order(down_own, down_more, step))
+    qkv_mine, qkv_swapped = halves_of_chip((grad_qkv_rows, 0))
+    qkv_swapped, *down_halves = fence(qkv_swapped, *down_halves)
+    qkv_halves = qkv_mine, qkv_swapped
+    flight = *share_one(*qkv_halves), *share_one(*down_halves)
+    grad_out_rows = scatter_rows(outer_sum(attended, grad_branch), ROWS)
+    forward_next = swap_rows(forward_far, 2)
     grad_gate_up, gain_two_sums = merge_wide(
         shared(wide_held, wide_flight), w_gate_up, gain_two, place, 8, chunk
     )
+    grad_gate_up, gain_two_sums, *flight = fence(grad_gate_up, gain_two_sums, *flight)
+    qkv_held, qkv_flight = share_two(*qkv_halves, *flight[:2])
+    down_held, down_flight = share_two(*down_halves, *flight[2:])
+    grad_out_rows, *qkv_flight = fence(grad_out_rows, *qkv_flight)
+    out_halves = halves(grad_out_rows)
     grad_qkv, gain_one_sums = merge_heads(
         shared(qkv_held, qkv_flight), w_qkv, gain_one, place, heads
     )
+    grad_qkv, gain_one_sums, forward_next, *flight = fence(
+        grad_qkv, gain_one_sums, forward_next, *down_flight, *share_one(*out_halves)
+    )
+    out_held, out_flight = share_two(*out_halves, *flight[2:])
+    output = middle + forward_next.astype(jnp.float32)
+    output = output + add_eighths(*forward_near, forward_first, forward_second)
+    grad_down = place_rows(shared(down_held, flight[:2]), place)
+    grad_down, output, *out_flight = fence(grad_down, output, *out_flight)
     return (
         output.astype(jnp.bfloat16)[None],
         grad_inputs[None],
         jnp.sum(gain_one_sums, axis=(0, 2)),
         grad_qkv,
-        place_rows(shared(out_held, out_flight), own_seq),
+        place_rows(shared(out_held, out_flight), place),
         jnp.sum(gain_two_sums, axis=(0, 2)),
         grad_gate_up,
-        place_rows(down_pieces, own_seq),
+        grad_down,
     )
 
 

time: 794 us -> 726 us (0.914)
  waiting for transfers between devices: 331 us -> 287 us
  other arithmetic: 87.9 us -> 61 us
  Pallas kernels: 58 us -> 68.4 us
    ppermute x8, waiting for transfers between devices: 92.8 us -> 17.2 us  [swap_rows(): return lax.ppermute(values, 'fsdp', xor_pairs(8, 2 * offset))]
    dynamic_update_slice x16 -> x0, other arithmetic: 18.1 us -> none  [place_rows(): lax.dynamic_update_slice(out, block, (((own_seq ^ k) * 2 + half) * rows, 0))]
    ppermute x64, waiting for transfers between devices: 213 us -> 225 us  [swap_seq(): return lax.ppermute(values, 'seq', xor_pairs(4, offset))]
    ppermute x16, waiting for transfers between devices: 7.76 us -> 19 us  [swap_cores(): return lax.ppermute(values, 'fsdp', xor_pairs(8, 1))]
    pallas_call x0 -> x2, Pallas kernels: none -> 11.1 us  [place_rows(): pl.pallas_call(body, grid_spec=pltpu.PrefetchScalarGridSpec(num_scalar_pr...]
    all_gather x4, waiting for transfers between devices: 15.4 us -> 25.5 us  [gather_rows(): lax.all_gather(block, 'fsdp', axis=0, tiled=True, axis_index_groups=groups)]
    concatenate x5 -> x0, other arithmetic: 8.8 us -> none  [the longest x1 6.68 us: sliced_plan(): jnp.concatenate([cotangent_own, cotangent_other, *cotangent_parts])]
    cond x104 -> x74, local copies, waits for them, and re-layouts: 38.2 us -> 38.5 us
  transfers between devices with their start and end apart: 96 -> 96, of which waited for: 53 -> 63; matrix products, arithmetic and copies ran while one was open for 34% -> 33% of each run, Pallas kernels for 6% -> 8%
where the time goes in v3:
time: 726 us; the launch traced here: 717 us
  waiting for transfers between devices  287 us (40%)
  matrix products  101 us (14%)
  local copies, waits for them, and re-layouts  94.5 us (13%)
  starting transfers between devices  89.3 us (12%)
  Pallas kernels  68.4 us (9%)
  other arithmetic  61 us (8%)
  between operations  15.2 us (2%)
    ppermute x64, waiting for transfers between devices, swap_seq(): return lax.ppermute(values, 'seq', xor_pairs(4, offset))  225 us
    ppermute x64, starting transfers between devices, swap_seq(): return lax.ppermute(values, 'seq', xor_pairs(4, offset))  72.7 us
    cond x74, local copies, waits for them, and re-layouts  38.5 us
    dot_general x8, matrix products, back_product(): lax.dot_general(grad, weight, (((1,), (1,)), ((), ())), preferred_element...  35.1 us
    dot_general x4, matrix products, outer_sum(): lax.dot_general(left, right, (((0,), (0,)), ((), ())), preferred_element_...  34.1 us
    all_gather x4, waiting for transfers between devices, gather_rows(): lax.all_gather(block, 'fsdp', axis=0, tiled=True, axis_index_groups=groups)  25.5 us
    ppermute x16, waiting for transfers between devices, swap_cores(): return lax.ppermute(values, 'fsdp', xor_pairs(8, 1))  19 us
    dot_general x7, matrix products, project(): jnp.dot(rows, weight, preferred_element_type=jnp.float32)  18.5 us
  transfers between devices with their start and end apart: 96, of which 63 were waited for; matrix products, arithmetic and copies ran while one was open for 33% of the time, Pallas kernels for 8%

profile of v3, /device:TPU:0, one launch (start us, length us, event | category | flops | bytes accessed | tf_op | source)
XLA Modules:
  0.0 716.9 jit_solution(1052488386867967105)
XLA Ops:
  22.5 64.5 %conditional.10 = (bf16[1024,2048]{1,0:T(8,128)(2,1)}, bf16[512,1024]{1,0:T(8,128)(2,1)S(1)}, bf16[512,1024]{1,0:T(8,128)(2,1)S(1)}, bf16[512,2048]{1,0:T(8,128)(2,1)}, bf16[512,2048]{1,0:T(8,128)(2,1)}) conditional(s32[]{:T(128)} %convert_element_type.295, () %tuple.140, (bf16[128,2048]{1,0:T(8,128)(2,1)S(1)}, s32[3]{0:T(128)S(1)}, ...), branch_computations={%region_1.2_spmd, %region_2.3_spmd} | conditional | flops 9437185 | bytes 88869488 | solution.py:256
  67.8 10.0 %collective-permute-done.8 = bf16[128,2048]{1,0:T(8,128)(2,1)S(1)} collective-permute-done((bf16[128,2048]{1,0:T(8,128)(2,1)S(1)}, bf16[128,2048]{1,0:T(8,128)(2,1)S(1)}, u32[]{:S(2)}, u32[]{:S(2)}) %collective-permute-start.8) | collective-permute-done | bytes 524320 | tf_op jit(solution)/shard_map/cond/branch_1_fun/ppermute | solution.py:247
  88.6 18.3 %conditional.11 = (bf16[1024,768]{1,0:T(8,128)(2,1)}, bf16[1024,256]{1,0:T(8,128)(2,1)S(1)}, bf16[1024,512]{1,0:T(8,128)(2,1)}) conditional(s32[]{:T(128)} %convert_element_type.295, () %tuple.139, (bf16[1024,2048]{1,0:T(8,128)(2,1)}, bf16[2048,768]{1,0:T(8,128)(2,1)}, f32[512,128]{0,1:T(8,128)}, f32[512,128]{0,1:T(8,128)}, s32[512,1]{0,1:T(1,128)S(1)}, ...), branch_computations={%region_3.4_spmd, %region_4.5_spmd} | conditional | flops 4295753728 | bytes 13111320 | solution.py:256
  88.7 7.8 %convolution_convert_fusion.mixed_ref = bf16[1024,768]{1,0:T(8,128)(2,1)} fusion(bf16[1024,2048]{1,0:T(8,128)(2,1)} %get-tuple-element.165, bf16[2048,768]{1,0:T(8,128)(2,1)} %get-tuple-element.166), kind=kOutput, calls=%fused_computation.29 | convolution fusion | flops 3222011904 | bytes 8912896 | tf_op jit(solution)/shard_map/cond/branch_1_fun/dot_general | solution.py:793
  98.8 8.2 %attend.1 = (bf16[1024,256]{1,0:T(8,128)(2,1)S(1)}, bf16[1024,512]{1,0:T(8,128)(2,1)}) custom-call(bf16[1024,768]{1,0:T(8,128)(2,1)} %convolution_convert_fusion.mixed_ref, f32[512,128]{1,0:T(8,128)S(1)} %copy.23.cosine_ref, f32[512,128]{1,0:T(8,128)S(1)} %copy.24.sine_ref, s32[512,1]{1,0:T(8,128)S(1)} %copy.25.rows_ref, ...), custom_call_target="tpu_custom_call" | custom-call | flops 1073741824 | bytes 3145728 | tf_op jit(solution)/shard_map/cond/branch_1_fun/attend/pallas_call | solution.py:646
  107.0 8.2 %all-gather.7.cloned.1.call-done = bf16[256,2048]{1,0:T(8,128)(2,1)} async-done(((bf16[64,2048]{1,0:T(8,128)(2,1)}), bf16[256,2048]{1,0:T(8,128)(2,1)}) %all-gather.7.cloned.1.call-update) | async-done | bytes 1048592 | tf_op jit(solution)/shard_map/all_gather | solution.py:378
  118.2 38.4 %conditional.12 = (f32[128,2048]{1,0:T(8,128)}, bf16[128,2048]{1,0:T(8,128)(2,1)}, f32[128,1]{0,1:T(1,128)}, bf16[128,2048]{1,0:T(8,128)(2,1)S(1)}) conditional(s32[]{:T(128)} %convert_element_type.295, () %tuple.138, (bf16[1024,256]{1,0:T(8,128)(2,1)S(1)}, bf16[256,2048]{1,0:T(8,128)(2,1)}, f32[128,2048]{1,0:T(8,128)}) %tuple.146), branch_computations={%region_5.6_spmd, %region_6.8_spmd} | conditional | flops 1085800576 | bytes 49809668 | solution.py:256
  128.5 11.0 %collective-permute-done.40 = bf16[128,2048]{1,0:T(8,128)(2,1)S(1)} collective-permute-done((bf16[128,2048]{1,0:T(8,128)(2,1)S(1)}, bf16[128,2048]{1,0:T(8,128)(2,1)S(1)}, u32[]{:S(2)}, u32[]{:S(2)}) %collective-permute-start.40) | collective-permute-done | bytes 524320 | tf_op jit(solution)/shard_map/cond/branch_1_fun/ppermute | solution.py:247
  157.7 27.2 %conditional.13 = (bf16[512,2048]{1,0:T(8,128)(2,1)}, bf16[512,2048]{1,0:T(8,128)(2,1)}) conditional(s32[]{:T(128)} %convert_element_type.295, () %tuple.147, bf16[128,2048]{1,0:T(8,128)(2,1)S(1)} %get-tuple-element.407), branch_computations={%region_8.9_spmd, %region_9.10_spmd} | conditional | flops 2097152 | bytes 21758168 | solution.py:256
  168.6 7.5 %collective-permute-done.24 = bf16[128,2048]{1,0:T(8,128)(2,1)S(1)} collective-permute-done((bf16[128,2048]{1,0:T(8,128)(2,1)S(1)}, bf16[128,2048]{1,0:T(8,128)(2,1)S(1)}, u32[]{:S(2)}, u32[]{:S(2)}) %collective-permute-start.24) | collective-permute-done | bytes 524320 | tf_op jit(solution)/shard_map/cond/branch_1_fun/ppermute | solution.py:247
  193.0 31.1 %conditional.14 = (bf16[2048,2048]{1,0:T(8,128)(2,1)}) conditional(s32[]{:T(128)} %convert_element_type.295, () %tuple.150, (bf16[128,2048]{1,0:T(8,128)(2,1)S(1)}, bf16[512,2048]{1,0:T(8,128)(2,1)}, bf16[512,2048]{1,0:T(8,128)(2,1)}) %tuple.151), branch_computations={%region_10.11_spmd, %region_11.12_spmd} | conditional | flops 2097152 | bytes 37748944 | solution.py:256
  225.0 32.3 %conditional.15 = (bf16[2048,2048]{1,0:T(8,128)(2,1)}) conditional(s32[]{:T(128)} %convert_element_type.295, () %tuple.149, (bf16[128,2048]{1,0:T(8,128)(2,1)S(1)}, bf16[512,2048]{1,0:T(8,128)(2,1)}, bf16[512,2048]{1,0:T(8,128)(2,1)}) %tuple.153), branch_computations={%region_12.13_spmd, %region_13.14_spmd} | conditional | flops 2097152 | bytes 37748944 | solution.py:256
  259.7 7.7 %all-gather.9.cloned.1.call-done = bf16[2048,1024]{1,0:T(8,128)(2,1)} async-done(((bf16[1024,1024]{1,0:T(8,128)(2,1)}), bf16[2048,1024]{1,0:T(8,128)(2,1)}) %all-gather.9.cloned.1.call-update) | async-done | bytes 4194320 | tf_op jit(solution)/shard_map/all_gather | solution.py:378
  267.4 13.5 %fusion.38 = f32[2048,1024]{0,1:T(8,128)S(1)} fusion(bf16[2048,2048]{1,0:T(8,128)(2,1)} %get-tuple-element.707, bf16[2048,1024]{1,0:T(8,128)(2,1)} %all-gather.9.cloned.1.call-done), kind=kOutput, calls=%fused_computation.265 | convolution fusion | flops 8589934592 | bytes 20971520 | tf_op jit(solution)/shard_map/dot_general | solution.py:920
  284.3 9.1 %convolution_convert_fusion.16 = bf16[512,2048]{1,0:T(8,128)(2,1)} fusion(bf16[2048,512]{0,1:T(8,128)(2,1)S(1)} %multiply_convert_fusion.3, bf16[2048,2048]{1,0:T(8,128)(2,1)} %get-tuple-element.708), kind=kOutput, calls=%fused_computation.194 | convolution fusion | flops 4296015872 | bytes 12582912 | tf_op jit(solution)/shard_map/dot_general | solution.py:20
  293.6 9.6 %all-gather.11.cloned.1.call-done = bf16[512,2048]{1,0:T(8,128)(2,1)} async-done(((bf16[256,2048]{1,0:T(8,128)(2,1)}), bf16[512,2048]{1,0:T(8,128)(2,1)}) %all-gather.11.cloned.1.call-update) | async-done | bytes 2097168 | tf_op jit(solution)/shard_map/all_gather | solution.py:378
  303.2 12.1 %multiply_convert_fusion.1 = (bf16[2048,512]{0,1:T(8,128)(2,1)S(1)}, bf16[2048,512]{0,1:T(8,128)(2,1)S(1)}) fusion(f32[2048,1024]{0,1:T(8,128)} %copy-done.5, bf16[2048,2048]{1,0:T(8,128)(2,1)} %get-tuple-element.708, bf16[512,2048]{1,0:T(8,128)(2,1)} %all-gather.11.cloned.1.call-done), kind=kOutput, calls=%fused_computation.182 | convolution fusion | flops 4308598784 | bytes 23068672 | tf_op jit(solution)/shard_map/dot_general | solution.py:26
  325.4 12.8 %convolution_convert_fusion.9 = bf16[2048,1024]{1,0:T(8,128)(2,1)} fusion(bf16[2048,2048]{1,0:T(8,128)(2,1)} %get-tuple-element.707, bf16[2048,512]{0,1:T(8,128)(2,1)S(1)} %get-tuple-element.624, bf16[2048,512]{0,1:T(8,128)(2,1)S(1)} %get-tuple-element.625), kind=kOutput, calls=%fused_computation.187 | convolution fusion | flops 8600420352 | bytes 16777216 | tf_op jit(solution)/shard_map/dot_general | solution.py:20
  357.5 56.6 %conditional.16 = (f32[128,2048]{1,0:T(8,128)S(1)}, bf16[128,2048]{1,0:T(8,128)(2,1)}) conditional(s32[]{:T(128)} %convert_element_type.295, () %tuple.137, (bf16[128,2048]{1,0:T(8,128)(2,1)S(1)}, f32[128,1]{0,1:T(1,128)}, f32[128,1]{0,1:T(1,128)S(1)}, bf16[512,2048]{1,0:T(8,128)(2,1)S(1)}, bf16[128,2048]{1,0:T(8,128)(2,1)S(1)}, ...), branch_computations={%region_15.16_spmd, %region_16.18_spmd} | conditional | flops 21234176 | bytes 90707536 | solution.py:256
  377.2 16.2 %collective-permute-done.30 = bf16[128,2048]{1,0:T(8,128)(2,1)S(1)} collective-permute-done((bf16[128,2048]{1,0:T(8,128)(2,1)S(1)}, bf16[128,2048]{1,0:T(8,128)(2,1)S(1)}, u32[]{:S(2)}, u32[]{:S(2)}) %collective-permute-start.30) | collective-permute-done | bytes 524320 | tf_op jit(solution)/shard_map/cond/branch_1_fun/ppermute | solution.py:243
  419.6 55.7 %conditional.17 = (bf16[1024,2048]{1,0:T(8,128)(2,1)}, f32[128,2048]{1,0:T(8,128)S(1)}, f32[128,2048]{1,0:T(8,128)}) conditional(s32[]{:T(128)} %convert_element_type.295, () %tuple.136, (f32[128,2048]{1,0:T(8,128)S(1)}, bf16[2048,512]{0,1:T(8,128)(2,1)S(1)}, bf16[512,2048]{1,0:T(8,128)(2,1)}) %tuple.161), branch_computations={%region_19.20_spmd, %region_20.21_spmd} | conditional | flops 2157707264 | bytes 78119288 | solution.py:256
  437.2 11.1 %collective-permute-done.47 = bf16[128,2048]{1,0:T(8,128)(2,1)S(1)} collective-permute-done((bf16[128,2048]{1,0:T(8,128)(2,1)S(1)}, bf16[128,2048]{1,0:T(8,128)(2,1)S(1)}, u32[]{:S(2)}, u32[]{:S(2)}) %collective-permute-start.47) | collective-permute-done | bytes 524320 | tf_op jit(solution)/shard_map/cond/branch_1_fun/ppermute | solution.py:247
  459.2 12.9 %collective-permute-done.50 = bf16[128,2048]{1,0:T(8,128)(2,1)S(1)} collective-permute-done((bf16[128,2048]{1,0:T(8,128)(2,1)S(1)}, bf16[128,2048]{1,0:T(8,128)(2,1)S(1)}, u32[]{:S(2)}, u32[]{:S(2)}) %collective-permute-start.50) | collective-permute-done | bytes 524320 | tf_op jit(solution)/shard_map/cond/branch_1_fun/ppermute | solution.py:247
  476.2 39.1 %conditional.18 = (bf16[1024,768]{1,0:T(8,128)(2,1)}, bf16[2,256,1024]{2,1,0:T(8,128)(2,1)}, bf16[2,256,1024]{2,1,0:T(8,128)(2,1)}, bf16[2048,768]{0,1:T(8,128)(...) conditional(s32[]{:T(128)} %convert_element_type.295, ...), branch_computations={%region_21.22_spmd, %region_22.23_spmd} | conditional | flops 6982467584 | bytes 58200684 | solution.py:256
  490.1 12.4 %attend_back.1 = bf16[1024,768]{1,0:T(8,128)(2,1)} custom-call(bf16[1024,512]{1,0:T(8,128)(2,1)} %get-tuple-element.236.turned_ref, bf16[1024,768]{1,0:T(8,128)(2,1)} %get-tuple-element.237.values_ref, bf16[1024,256]{1,0:T(8,128)(2,1)S(1)} %convolution_convert_fusion.6.grad_ref, f32[512,128]{1,0:T(8,128)S(1)} %copy.27.cosine_ref, ...), custom_call_target="tpu_custom_call" | custom-call | flops 2684354560 | bytes 4194304 | tf_op jit(solution)/shard_map/cond/branch_1_fun/attend_back/pallas_call | solution.py:714
  506.7 7.8 %fusion.10 = bf16[2048,768]{0,1:T(8,128)(2,1)} fusion(bf16[1024,768]{1,0:T(8,128)(2,1)} %attend_back.1, bf16[1024,2048]{1,0:T(8,128)(2,1)} %get-tuple-element.254), kind=kOutput, calls=%fused_computation.146 | convolution fusion | flops 3222798336 | bytes 8912896 | tf_op jit(solution)/shard_map/cond/branch_1_fun/dot_general | solution.py:20
  526.2 68.6 %conditional.19 = (f32[128,2048]{1,0:T(8,128)}) conditional(s32[]{:T(128)} %convert_element_type.295, () %tuple.164, (f32[128]{0:T(128)S(1)}, f32[128,1]{0,1:T(1,128)S(1)}, bf16[1024,768]{1,0:T(8,128)(2,1)}, bf16[2048,768]{1,0:T(8,128)(2,1)}, f32[128,2048]{1,0:T(8,128)}, /*index=5*/f32[128,2048]{1,0:T(8,128)}) %tuple.289), branch_computations={%region_24.25_spmd, %region_25.27_spmd} | conditional | flops 3231973888 | bytes 66065672 | solution.py:256
  537.1 45.7 %collective-permute-done.59 = bf16[128,2048]{1,0:T(8,128)(2,1)S(1)} collective-permute-done((bf16[128,2048]{1,0:T(8,128)(2,1)S(1)}, bf16[128,2048]{1,0:T(8,128)(2,1)S(1)}, u32[]{:S(2)}, u32[]{:S(2)}) %collective-permute-start.59) | collective-permute-done | bytes 524320 | tf_op jit(solution)/shard_map/cond/branch_1_fun/ppermute | solution.py:247
  602.8 16.0 %merge_wide.1 = (f32[256,16384]{1,0:T(8,128)}, f32[4,256,128]{2,1,0:T(8,128)S(1)}) custom-call(s32[3]{0:T(128)S(1)} %copy-done.37, bf16[4,256,1024]{2,1,0:T(8,128)(2,1)} %constant_dynamic-update-slice_fusion.68.refs_0_, bf16[4,256,1024]{2,1,0:T(8,128)(2,1)} %collective-permute-done.73.refs_1_, ...), custom_call_target="tpu_custom_call" | custom-call | tf_op jit(solution)/shard_map/merge_wide/pallas_call | solution.py:504
  624.4 19.0 %collective-permute-done.76 = bf16[1,256,768]{2,1,0:T(8,128)(2,1)S(1)} collective-permute-done((bf16[1,256,768]{2,1,0:T(8,128)(2,1)}, bf16[1,256,768]{2,1,0:T(8,128)(2,1)S(1)}, u32[]{:S(2)}, u32[]{:S(2)}) %collective-permute-start.76) | collective-permute-done | bytes 393248 | tf_op jit(solution)/shard_map/ppermute | solution.py:247
  652.3 11.7 %collective-permute-done.80.refs_3_ = bf16[2,256,768]{2,1,0:T(8,128)(2,1)S(1)} collective-permute-done((bf16[2,256,768]{2,1,0:T(8,128)(2,1)S(1)}, bf16[2,256,768]{2,1,0:T(8,128)(2,1)S(1)}, u32[]{:S(2)}, u32[]{:S(2)}) %collective-permute-start.80) | collective-permute-done | bytes 786464 | tf_op jit(solution)/shard_map/ppermute | solution.py:247
  673.3 9.0 %merge_heads.1 = (f32[256,6144]{1,0:T(8,128)}, f32[2,256,128]{2,1,0:T(8,128)}) custom-call(s32[3]{0:T(128)S(1)} %copy-done.37, bf16[2,256,768]{2,1,0:T(8,128)(2,1)} %copy-done.17, bf16[2,256,768]{2,1,0:T(8,128)(2,1)} %collective-permute-done.79.refs_1_, bf16[2,256,768]{2,1,0:T(8,128)(2,1)} %copy-done.26, bf16[2,256,768]{2,1,0:T(8,128)(2,1)} %copy-done.31, ...), custom_call_target="tpu_custom_call" | custom-call | tf_op jit(solution)/shard_map/merge_heads/pallas_call | solution.py:571
  (509 shorter events, 421.7 us)
Async XLA Ops:
  7.2 79.9 %all-gather.5.cloned.1.call-start = ((), (), s32[]{:S(2)}) async-start(), calls=%async_computation.4 | async-start | bytes 3932160 | tf_op jit(solution)/shard_map/all_gather | solution.py:378
  20.8 94.5 %all-gather.7.cloned.1.call-start = ((), (), s32[]{:S(2)}) async-start(), calls=%async_computation.5 | async-start | bytes 1310720 | tf_op jit(solution)/shard_map/all_gather | solution.py:378
  21.6 245.8 %all-gather.9.cloned.1.call-start = ((), (), s32[]{:S(2)}) async-start(), calls=%async_computation.6 | async-start | bytes 6291456 | tf_op jit(solution)/shard_map/all_gather | solution.py:378
  115.2 70.8 %collective-permute-start.64 = (bf16[512,1024]{1,0:T(8,128)(2,1)}, bf16[512,1024]{1,0:T(8,128)(2,1)}, u32[]{:S(2)}, u32[]{:S(2)}) collective-permute-start(bf16[512,1024]{1,0:T(8,128)(2,1)} %copy-done.30), channel_id=1, source_target_pairs={{0,4},{1,5},{2,6},{3,7},{4,0},{5,1},{6,2},{7,3},{8,12},{9,13},{10,... | collective-permute-start | bytes 3145736 | tf_op jit(solution)/shard_map/ppermute | solution.py:243
  156.6 29.5 %collective-permute-start.65 = (bf16[128,2048]{1,0:T(8,128)(2,1)}, bf16[128,2048]{1,0:T(8,128)(2,1)S(1)}, u32[]{:S(2)}, u32[]{:S(2)}) collective-permute-start(bf16[128,2048]{1,0:T(8,128)(2,1)} %get-tuple-element.405), channel_id=1, source_target_pairs={{0,4},{1,5},{2,6},{3,7},{4,0},{5,1},{6,2},{7,3},{8,12},{9,13},{10,... | collective-permute-start | bytes 1572872 | tf_op jit(solution)/shard_map/ppermute | solution.py:243
  189.0 114.2 %all-gather.11.cloned.1.call-start = ((), (), s32[]{:S(2)}) async-start(), calls=%async_computation.7 | async-start | bytes 3145728 | tf_op jit(solution)/shard_map/all_gather | solution.py:378
  190.0 35.0 %collective-permute-start.67 = (bf16[128,2048]{1,0:T(8,128)(2,1)S(1)}, bf16[128,2048]{1,0:T(8,128)(2,1)S(1)}, u32[]{:S(2)}, u32[]{:S(2)}) collective-permute-start(bf16[128,2048]{1,0:T(8,128)(2,1)S(1)} %bitcast.82), channel_id=1, source_target_pairs={{0,4},{1,5},{2,6},{3,7},{4,0},{5,1},{6,2},{7,3},{8,12},{9,13},{10,... | collective-permute-start | bytes 1572872 | tf_op jit(solution)/shard_map/ppermute | solution.py:243
  191.7 65.6 %collective-permute-start.66 = (bf16[128,2048]{1,0:T(8,128)(2,1)S(1)}, bf16[128,2048]{1,0:T(8,128)(2,1)S(1)}, u32[]{:S(2)}, u32[]{:S(2)}) collective-permute-start(bf16[128,2048]{1,0:T(8,128)(2,1)S(1)} %constant_dynamic-slice_fusion.5), channel_id=1, source_target_pairs={{0,4},{1,5},{2,6},{3,7},{4,0},{5,1},{6,2},{7,3},{8,12},{9,13},{10,... | collective-permute-start | bytes 1572872 | tf_op jit(solution)/shard_map/ppermute | solution.py:243
  259.6 78.6 %reduce-scatter.5.cloned.1.call-start = ((), (), s32[]{:S(2)}) async-start(), calls=%async_computation.8 | async-start | bytes 3145728 | tf_op jit(solution)/shard_map/reduce_scatter | solution.py:382
  293.4 120.7 %reduce-scatter.7.cloned.1.call-start = ((), (), s32[]{:S(2)}) async-start(), calls=%async_computation.9 | async-start | bytes 6291456 | tf_op jit(solution)/shard_map/reduce_scatter | solution.py:382
  338.2 256.6 %reduce-scatter.9.cloned.1.call-start = ((), (), s32[]{:S(2)}) async-start(), calls=%async_computation.10 | async-start | bytes 3932160 | tf_op jit(solution)/shard_map/reduce_scatter | solution.py:382
  368.1 25.3 %collective-permute-start.30 = (bf16[128,2048]{1,0:T(8,128)(2,1)S(1)}, bf16[128,2048]{1,0:T(8,128)(2,1)S(1)}, u32[]{:S(2)}, u32[]{:S(2)}) collective-permute-start(bf16[128,2048]{1,0:T(8,128)(2,1)S(1)} %pad_maximum_fusion.14), channel_id=1, source_target_pairs={{0,4},{1,5},{2,6},{3,7},{4,0},{5,1},{6,2},{7,3},{8,12},{9,13},{10,... | collective-permute-start | bytes 1572872 | tf_op jit(solution)/shard_map/cond/branch_1_fun/ppermute | solution.py:243
  374.2 22.6 %collective-permute-start.33 = (bf16[128,2048]{1,0:T(8,128)(2,1)S(1)}, bf16[128,2048]{1,0:T(8,128)(2,1)S(1)}, u32[]{:S(2)}, u32[]{:S(2)}) collective-permute-start(bf16[128,2048]{1,0:T(8,128)(2,1)S(1)} %get-tuple-element.574), channel_id=1, source_target_pairs={{0,16},{8,24},{16,0},{24,8},{1,17},{9,25},{17,1},{25,9},{2,18},{10... | collective-permute-start | bytes 1572872 | tf_op jit(solution)/shard_map/cond/branch_1_fun/ppermute | solution.py:247
  375.8 21.3 %collective-permute-start.34 = (bf16[128,2048]{1,0:T(8,128)(2,1)S(1)}, bf16[128,2048]{1,0:T(8,128)(2,1)S(1)}, u32[]{:S(2)}, u32[]{:S(2)}) collective-permute-start(bf16[128,2048]{1,0:T(8,128)(2,1)S(1)} %get-tuple-element.573), channel_id=1, source_target_pairs={{0,8},{8,0},{16,24},{24,16},{1,9},{9,1},{17,25},{25,17},{2,10},{10... | collective-permute-start | bytes 1572872 | tf_op jit(solution)/shard_map/cond/branch_1_fun/ppermute | solution.py:247
  416.7 58.5 %collective-permute-start.71 = (bf16[512,1024]{1,0:T(8,128)(2,1)}, bf16[512,1024]{1,0:T(8,128)(2,1)}, u32[]{:S(2)}, u32[]{:S(2)}) collective-permute-start(bf16[512,1024]{1,0:T(8,128)(2,1)} %constant_dynamic-slice_fusion.4), channel_id=1, source_target_pairs={{0,4},{1,5},{2,6},{3,7},{4,0},{5,1},{6,2},{7,3},{8,12},{9,13},{10,... | collective-permute-start | bytes 3145736 | tf_op jit(solution)/shard_map/ppermute | solution.py:243
  483.1 32.0 %collective-permute-start.56 = (bf16[2,256,1024]{2,1,0:T(8,128)(2,1)}, bf16[2,256,1024]{2,1,0:T(8,128)(2,1)}, u32[]{:S(2)}, u32[]{:S(2)}) collective-permute-start(bf16[2,256,1024]{2,1,0:T(8,128)(2,1)} %pad_maximum_fusion.18), channel_id=1, source_target_pairs={{0,8},{8,0},{16,24},{24,16},{1,9},{9,1},{17,25},{25,17},{2,10},{10... | collective-permute-start | bytes 3145736 | tf_op jit(solution)/shard_map/cond/branch_1_fun/ppermute | solution.py:247
  484.0 31.1 %collective-permute-start.57 = (bf16[2,256,1024]{2,1,0:T(8,128)(2,1)}, bf16[2,256,1024]{2,1,0:T(8,128)(2,1)}, u32[]{:S(2)}, u32[]{:S(2)}) collective-permute-start(bf16[2,256,1024]{2,1,0:T(8,128)(2,1)} %collective-permute-done.52), channel_id=1, source_target_pairs={{0,16},{8,24},{16,0},{24,8},{1,17},{9,25},{17,1},{25,9},{2,18},{10... | collective-permute-start | bytes 3145736 | tf_op jit(solution)/shard_map/cond/branch_1_fun/ppermute | solution.py:247
  485.3 29.3 %collective-permute-start.53 = (bf16[128,2048]{1,0:T(8,128)(2,1)S(1)}, bf16[128,2048]{1,0:T(8,128)(2,1)}, u32[]{:S(2)}, u32[]{:S(2)}) collective-permute-start(bf16[128,2048]{1,0:T(8,128)(2,1)S(1)} %copy-done.32), channel_id=1, source_target_pairs={{0,4},{1,5},{2,6},{3,7},{4,0},{5,1},{6,2},{7,3},{8,12},{9,13},{10,... | collective-permute-start | bytes 1572872 | tf_op jit(solution)/shard_map/cond/branch_1_fun/ppermute | solution.py:243
  515.3 151.0 %reduce-scatter.11.cloned.1.call-start = ((), (), s32[]{:S(2)}) async-start(), calls=%async_computation.11 | async-start | bytes 1310720 | tf_op jit(solution)/shard_map/reduce_scatter | solution.py:382
  518.8 83.9 %collective-permute-start.74 = (bf16[4,256,1024]{2,1,0:T(8,128)(2,1)S(1)}, bf16[4,256,1024]{2,1,0:T(8,128)(2,1)}, u32[]{:S(2)}, u32[]{:S(2)}) collective-permute-start(bf16[4,256,1024]{2,1,0:T(8,128)(2,1)S(1)} %constant_dynamic-update-slice_fusion.70.refs_2_), channel_id=1, source_target_pairs={{0,8},{8,0},{16,24},{24,16},{1,9},{9,1},{17,25},{25,17},{2,10},{10... | collective-permute-start | bytes 6291464 | tf_op jit(solution)/shard_map/ppermute | solution.py:247
  524.7 78.0 %collective-permute-start.73 = (bf16[4,256,1024]{2,1,0:T(8,128)(2,1)}, bf16[4,256,1024]{2,1,0:T(8,128)(2,1)}, u32[]{:S(2)}, u32[]{:S(2)}) collective-permute-start(bf16[4,256,1024]{2,1,0:T(8,128)(2,1)} %constant_dynamic-update-slice_fusion.68.refs_0_), channel_id=1, source_target_pairs={{0,16},{8,24},{16,0},{24,8},{1,17},{9,25},{17,1},{25,9},{2,18},{10... | collective-permute-start | bytes 6291464 | tf_op jit(solution)/shard_map/ppermute | solution.py:247
  535.6 47.3 %collective-permute-start.59 = (bf16[128,2048]{1,0:T(8,128)(2,1)S(1)}, bf16[128,2048]{1,0:T(8,128)(2,1)S(1)}, u32[]{:S(2)}, u32[]{:S(2)}) collective-permute-start(bf16[128,2048]{1,0:T(8,128)(2,1)S(1)} %get-tuple-element.609), channel_id=1, source_target_pairs={{0,16},{8,24},{16,0},{24,8},{1,17},{9,25},{17,1},{25,9},{2,18},{10... | collective-permute-start | bytes 1572872 | tf_op jit(solution)/shard_map/cond/branch_1_fun/ppermute | solution.py:247
  536.3 46.5 %collective-permute-start.60 = (bf16[128,2048]{1,0:T(8,128)(2,1)S(1)}, bf16[128,2048]{1,0:T(8,128)(2,1)S(1)}, u32[]{:S(2)}, u32[]{:S(2)}) collective-permute-start(bf16[128,2048]{1,0:T(8,128)(2,1)S(1)} %get-tuple-element.608), channel_id=1, source_target_pairs={{0,8},{8,0},{16,24},{24,16},{1,9},{9,1},{17,25},{25,17},{2,10},{10... | collective-permute-start | bytes 1572872 | tf_op jit(solution)/shard_map/cond/branch_1_fun/ppermute | solution.py:247
  596.9 23.2 %collective-permute-start.72 = (bf16[1,256,768]{2,1,0:T(8,128)(2,1)}, bf16[1,256,768]{2,1,0:T(8,128)(2,1)}, u32[]{:S(2)}, u32[]{:S(2)}) collective-permute-start(bf16[1,256,768]{2,1,0:T(8,128)(2,1)} %bitcast.88), channel_id=1, source_target_pairs={{0,1},{1,0},{2,3},{3,2},{4,5},{5,4},{6,7},{7,6},{8,9},{9,8},{10,11... | collective-permute-start | bytes 1179656 | tf_op jit(solution)/shard_map/ppermute | solution.py:239
  597.1 27.2 %collective-permute-start.75 = (bf16[1,256,768]{2,1,0:T(8,128)(2,1)S(1)}, bf16[1,256,768]{2,1,0:T(8,128)(2,1)}, u32[]{:S(2)}, u32[]{:S(2)}) collective-permute-start(bf16[1,256,768]{2,1,0:T(8,128)(2,1)S(1)} %bitcast.84), channel_id=1, source_target_pairs={{0,8},{8,0},{16,24},{24,16},{1,9},{9,1},{17,25},{25,17},{2,10},{10... | collective-permute-start | bytes 1179656 | tf_op jit(solution)/shard_map/ppermute | solution.py:247
  620.1 23.3 %collective-permute-start.77 = (bf16[128,2048]{1,0:T(8,128)(2,1)S(1)}, bf16[128,2048]{1,0:T(8,128)(2,1)S(1)}, u32[]{:S(2)}, u32[]{:S(2)}) collective-permute-start(bf16[128,2048]{1,0:T(8,128)(2,1)S(1)} %get-tuple-element.457), channel_id=1, source_target_pairs={{0,8},{8,0},{16,24},{24,16},{1,9},{9,1},{17,25},{25,17},{2,10},{10... | collective-permute-start | bytes 1572872 | tf_op jit(solution)/shard_map/ppermute | solution.py:247
  621.2 22.2 %collective-permute-start.78 = (bf16[128,2048]{1,0:T(8,128)(2,1)S(1)}, bf16[128,2048]{1,0:T(8,128)(2,1)S(1)}, u32[]{:S(2)}, u32[]{:S(2)}) collective-permute-start(bf16[128,2048]{1,0:T(8,128)(2,1)S(1)} %get-tuple-element.466), channel_id=1, source_target_pairs={{0,16},{8,24},{16,0},{24,8},{1,17},{9,25},{17,1},{25,9},{2,18},{10... | collective-permute-start | bytes 1572872 | tf_op jit(solution)/shard_map/ppermute | solution.py:247
  622.2 21.2 %collective-permute-start.76 = (bf16[1,256,768]{2,1,0:T(8,128)(2,1)}, bf16[1,256,768]{2,1,0:T(8,128)(2,1)S(1)}, u32[]{:S(2)}, u32[]{:S(2)}) collective-permute-start(bf16[1,256,768]{2,1,0:T(8,128)(2,1)} %collective-permute-done.72), channel_id=1, source_target_pairs={{0,16},{8,24},{16,0},{24,8},{1,17},{9,25},{17,1},{25,9},{2,18},{10... | collective-permute-start | bytes 1179656 | tf_op jit(solution)/shard_map/ppermute | solution.py:247
  647.2 38.7 %collective-permute-start.83 = (bf16[256,2048]{1,0:T(8,128)(2,1)S(1)}, bf16[256,2048]{1,0:T(8,128)(2,1)S(1)}, u32[]{:S(2)}, u32[]{:S(2)}) collective-permute-start(bf16[256,2048]{1,0:T(8,128)(2,1)S(1)} %constant_dynamic-update-slice_fusion.76.refs_2_), channel_id=1, source_target_pairs={{0,8},{8,0},{16,24},{24,16},{1,9},{9,1},{17,25},{25,17},{2,10},{10... | collective-permute-start | bytes 3145736 | tf_op jit(solution)/shard_map/ppermute | solution.py:247
  648.0 39.9 %collective-permute-start.82 = (bf16[256,2048]{1,0:T(8,128)(2,1)S(1)}, bf16[256,2048]{1,0:T(8,128)(2,1)}, u32[]{:S(2)}, u32[]{:S(2)}) collective-permute-start(bf16[256,2048]{1,0:T(8,128)(2,1)S(1)} %constant_dynamic-update-slice_fusion.72.refs_0_), channel_id=1, source_target_pairs={{0,16},{8,24},{16,0},{24,8},{1,17},{9,25},{17,1},{25,9},{2,18},{10... | collective-permute-start | bytes 3145736 | tf_op jit(solution)/shard_map/ppermute | solution.py:247
  649.8 32.4 %collective-permute-start.81 = (bf16[128,2048]{1,0:T(8,128)(2,1)}, bf16[128,2048]{1,0:T(8,128)(2,1)}, u32[]{:S(2)}, u32[]{:S(2)}) collective-permute-start(bf16[128,2048]{1,0:T(8,128)(2,1)} %get-tuple-element.475), channel_id=1, source_target_pairs={{0,4},{1,5},{2,6},{3,7},{4,0},{5,1},{6,2},{7,3},{8,12},{9,13},{10,... | collective-permute-start | bytes 1572872 | tf_op jit(solution)/shard_map/ppermute | solution.py:243
  668.3 20.9 %collective-permute-start.85 = (bf16[32,2048]{1,0:T(8,128)(2,1)S(1)}, bf16[32,2048]{1,0:T(8,128)(2,1)}, u32[]{:S(2)}, u32[]{:S(2)}) collective-permute-start(bf16[32,2048]{1,0:T(8,128)(2,1)S(1)} %get-tuple-element.642), channel_id=1, source_target_pairs={{0,16},{8,24},{16,0},{24,8},{1,17},{9,25},{17,1},{25,9},{2,18},{10... | collective-permute-start | bytes 393224 | tf_op jit(solution)/shard_map/ppermute | solution.py:247
  (118 other events, 1190.9 us)
Sparse Core Ops, SparseCore 0:
  20.9 66.1 all-gather.4
  88.6 26.5 all-gather.6
  189.1 78.2 all-gather.8
  269.4 33.7 all-gather.10
  305.3 31.8 reduce-scatter.4
  339.4 65.5 reduce-scatter.6
  515.4 60.0 reduce-scatter.8
  602.8 26.3 reduce-scatter.10

commit v4 on v3

--- a/solution.py
+++ b/solution.py
@@ -943,12 +943,11 @@
     )
     grad_gate_up_pair = scatter_rows(grad_gate_up_term, ROW_PAIRS)
     far = add(far, swapped)
-    *flight, near, near_other, forward_far, forward_other = fence(
+    *flight, near, near_other, forward_near, near_forward_other, forward_far, forward_other = fence(
         *send_quarters(far),
         backward_part(grad_low, gate_up_w, 0),
         backward_part(grad_low, gate_up_w, 1),
-        project(token_part(hidden, 2), down),
-        project(token_part(hidden, 3), down),
+        *(project(token_part(hidden, k), down) for k in range(4)),
     )
     far = add_quarters(far, *flight)
 
@@ -982,16 +981,15 @@
 
     def gather_branch():
         block = grad_middle.astype(jnp.bfloat16)
-        forward = [project(token_part(hidden, k), down) for k in range(2)]
-        *flight, swapped = fence(*row_one(block), swap_cores(forward[1]))
+        *flight, swapped = fence(*row_one(block), swap_cores(near_forward_other))
         held, flight = row_two(block, *flight)
         flight = fence(*flight)
         own, other = row_three(held, flight)
-        forward_sum = add(forward[0], swapped)
+        forward_sum = add(forward_near, swapped)
         other, *flight = fence(other, *send_quarters(forward_sum))
         return jnp.concatenate([own, other]), add_quarters(forward_sum, *flight)
 
-    grad_branch, forward_near = window(needed, gather_branch)
+    grad_branch, forward_quarters = window(needed, gather_branch)
 
     down_own, down_send = own_rows(grad_down_pair, chunk)
     grad_branch, wide_more, down_send = fence(grad_branch, wide_more, down_send)
@@ -1004,7 +1002,7 @@
         flight = share_one(*wide_halves)
         down_more = swap_rows(down_send, 2)
         grad_mixed = attend_back(turned, mixed, grad_heads, *tables)
-        grad_mixed, *near = fence(grad_mixed, *forward_near)
+        grad_mixed, *near = fence(grad_mixed, *forward_quarters)
         grad_qkv_term = outer_sum(normed_all, grad_mixed).astype(jnp.bfloat16)
         arrived = fence(grad_qkv_term, down_more, *send_eighths(*near), *flight)
         return grad_mixed, wide_halves, arrived
@@ -1033,7 +1031,9 @@
     )
     down_halves = halves(in_order(down_own, down_more, step))
     qkv_mine, qkv_swapped = halves_of_chip((grad_qkv_rows, 0))
-    qkv_swapped, *down_halves = fence(qkv_swapped, *down_halves)
+    qkv_swapped, w_gate_up, attended, *down_halves = fence(
+        qkv_swapped, w_gate_up, attended, *down_halves
+    )
     qkv_halves = qkv_mine, qkv_swapped
     flight = *share_one(*qkv_halves), *share_one(*down_halves)
     grad_out_rows = scatter_rows(outer_sum(attended, grad_branch), ROWS)
@@ -1054,7 +1054,7 @@
     )
     out_held, out_flight = share_two(*out_halves, *flight[2:])
     output = middle + forward_next.astype(jnp.float32)
-    output = output + add_eighths(*forward_near, forward_first, forward_second)
+    output = output + add_eighths(*forward_quarters, forward_first, forward_second)
     grad_down = place_rows(shared(down_held, flight[:2]), place)
     grad_down, output, *out_flight = fence(grad_down, output, *out_flight)
     return (

time: 726 us -> 701 us (0.966)
  waiting for transfers between devices: 287 us -> 266 us
    ppermute x64, waiting for transfers between devices: 225 us -> 203 us  [swap_seq(): return lax.ppermute(values, 'seq', xor_pairs(4, offset))]
    cond x74 -> x64, local copies, waits for them, and re-layouts: 38.5 us -> 38.5 us
  transfers between devices with their start and end apart: 96 -> 96, of which waited for: 63 -> 63; matrix products, arithmetic and copies ran while one was open for 33% -> 33% of each run, Pallas kernels for 8% -> 9%
where the time goes in v4:
time: 701 us; the launch traced here: 692 us
  waiting for transfers between devices  266 us (38%)
  matrix products  102 us (15%)
  local copies, waits for them, and re-layouts  90.4 us (13%)
  starting transfers between devices  89.9 us (13%)
  Pallas kernels  68.7 us (10%)
  other arithmetic  58.9 us (8%)
  between operations  15.2 us (2%)
    ppermute x64, waiting for transfers between devices, swap_seq(): return lax.ppermute(values, 'seq', xor_pairs(4, offset))  203 us
    ppermute x64, starting transfers between devices, swap_seq(): return lax.ppermute(values, 'seq', xor_pairs(4, offset))  72.9 us
    cond x64, local copies, waits for them, and re-layouts  38.5 us
    dot_general x8, matrix products, back_product(): lax.dot_general(grad, weight, (((1,), (1,)), ((), ())), preferred_element...  35.1 us
    dot_general x4, matrix products, outer_sum(): lax.dot_general(left, right, (((0,), (0,)), ((), ())), preferred_element_...  34.3 us
    all_gather x4, waiting for transfers between devices, gather_rows(): lax.all_gather(block, 'fsdp', axis=0, tiled=True, axis_index_groups=groups)  27 us
    dot_general x7, matrix products, project(): jnp.dot(rows, weight, preferred_element_type=jnp.float32)  19.4 us
    ppermute x16, waiting for transfers between devices, swap_cores(): return lax.ppermute(values, 'fsdp', xor_pairs(8, 1))  18.1 us
  transfers between devices with their start and end apart: 96, of which 63 were waited for; matrix products, arithmetic and copies ran while one was open for 33% of the time, Pallas kernels for 9%

profile of v4, /device:TPU:0, one launch (start us, length us, event | category | flops | bytes accessed | tf_op | source)
XLA Modules:
  0.0 692.2 jit_solution(15698434836892866418)
XLA Ops:
  22.6 63.3 %conditional.10 = (bf16[1024,2048]{1,0:T(8,128)(2,1)}, bf16[512,1024]{1,0:T(8,128)(2,1)S(1)}, bf16[512,1024]{1,0:T(8,128)(2,1)}, bf16[512,2048]{1,0:T(8,128)(2,1)}, bf16[512,2048]{1,0:T(8,128)(2,1)}) conditional(s32[]{:T(128)} %convert_element_type.295, () %tuple.140, (bf16[128,2048]{1,0:T(8,128)(2,1)S(1)}, s32[3]{0:T(128)S(1)}, ...), branch_computations={%region_1.2_spmd, %region_2.3_spmd} | conditional | flops 9437185 | bytes 80480824 | solution.py:256
  57.6 7.1 %collective-permute-done.5 = bf16[64,2048]{1,0:T(8,128)(2,1)S(1)} collective-permute-done((bf16[64,2048]{1,0:T(8,128)(2,1)S(1)}, bf16[64,2048]{1,0:T(8,128)(2,1)S(1)}, u32[]{:S(2)}, u32[]{:S(2)}) %collective-permute-start.5) | collective-permute-done | bytes 262176 | tf_op jit(solution)/shard_map/cond/branch_1_fun/ppermute | solution.py:247
  67.8 10.0 %collective-permute-done.8 = bf16[128,2048]{1,0:T(8,128)(2,1)S(1)} collective-permute-done((bf16[128,2048]{1,0:T(8,128)(2,1)S(1)}, bf16[128,2048]{1,0:T(8,128)(2,1)S(1)}, u32[]{:S(2)}, u32[]{:S(2)}) %collective-permute-start.8) | collective-permute-done | bytes 524320 | tf_op jit(solution)/shard_map/cond/branch_1_fun/ppermute | solution.py:247
  88.5 18.9 %conditional.11 = (bf16[1024,768]{1,0:T(8,128)(2,1)}, bf16[1024,256]{1,0:T(8,128)(2,1)}, bf16[1024,512]{1,0:T(8,128)(2,1)}) conditional(s32[]{:T(128)} %convert_element_type.295, () %tuple.139, (bf16[1024,2048]{1,0:T(8,128)(2,1)}, bf16[2048,768]{1,0:T(8,128)(2,1)}, f32[512,128]{0,1:T(8,128)}, f32[512,128]{0,1:T(8,128)}, s32[512,1]{0,1:T(1,128)S(1)}, ...), branch_computations={%region_3.4_spmd, %region_4.5_spmd} | conditional | flops 4295753728 | bytes 13111320 | solution.py:256
  88.5 7.8 %convolution_convert_fusion.mixed_ref = bf16[1024,768]{1,0:T(8,128)(2,1)} fusion(bf16[1024,2048]{1,0:T(8,128)(2,1)} %get-tuple-element.165, bf16[2048,768]{1,0:T(8,128)(2,1)} %get-tuple-element.166), kind=kOutput, calls=%fused_computation.29 | convolution fusion | flops 3222011904 | bytes 8912896 | tf_op jit(solution)/shard_map/cond/branch_1_fun/dot_general | solution.py:793
  98.7 8.7 %attend.1 = (bf16[1024,256]{1,0:T(8,128)(2,1)}, bf16[1024,512]{1,0:T(8,128)(2,1)}) custom-call(bf16[1024,768]{1,0:T(8,128)(2,1)} %convolution_convert_fusion.mixed_ref, f32[512,128]{1,0:T(8,128)S(1)} %copy.22.cosine_ref, f32[512,128]{1,0:T(8,128)S(1)} %copy.23.sine_ref, s32[512,1]{1,0:T(8,128)S(1)} %copy.24.rows_ref, s32[1,512]{1,0:T(1,128)S(1)} %get-tuple-element.170.columns_ref), custom_call_target="tpu_custom_call" | custom-call | flops 1073741824 | bytes 3145728 | tf_op jit(solution)/shard_map/cond/branch_1_fun/attend/pallas_call | solution.py:646
  107.4 7.8 %all-gather.7.cloned.1.call-done = bf16[256,2048]{1,0:T(8,128)(2,1)} async-done(((bf16[64,2048]{1,0:T(8,128)(2,1)}), bf16[256,2048]{1,0:T(8,128)(2,1)}) %all-gather.7.cloned.1.call-update) | async-done | bytes 1048592 | tf_op jit(solution)/shard_map/all_gather | solution.py:378
  118.2 38.4 %conditional.12 = (f32[128,2048]{1,0:T(8,128)}, bf16[128,2048]{1,0:T(8,128)(2,1)}, f32[128,1]{0,1:T(1,128)}, bf16[128,2048]{1,0:T(8,128)(2,1)S(1)}) conditional(s32[]{:T(128)} %convert_element_type.295, () %tuple.138, (bf16[1024,256]{1,0:T(8,128)(2,1)}, bf16[256,2048]{1,0:T(8,128)(2,1)}, f32[128,2048]{1,0:T(8,128)}) %tuple.146), branch_computations={%region_5.6_spmd, %region_6.8_spmd} | conditional | flops 1085800576 | bytes 49809668 | solution.py:256
  128.6 11.0 %collective-permute-done.48 = bf16[128,2048]{1,0:T(8,128)(2,1)S(1)} collective-permute-done((bf16[128,2048]{1,0:T(8,128)(2,1)S(1)}, bf16[128,2048]{1,0:T(8,128)(2,1)S(1)}, u32[]{:S(2)}, u32[]{:S(2)}) %collective-permute-start.48) | collective-permute-done | bytes 524320 | tf_op jit(solution)/shard_map/cond/branch_1_fun/ppermute | solution.py:247
  157.6 27.0 %conditional.13 = (bf16[512,2048]{1,0:T(8,128)(2,1)}, bf16[512,2048]{1,0:T(8,128)(2,1)}) conditional(s32[]{:T(128)} %convert_element_type.295, () %tuple.147, bf16[128,2048]{1,0:T(8,128)(2,1)S(1)} %get-tuple-element.411), branch_computations={%region_8.9_spmd, %region_9.10_spmd} | conditional | flops 2097152 | bytes 21758168 | solution.py:256
  168.7 7.3 %collective-permute-done.24 = bf16[128,2048]{1,0:T(8,128)(2,1)S(1)} collective-permute-done((bf16[128,2048]{1,0:T(8,128)(2,1)S(1)}, bf16[128,2048]{1,0:T(8,128)(2,1)S(1)}, u32[]{:S(2)}, u32[]{:S(2)}) %collective-permute-start.24) | collective-permute-done | bytes 524320 | tf_op jit(solution)/shard_map/cond/branch_1_fun/ppermute | solution.py:247
  191.7 31.1 %conditional.14 = (bf16[2048,2048]{1,0:T(8,128)(2,1)}) conditional(s32[]{:T(128)} %convert_element_type.295, () %tuple.150, (bf16[128,2048]{1,0:T(8,128)(2,1)S(1)}, bf16[512,2048]{1,0:T(8,128)(2,1)}, bf16[512,2048]{1,0:T(8,128)(2,1)}) %tuple.151), branch_computations={%region_10.11_spmd, %region_11.12_spmd} | conditional | flops 2097152 | bytes 37748944 | solution.py:256
  223.8 31.7 %conditional.15 = (bf16[2048,2048]{1,0:T(8,128)(2,1)}) conditional(s32[]{:T(128)} %convert_element_type.295, () %tuple.149, (bf16[128,2048]{1,0:T(8,128)(2,1)S(1)}, bf16[512,2048]{1,0:T(8,128)(2,1)}, bf16[512,2048]{1,0:T(8,128)(2,1)}) %tuple.153), branch_computations={%region_12.13_spmd, %region_13.14_spmd} | conditional | flops 2097152 | bytes 37748944 | solution.py:256
  257.9 8.0 %all-gather.9.cloned.1.call-done = bf16[2048,1024]{1,0:T(8,128)(2,1)} async-done(((bf16[1024,1024]{1,0:T(8,128)(2,1)}), bf16[2048,1024]{1,0:T(8,128)(2,1)}) %all-gather.9.cloned.1.call-update) | async-done | bytes 4194320 | tf_op jit(solution)/shard_map/all_gather | solution.py:378
  265.9 13.3 %fusion.38 = f32[2048,1024]{0,1:T(8,128)S(1)} fusion(bf16[2048,2048]{1,0:T(8,128)(2,1)} %get-tuple-element.709, bf16[2048,1024]{1,0:T(8,128)(2,1)} %all-gather.9.cloned.1.call-done), kind=kOutput, calls=%fused_computation.265 | convolution fusion | flops 8589934592 | bytes 20971520 | tf_op jit(solution)/shard_map/dot_general | solution.py:920
  282.6 9.1 %convolution_convert_fusion.16 = bf16[512,2048]{1,0:T(8,128)(2,1)} fusion(bf16[2048,512]{0,1:T(8,128)(2,1)S(1)} %multiply_convert_fusion.3, bf16[2048,2048]{1,0:T(8,128)(2,1)} %get-tuple-element.710), kind=kOutput, calls=%fused_computation.192 | convolution fusion | flops 4296015872 | bytes 12582912 | tf_op jit(solution)/shard_map/dot_general | solution.py:20
  291.9 10.0 %all-gather.11.cloned.1.call-done = bf16[512,2048]{1,0:T(8,128)(2,1)} async-done(((bf16[256,2048]{1,0:T(8,128)(2,1)}), bf16[512,2048]{1,0:T(8,128)(2,1)}) %all-gather.11.cloned.1.call-update) | async-done | bytes 2097168 | tf_op jit(solution)/shard_map/all_gather | solution.py:378
  301.9 12.1 %multiply_convert_fusion.1 = (bf16[2048,512]{0,1:T(8,128)(2,1)S(1)}, bf16[2048,512]{0,1:T(8,128)(2,1)S(1)}) fusion(f32[2048,1024]{0,1:T(8,128)} %copy-done.5, bf16[2048,2048]{1,0:T(8,128)(2,1)} %get-tuple-element.710, bf16[512,2048]{1,0:T(8,128)(2,1)} %all-gather.11.cloned.1.call-done), kind=kOutput, calls=%fused_computation.178 | convolution fusion | flops 4308598784 | bytes 23068672 | tf_op jit(solution)/shard_map/dot_general | solution.py:26
  324.1 12.8 %convolution_convert_fusion.7 = bf16[2048,1024]{1,0:T(8,128)(2,1)} fusion(bf16[2048,2048]{1,0:T(8,128)(2,1)} %get-tuple-element.709, bf16[2048,512]{0,1:T(8,128)(2,1)S(1)} %get-tuple-element.626, bf16[2048,512]{0,1:T(8,128)(2,1)S(1)} %get-tuple-element.627), kind=kOutput, calls=%fused_computation.183 | convolution fusion | flops 8600420352 | bytes 16777216 | tf_op jit(solution)/shard_map/dot_general | solution.py:20
  356.3 56.3 %conditional.16 = (f32[128,2048]{1,0:T(8,128)S(1)}, bf16[128,2048]{1,0:T(8,128)(2,1)}) conditional(s32[]{:T(128)} %convert_element_type.295, () %tuple.137, (bf16[128,2048]{1,0:T(8,128)(2,1)S(1)}, f32[128,1]{0,1:T(1,128)}, f32[128,1]{0,1:T(1,128)S(1)}, bf16[512,2048]{1,0:T(8,128)(2,1)S(1)}, bf16[128,2048]{1,0:T(8,128)(2,1)S(1)}, ...), branch_computations={%region_15.16_spmd, %region_16.18_spmd} | conditional | flops 21234176 | bytes 90707536 | solution.py:256
  375.9 16.2 %collective-permute-done.30 = bf16[128,2048]{1,0:T(8,128)(2,1)S(1)} collective-permute-done((bf16[128,2048]{1,0:T(8,128)(2,1)S(1)}, bf16[128,2048]{1,0:T(8,128)(2,1)S(1)}, u32[]{:S(2)}, u32[]{:S(2)}) %collective-permute-start.30) | collective-permute-done | bytes 524320 | tf_op jit(solution)/shard_map/cond/branch_1_fun/ppermute | solution.py:243
  417.0 47.9 %conditional.17 = (bf16[1024,2048]{1,0:T(8,128)(2,1)}, f32[128,2048]{1,0:T(8,128)S(1)}, f32[128,2048]{1,0:T(8,128)}) conditional(s32[]{:T(128)} %convert_element_type.295, () %tuple.136, (f32[128,2048]{1,0:T(8,128)S(1)}, bf16[512,2048]{1,0:T(8,128)(2,1)S(1)}, bf16[512,2048]{1,0:T(8,128)(2,1)}) %tuple.290), branch_computations={%region_19.20_spmd, %region_20.21_spmd} | conditional | flops 8126464 | bytes 64487796 | solution.py:256
  429.5 10.8 %collective-permute-done.42 = bf16[128,2048]{1,0:T(8,128)(2,1)S(1)} collective-permute-done((bf16[128,2048]{1,0:T(8,128)(2,1)S(1)}, bf16[128,2048]{1,0:T(8,128)(2,1)S(1)}, u32[]{:S(2)}, u32[]{:S(2)}) %collective-permute-start.42) | collective-permute-done | bytes 524320 | tf_op jit(solution)/shard_map/cond/branch_1_fun/ppermute | solution.py:247
  448.8 13.0 %collective-permute-done.45 = bf16[128,2048]{1,0:T(8,128)(2,1)S(1)} collective-permute-done((bf16[128,2048]{1,0:T(8,128)(2,1)S(1)}, bf16[128,2048]{1,0:T(8,128)(2,1)S(1)}, u32[]{:S(2)}, u32[]{:S(2)}) %collective-permute-start.45) | collective-permute-done | bytes 524320 | tf_op jit(solution)/shard_map/cond/branch_1_fun/ppermute | solution.py:247
  465.8 38.6 %conditional.18 = (bf16[1024,768]{1,0:T(8,128)(2,1)}, bf16[2,256,1024]{2,1,0:T(8,128)(2,1)}, bf16[2,256,1024]{2,1,0:T(8,128)(2,1)}, bf16[2048,768]{0,1:T(8,128)(...) conditional(s32[]{:T(128)} %convert_element_type.295, ...), branch_computations={%region_21.22_spmd, %region_22.23_spmd} | conditional | flops 6982467584 | bytes 49812020 | solution.py:256
  479.6 12.4 %attend_back.1 = bf16[1024,768]{1,0:T(8,128)(2,1)} custom-call(bf16[1024,512]{1,0:T(8,128)(2,1)} %get-tuple-element.236.turned_ref, bf16[1024,768]{1,0:T(8,128)(2,1)} %get-tuple-element.237.values_ref, bf16[1024,256]{1,0:T(8,128)(2,1)S(1)} %convolution_convert_fusion.4.grad_ref, f32[512,128]{1,0:T(8,128)S(1)} %copy.25.cosine_ref, ...), custom_call_target="tpu_custom_call" | custom-call | flops 2684354560 | bytes 4194304 | tf_op jit(solution)/shard_map/cond/branch_1_fun/attend_back/pallas_call | solution.py:714
  494.9 7.8 %fusion.8 = bf16[2048,768]{0,1:T(8,128)(2,1)} fusion(bf16[1024,768]{1,0:T(8,128)(2,1)} %attend_back.1, bf16[1024,2048]{1,0:T(8,128)(2,1)} %get-tuple-element.254), kind=kOutput, calls=%fused_computation.142 | convolution fusion | flops 3222798336 | bytes 8912896 | tf_op jit(solution)/shard_map/cond/branch_1_fun/dot_general | solution.py:20
  515.2 68.7 %conditional.19 = (f32[128,2048]{1,0:T(8,128)}) conditional(s32[]{:T(128)} %convert_element_type.295, () %tuple.164, (f32[128]{0:T(128)S(1)}, f32[128,1]{0,1:T(1,128)S(1)}, bf16[1024,768]{1,0:T(8,128)(2,1)}, bf16[2048,768]{1,0:T(8,128)(2,1)}, f32[128,2048]{1,0:T(8,128)S(1)}, /*index=5*/f32[128,2048]{1,0:T(8,128)}) %tuple.288), branch_computations={%region_24.25_spmd, %region_25.27_spmd} | conditional | flops 3231973888 | bytes 61871340 | solution.py:256
  526.1 45.9 %collective-permute-done.59 = bf16[128,2048]{1,0:T(8,128)(2,1)S(1)} collective-permute-done((bf16[128,2048]{1,0:T(8,128)(2,1)S(1)}, bf16[128,2048]{1,0:T(8,128)(2,1)S(1)}, u32[]{:S(2)}, u32[]{:S(2)}) %collective-permute-start.59) | collective-permute-done | bytes 524320 | tf_op jit(solution)/shard_map/cond/branch_1_fun/ppermute | solution.py:247
  599.1 15.8 %merge_wide.1 = (f32[256,16384]{1,0:T(8,128)}, f32[4,256,128]{2,1,0:T(8,128)S(1)}) custom-call(s32[3]{0:T(128)S(1)} %copy-done.33, bf16[4,256,1024]{2,1,0:T(8,128)(2,1)} %constant_dynamic-update-slice_fusion.68.refs_0_, bf16[4,256,1024]{2,1,0:T(8,128)(2,1)} %collective-permute-done.73.refs_1_, ...), custom_call_target="tpu_custom_call" | custom-call | tf_op jit(solution)/shard_map/merge_wide/pallas_call | solution.py:504
  627.3 11.6 %collective-permute-done.80.refs_3_ = bf16[2,256,768]{2,1,0:T(8,128)(2,1)S(1)} collective-permute-done((bf16[2,256,768]{2,1,0:T(8,128)(2,1)S(1)}, bf16[2,256,768]{2,1,0:T(8,128)(2,1)S(1)}, u32[]{:S(2)}, u32[]{:S(2)}) %collective-permute-start.80) | collective-permute-done | bytes 786464 | tf_op jit(solution)/shard_map/ppermute | solution.py:247
  648.5 9.0 %merge_heads.1 = (f32[256,6144]{1,0:T(8,128)}, f32[2,256,128]{2,1,0:T(8,128)}) custom-call(s32[3]{0:T(128)S(1)} %copy-done.33, bf16[2,256,768]{2,1,0:T(8,128)(2,1)} %copy-done.16, bf16[2,256,768]{2,1,0:T(8,128)(2,1)} %collective-permute-done.79.refs_1_, bf16[2,256,768]{2,1,0:T(8,128)(2,1)} %copy-done.24, bf16[2,256,768]{2,1,0:T(8,128)(2,1)} %copy-done.27, ...), custom_call_target="tpu_custom_call" | custom-call | tf_op jit(solution)/shard_map/merge_heads/pallas_call | solution.py:571
  (500 shorter events, 408.8 us)
Async XLA Ops:
  7.2 79.9 %all-gather.5.cloned.1.call-start = ((), (), s32[]{:S(2)}) async-start(), calls=%async_computation.4 | async-start | bytes 3932160 | tf_op jit(solution)/shard_map/all_gather | solution.py:378
  20.8 94.5 %all-gather.7.cloned.1.call-start = ((), (), s32[]{:S(2)}) async-start(), calls=%async_computation.5 | async-start | bytes 1310720 | tf_op jit(solution)/shard_map/all_gather | solution.py:378
  21.6 244.3 %all-gather.9.cloned.1.call-start = ((), (), s32[]{:S(2)}) async-start(), calls=%async_computation.6 | async-start | bytes 6291456 | tf_op jit(solution)/shard_map/all_gather | solution.py:378
  115.2 70.8 %collective-permute-start.64 = (bf16[512,1024]{1,0:T(8,128)(2,1)}, bf16[512,1024]{1,0:T(8,128)(2,1)S(1)}, u32[]{:S(2)}, u32[]{:S(2)}) collective-permute-start(bf16[512,1024]{1,0:T(8,128)(2,1)} %get-tuple-element.408), channel_id=1, source_target_pairs={{0,4},{1,5},{2,6},{3,7},{4,0},{5,1},{6,2},{7,3},{8,12},{9,13},{10,... | collective-permute-start | bytes 3145736 | tf_op jit(solution)/shard_map/ppermute | solution.py:243
  156.6 29.5 %collective-permute-start.65 = (bf16[128,2048]{1,0:T(8,128)(2,1)}, bf16[128,2048]{1,0:T(8,128)(2,1)S(1)}, u32[]{:S(2)}, u32[]{:S(2)}) collective-permute-start(bf16[128,2048]{1,0:T(8,128)(2,1)} %get-tuple-element.409), channel_id=1, source_target_pairs={{0,4},{1,5},{2,6},{3,7},{4,0},{5,1},{6,2},{7,3},{8,12},{9,13},{10,... | collective-permute-start | bytes 1572872 | tf_op jit(solution)/shard_map/ppermute | solution.py:243
  187.7 114.2 %all-gather.11.cloned.1.call-start = ((), (), s32[]{:S(2)}) async-start(), calls=%async_computation.7 | async-start | bytes 3145728 | tf_op jit(solution)/shard_map/all_gather | solution.py:378
  188.7 35.1 %collective-permute-start.67 = (bf16[128,2048]{1,0:T(8,128)(2,1)S(1)}, bf16[128,2048]{1,0:T(8,128)(2,1)S(1)}, u32[]{:S(2)}, u32[]{:S(2)}) collective-permute-start(bf16[128,2048]{1,0:T(8,128)(2,1)S(1)} %bitcast.82), channel_id=1, source_target_pairs={{0,4},{1,5},{2,6},{3,7},{4,0},{5,1},{6,2},{7,3},{8,12},{9,13},{10,... | collective-permute-start | bytes 1572872 | tf_op jit(solution)/shard_map/ppermute | solution.py:243
  190.3 65.2 %collective-permute-start.66 = (bf16[128,2048]{1,0:T(8,128)(2,1)S(1)}, bf16[128,2048]{1,0:T(8,128)(2,1)S(1)}, u32[]{:S(2)}, u32[]{:S(2)}) collective-permute-start(bf16[128,2048]{1,0:T(8,128)(2,1)S(1)} %constant_dynamic-slice_fusion.5), channel_id=1, source_target_pairs={{0,4},{1,5},{2,6},{3,7},{4,0},{5,1},{6,2},{7,3},{8,12},{9,13},{10,... | collective-permute-start | bytes 1572872 | tf_op jit(solution)/shard_map/ppermute | solution.py:243
  257.8 79.1 %reduce-scatter.5.cloned.1.call-start = ((), (), s32[]{:S(2)}) async-start(), calls=%async_computation.8 | async-start | bytes 3145728 | tf_op jit(solution)/shard_map/reduce_scatter | solution.py:382
  291.7 121.0 %reduce-scatter.7.cloned.1.call-start = ((), (), s32[]{:S(2)}) async-start(), calls=%async_computation.9 | async-start | bytes 6291456 | tf_op jit(solution)/shard_map/reduce_scatter | solution.py:382
  336.9 247.0 %reduce-scatter.9.cloned.1.call-start = ((), (), s32[]{:S(2)}) async-start(), calls=%async_computation.10 | async-start | bytes 3932160 | tf_op jit(solution)/shard_map/reduce_scatter | solution.py:382
  366.8 25.3 %collective-permute-start.30 = (bf16[128,2048]{1,0:T(8,128)(2,1)S(1)}, bf16[128,2048]{1,0:T(8,128)(2,1)S(1)}, u32[]{:S(2)}, u32[]{:S(2)}) collective-permute-start(bf16[128,2048]{1,0:T(8,128)(2,1)S(1)} %pad_maximum_fusion.14), channel_id=1, source_target_pairs={{0,4},{1,5},{2,6},{3,7},{4,0},{5,1},{6,2},{7,3},{8,12},{9,13},{10,... | collective-permute-start | bytes 1572872 | tf_op jit(solution)/shard_map/cond/branch_1_fun/ppermute | solution.py:243
  373.1 22.3 %collective-permute-start.33 = (bf16[128,2048]{1,0:T(8,128)(2,1)S(1)}, bf16[128,2048]{1,0:T(8,128)(2,1)S(1)}, u32[]{:S(2)}, u32[]{:S(2)}) collective-permute-start(bf16[128,2048]{1,0:T(8,128)(2,1)S(1)} %get-tuple-element.576), channel_id=1, source_target_pairs={{0,16},{8,24},{16,0},{24,8},{1,17},{9,25},{17,1},{25,9},{2,18},{10... | collective-permute-start | bytes 1572872 | tf_op jit(solution)/shard_map/cond/branch_1_fun/ppermute | solution.py:247
  374.7 21.1 %collective-permute-start.34 = (bf16[128,2048]{1,0:T(8,128)(2,1)S(1)}, bf16[128,2048]{1,0:T(8,128)(2,1)S(1)}, u32[]{:S(2)}, u32[]{:S(2)}) collective-permute-start(bf16[128,2048]{1,0:T(8,128)(2,1)S(1)} %get-tuple-element.575), channel_id=1, source_target_pairs={{0,8},{8,0},{16,24},{24,16},{1,9},{9,1},{17,25},{25,17},{2,10},{10... | collective-permute-start | bytes 1572872 | tf_op jit(solution)/shard_map/cond/branch_1_fun/ppermute | solution.py:247
  414.4 50.4 %collective-permute-start.71 = (bf16[512,1024]{1,0:T(8,128)(2,1)S(1)}, bf16[512,1024]{1,0:T(8,128)(2,1)}, u32[]{:S(2)}, u32[]{:S(2)}) collective-permute-start(bf16[512,1024]{1,0:T(8,128)(2,1)S(1)} %constant_dynamic-slice_fusion.4), channel_id=1, source_target_pairs={{0,4},{1,5},{2,6},{3,7},{4,0},{5,1},{6,2},{7,3},{8,12},{9,13},{10,... | collective-permute-start | bytes 3145736 | tf_op jit(solution)/shard_map/ppermute | solution.py:243
  472.4 32.0 %collective-permute-start.56 = (bf16[2,256,1024]{2,1,0:T(8,128)(2,1)}, bf16[2,256,1024]{2,1,0:T(8,128)(2,1)}, u32[]{:S(2)}, u32[]{:S(2)}) collective-permute-start(bf16[2,256,1024]{2,1,0:T(8,128)(2,1)} %pad_maximum_fusion.18), channel_id=1, source_target_pairs={{0,8},{8,0},{16,24},{24,16},{1,9},{9,1},{17,25},{25,17},{2,10},{10... | collective-permute-start | bytes 3145736 | tf_op jit(solution)/shard_map/cond/branch_1_fun/ppermute | solution.py:247
  473.2 31.1 %collective-permute-start.57 = (bf16[2,256,1024]{2,1,0:T(8,128)(2,1)}, bf16[2,256,1024]{2,1,0:T(8,128)(2,1)}, u32[]{:S(2)}, u32[]{:S(2)}) collective-permute-start(bf16[2,256,1024]{2,1,0:T(8,128)(2,1)} %collective-permute-done.52), channel_id=1, source_target_pairs={{0,16},{8,24},{16,0},{24,8},{1,17},{9,25},{17,1},{25,9},{2,18},{10... | collective-permute-start | bytes 3145736 | tf_op jit(solution)/shard_map/cond/branch_1_fun/ppermute | solution.py:247
  474.7 28.0 %collective-permute-start.53 = (bf16[128,2048]{1,0:T(8,128)(2,1)S(1)}, bf16[128,2048]{1,0:T(8,128)(2,1)}, u32[]{:S(2)}, u32[]{:S(2)}) collective-permute-start(bf16[128,2048]{1,0:T(8,128)(2,1)S(1)} %copy-done.28), channel_id=1, source_target_pairs={{0,4},{1,5},{2,6},{3,7},{4,0},{5,1},{6,2},{7,3},{8,12},{9,13},{10,... | collective-permute-start | bytes 1572872 | tf_op jit(solution)/shard_map/cond/branch_1_fun/ppermute | solution.py:243
  504.5 136.9 %reduce-scatter.11.cloned.1.call-start = ((), (), s32[]{:S(2)}) async-start(), calls=%async_computation.11 | async-start | bytes 1310720 | tf_op jit(solution)/shard_map/reduce_scatter | solution.py:382
  507.9 89.5 %collective-permute-start.74 = (bf16[4,256,1024]{2,1,0:T(8,128)(2,1)S(1)}, bf16[4,256,1024]{2,1,0:T(8,128)(2,1)}, u32[]{:S(2)}, u32[]{:S(2)}) collective-permute-start(bf16[4,256,1024]{2,1,0:T(8,128)(2,1)S(1)} %constant_dynamic-update-slice_fusion.70.refs_2_), channel_id=1, source_target_pairs={{0,8},{8,0},{16,24},{24,16},{1,9},{9,1},{17,25},{25,17},{2,10},{10... | collective-permute-start | bytes 6291464 | tf_op jit(solution)/shard_map/ppermute | solution.py:247
  513.8 85.2 %collective-permute-start.73 = (bf16[4,256,1024]{2,1,0:T(8,128)(2,1)}, bf16[4,256,1024]{2,1,0:T(8,128)(2,1)}, u32[]{:S(2)}, u32[]{:S(2)}) collective-permute-start(bf16[4,256,1024]{2,1,0:T(8,128)(2,1)} %constant_dynamic-update-slice_fusion.68.refs_0_), channel_id=1, source_target_pairs={{0,16},{8,24},{16,0},{24,8},{1,17},{9,25},{17,1},{25,9},{2,18},{10... | collective-permute-start | bytes 6291464 | tf_op jit(solution)/shard_map/ppermute | solution.py:247
  524.6 47.5 %collective-permute-start.59 = (bf16[128,2048]{1,0:T(8,128)(2,1)S(1)}, bf16[128,2048]{1,0:T(8,128)(2,1)S(1)}, u32[]{:S(2)}, u32[]{:S(2)}) collective-permute-start(bf16[128,2048]{1,0:T(8,128)(2,1)S(1)} %get-tuple-element.611), channel_id=1, source_target_pairs={{0,16},{8,24},{16,0},{24,8},{1,17},{9,25},{17,1},{25,9},{2,18},{10... | collective-permute-start | bytes 1572872 | tf_op jit(solution)/shard_map/cond/branch_1_fun/ppermute | solution.py:247
  525.3 46.8 %collective-permute-start.60 = (bf16[128,2048]{1,0:T(8,128)(2,1)S(1)}, bf16[128,2048]{1,0:T(8,128)(2,1)S(1)}, u32[]{:S(2)}, u32[]{:S(2)}) collective-permute-start(bf16[128,2048]{1,0:T(8,128)(2,1)S(1)} %get-tuple-element.610), channel_id=1, source_target_pairs={{0,8},{8,0},{16,24},{24,16},{1,9},{9,1},{17,25},{25,17},{2,10},{10... | collective-permute-start | bytes 1572872 | tf_op jit(solution)/shard_map/cond/branch_1_fun/ppermute | solution.py:247
  593.9 23.3 %collective-permute-start.75 = (bf16[1,256,768]{2,1,0:T(8,128)(2,1)}, bf16[1,256,768]{2,1,0:T(8,128)(2,1)S(1)}, u32[]{:S(2)}, u32[]{:S(2)}) collective-permute-start(bf16[1,256,768]{2,1,0:T(8,128)(2,1)} %bitcast.26), channel_id=1, source_target_pairs={{0,8},{8,0},{16,24},{24,16},{1,9},{9,1},{17,25},{25,17},{2,10},{10... | collective-permute-start | bytes 1179656 | tf_op jit(solution)/shard_map/ppermute | solution.py:247
  595.1 23.3 %collective-permute-start.77 = (bf16[128,2048]{1,0:T(8,128)(2,1)}, bf16[128,2048]{1,0:T(8,128)(2,1)S(1)}, u32[]{:S(2)}, u32[]{:S(2)}) collective-permute-start(bf16[128,2048]{1,0:T(8,128)(2,1)} %get-tuple-element.465), channel_id=1, source_target_pairs={{0,8},{8,0},{16,24},{24,16},{1,9},{9,1},{17,25},{25,17},{2,10},{10... | collective-permute-start | bytes 1572872 | tf_op jit(solution)/shard_map/ppermute | solution.py:247
  595.9 22.4 %collective-permute-start.78 = (bf16[128,2048]{1,0:T(8,128)(2,1)}, bf16[128,2048]{1,0:T(8,128)(2,1)S(1)}, u32[]{:S(2)}, u32[]{:S(2)}) collective-permute-start(bf16[128,2048]{1,0:T(8,128)(2,1)} %get-tuple-element.474), channel_id=1, source_target_pairs={{0,16},{8,24},{16,0},{24,8},{1,17},{9,25},{17,1},{25,9},{2,18},{10... | collective-permute-start | bytes 1572872 | tf_op jit(solution)/shard_map/ppermute | solution.py:247
  597.4 21.0 %collective-permute-start.76 = (bf16[1,256,768]{2,1,0:T(8,128)(2,1)}, bf16[1,256,768]{2,1,0:T(8,128)(2,1)S(1)}, u32[]{:S(2)}, u32[]{:S(2)}) collective-permute-start(bf16[1,256,768]{2,1,0:T(8,128)(2,1)} %collective-permute-done.72), channel_id=1, source_target_pairs={{0,16},{8,24},{16,0},{24,8},{1,17},{9,25},{17,1},{25,9},{2,18},{10... | collective-permute-start | bytes 1179656 | tf_op jit(solution)/shard_map/ppermute | solution.py:247
  622.4 38.6 %collective-permute-start.83 = (bf16[256,2048]{1,0:T(8,128)(2,1)S(1)}, bf16[256,2048]{1,0:T(8,128)(2,1)S(1)}, u32[]{:S(2)}, u32[]{:S(2)}) collective-permute-start(bf16[256,2048]{1,0:T(8,128)(2,1)S(1)} %constant_dynamic-update-slice_fusion.76.refs_2_), channel_id=1, source_target_pairs={{0,8},{8,0},{16,24},{24,16},{1,9},{9,1},{17,25},{25,17},{2,10},{10... | collective-permute-start | bytes 3145736 | tf_op jit(solution)/shard_map/ppermute | solution.py:247
  623.3 39.9 %collective-permute-start.82 = (bf16[256,2048]{1,0:T(8,128)(2,1)S(1)}, bf16[256,2048]{1,0:T(8,128)(2,1)}, u32[]{:S(2)}, u32[]{:S(2)}) collective-permute-start(bf16[256,2048]{1,0:T(8,128)(2,1)S(1)} %constant_dynamic-update-slice_fusion.72.refs_0_), channel_id=1, source_target_pairs={{0,16},{8,24},{16,0},{24,8},{1,17},{9,25},{17,1},{25,9},{2,18},{10... | collective-permute-start | bytes 3145736 | tf_op jit(solution)/shard_map/ppermute | solution.py:247
  624.8 32.7 %collective-permute-start.81 = (bf16[128,2048]{1,0:T(8,128)(2,1)}, bf16[128,2048]{1,0:T(8,128)(2,1)}, u32[]{:S(2)}, u32[]{:S(2)}) collective-permute-start(bf16[128,2048]{1,0:T(8,128)(2,1)} %get-tuple-element.483), channel_id=1, source_target_pairs={{0,4},{1,5},{2,6},{3,7},{4,0},{5,1},{6,2},{7,3},{8,12},{9,13},{10,... | collective-permute-start | bytes 1572872 | tf_op jit(solution)/shard_map/ppermute | solution.py:243
  642.4 20.8 %collective-permute-start.84 = (bf16[32,2048]{1,0:T(8,128)(2,1)S(1)}, bf16[32,2048]{1,0:T(8,128)(2,1)S(1)}, u32[]{:S(2)}, u32[]{:S(2)}) collective-permute-start(bf16[32,2048]{1,0:T(8,128)(2,1)S(1)} %get-tuple-element.645), channel_id=1, source_target_pairs={{0,8},{8,0},{16,24},{24,16},{1,9},{9,1},{17,25},{25,17},{2,10},{10... | collective-permute-start | bytes 393224 | tf_op jit(solution)/shard_map/ppermute | solution.py:247
  643.3 21.2 %collective-permute-start.85 = (bf16[32,2048]{1,0:T(8,128)(2,1)S(1)}, bf16[32,2048]{1,0:T(8,128)(2,1)}, u32[]{:S(2)}, u32[]{:S(2)}) collective-permute-start(bf16[32,2048]{1,0:T(8,128)(2,1)S(1)} %get-tuple-element.644), channel_id=1, source_target_pairs={{0,16},{8,24},{16,0},{24,8},{1,17},{9,25},{17,1},{25,9},{2,18},{10... | collective-permute-start | bytes 393224 | tf_op jit(solution)/shard_map/ppermute | solution.py:247
  (114 other events, 1158.2 us)
Sparse Core Ops, SparseCore 0:
  20.9 66.1 all-gather.4
  88.6 26.5 all-gather.6
  187.8 78.0 all-gather.8
  267.9 33.9 all-gather.10
  304.0 31.8 reduce-scatter.4
  338.1 65.5 reduce-scatter.6
  504.6 60.0 reduce-scatter.8
  592.9 27.1 reduce-scatter.10

commit v5 on v4

--- a/solution.py
+++ b/solution.py
@@ -821,9 +821,8 @@
         return of_core(own_core), swap_cores(of_core(1 - own_core))
 
     factor_one = lax.rsqrt(jnp.mean(inputs * inputs, axis=-1, keepdims=True) + EPSILON)
-    normed, qkv_own, qkv_other = fence(
-        (inputs * factor_one).astype(jnp.bfloat16), *slice_heads(w_qkv, gain_one, place, heads)
-    )
+    normed = (inputs * factor_one).astype(jnp.bfloat16)
+    qkv_own, qkv_other = slice_heads(w_qkv, gain_one, place, heads)
     normed, qkv_chip, w_out, w_down = fence(
         normed, in_order(qkv_own, swap_cores(qkv_other), own_core), w_out, w_down
     )

time: 701 us -> 701 us (level)
    cond x64 -> x62, local copies, waits for them, and re-layouts: 38.5 us -> 38.8 us
    unnamed x87 -> x89, local copies, waits for them, and re-layouts: 14.3 us -> 14.5 us
  transfers between devices with their start and end apart: 96 -> 96, of which waited for: 63 -> 60; matrix products, arithmetic and copies ran while one was open for 33% -> 34% of each run, Pallas kernels for 9% -> 9%
where the time goes in v5:
time: 701 us; the launch traced here: 692 us
  waiting for transfers between devices  265 us (38%)
  matrix products  102 us (15%)
  local copies, waits for them, and re-layouts  92.9 us (13%)
  starting transfers between devices  86.2 us (12%)
  Pallas kernels  68.8 us (10%)
  other arithmetic  61.4 us (9%)
  between operations  15.2 us (2%)
    ppermute x64, waiting for transfers between devices, swap_seq(): return lax.ppermute(values, 'seq', xor_pairs(4, offset))  207 us
    ppermute x64, starting transfers between devices, swap_seq(): return lax.ppermute(values, 'seq', xor_pairs(4, offset))  69.2 us
    cond x62, local copies, waits for them, and re-layouts  38.8 us
    dot_general x8, matrix products, back_product(): lax.dot_general(grad, weight, (((1,), (1,)), ((), ())), preferred_element...  35.1 us
    dot_general x4, matrix products, outer_sum(): lax.dot_general(left, right, (((0,), (0,)), ((), ())), preferred_element_...  34.3 us
    all_gather x4, waiting for transfers between devices, gather_rows(): lax.all_gather(block, 'fsdp', axis=0, tiled=True, axis_index_groups=groups)  22.2 us
    dot_general x7, matrix products, project(): jnp.dot(rows, weight, preferred_element_type=jnp.float32)  19.3 us
    ppermute x8, waiting for transfers between devices, swap_rows(): return lax.ppermute(values, 'fsdp', xor_pairs(8, 2 * offset))  17.8 us
  transfers between devices with their start and end apart: 96, of which 60 were waited for; matrix products, arithmetic and copies ran while one was open for 34% of the time, Pallas kernels for 9%

profile of v5, /device:TPU:0, one launch (start us, length us, event | category | flops | bytes accessed | tf_op | source)
XLA Modules:
  0.0 691.9 jit_solution(11456155651796097257)
XLA Ops:
  20.1 65.7 %conditional.10 = (bf16[1024,2048]{1,0:T(8,128)(2,1)}, bf16[512,1024]{1,0:T(8,128)(2,1)S(1)}, bf16[512,1024]{1,0:T(8,128)(2,1)}, bf16[512,2048]{1,0:T(8,128)(2,1)}, bf16[512,2048]{1,0:T(8,128)(2,1)}) conditional(s32[]{:T(128)} %convert_element_type.295, () %tuple.139, (bf16[128,2048]{1,0:T(8,128)(2,1)S(1)}, s32[3]{0:T(128)S(1)}, ...), branch_computations={%region_1.2_spmd, %region_2.3_spmd} | conditional | flops 9437185 | bytes 84675160 | solution.py:256
  36.4 6.9 slice_wide.1
  55.9 7.1 %collective-permute-done.5 = bf16[64,2048]{1,0:T(8,128)(2,1)S(1)} collective-permute-done((bf16[64,2048]{1,0:T(8,128)(2,1)S(1)}, bf16[64,2048]{1,0:T(8,128)(2,1)S(1)}, u32[]{:S(2)}, u32[]{:S(2)}) %collective-permute-start.5) | collective-permute-done | bytes 262176 | tf_op jit(solution)/shard_map/cond/branch_1_fun/ppermute | solution.py:247
  66.5 9.7 %collective-permute-done.8 = bf16[128,2048]{1,0:T(8,128)(2,1)S(1)} collective-permute-done((bf16[128,2048]{1,0:T(8,128)(2,1)S(1)}, bf16[128,2048]{1,0:T(8,128)(2,1)S(1)}, u32[]{:S(2)}, u32[]{:S(2)}) %collective-permute-start.8) | collective-permute-done | bytes 524320 | tf_op jit(solution)/shard_map/cond/branch_1_fun/ppermute | solution.py:247
  88.2 18.9 %conditional.11 = (bf16[1024,768]{1,0:T(8,128)(2,1)}, bf16[1024,256]{1,0:T(8,128)(2,1)}, bf16[1024,512]{1,0:T(8,128)(2,1)}) conditional(s32[]{:T(128)} %convert_element_type.295, () %tuple.138, (bf16[1024,2048]{1,0:T(8,128)(2,1)}, bf16[2048,768]{1,0:T(8,128)(2,1)}, f32[512,128]{0,1:T(8,128)}, f32[512,128]{0,1:T(8,128)}, s32[512,1]{0,1:T(1,128)S(1)}, ...), branch_computations={%region_3.4_spmd, %region_4.5_spmd} | conditional | flops 4295753728 | bytes 13111320 | solution.py:256
  88.2 7.8 %convolution_convert_fusion.mixed_ref = bf16[1024,768]{1,0:T(8,128)(2,1)} fusion(bf16[1024,2048]{1,0:T(8,128)(2,1)} %get-tuple-element.165, bf16[2048,768]{1,0:T(8,128)(2,1)} %get-tuple-element.166), kind=kOutput, calls=%fused_computation.29 | convolution fusion | flops 3222011904 | bytes 8912896 | tf_op jit(solution)/shard_map/cond/branch_1_fun/dot_general | solution.py:793
  98.3 8.7 %attend.1 = (bf16[1024,256]{1,0:T(8,128)(2,1)}, bf16[1024,512]{1,0:T(8,128)(2,1)}) custom-call(bf16[1024,768]{1,0:T(8,128)(2,1)} %convolution_convert_fusion.mixed_ref, f32[512,128]{1,0:T(8,128)S(1)} %copy.22.cosine_ref, f32[512,128]{1,0:T(8,128)S(1)} %copy.23.sine_ref, s32[512,1]{1,0:T(8,128)S(1)} %copy.24.rows_ref, s32[1,512]{1,0:T(1,128)S(1)} %get-tuple-element.170.columns_ref), custom_call_target="tpu_custom_call" | custom-call | flops 1073741824 | bytes 3145728 | tf_op jit(solution)/shard_map/cond/branch_1_fun/attend/pallas_call | solution.py:646
  115.3 38.5 %conditional.12 = (f32[128,2048]{1,0:T(8,128)}, bf16[128,2048]{1,0:T(8,128)(2,1)}, f32[128,1]{0,1:T(1,128)}, bf16[128,2048]{1,0:T(8,128)(2,1)S(1)}) conditional(s32[]{:T(128)} %convert_element_type.295, () %tuple.137, (bf16[1024,256]{1,0:T(8,128)(2,1)}, bf16[256,2048]{1,0:T(8,128)(2,1)}, f32[128,2048]{1,0:T(8,128)}) %tuple.144), branch_computations={%region_5.6_spmd, %region_6.8_spmd} | conditional | flops 1085800576 | bytes 49809668 | solution.py:256
  125.7 11.0 %collective-permute-done.48 = bf16[128,2048]{1,0:T(8,128)(2,1)S(1)} collective-permute-done((bf16[128,2048]{1,0:T(8,128)(2,1)S(1)}, bf16[128,2048]{1,0:T(8,128)(2,1)S(1)}, u32[]{:S(2)}, u32[]{:S(2)}) %collective-permute-start.48) | collective-permute-done | bytes 524320 | tf_op jit(solution)/shard_map/cond/branch_1_fun/ppermute | solution.py:247
  155.0 27.2 %conditional.13 = (bf16[512,2048]{1,0:T(8,128)(2,1)}, bf16[512,2048]{1,0:T(8,128)(2,1)}) conditional(s32[]{:T(128)} %convert_element_type.295, () %tuple.145, bf16[128,2048]{1,0:T(8,128)(2,1)S(1)} %get-tuple-element.405), branch_computations={%region_8.9_spmd, %region_9.10_spmd} | conditional | flops 2097152 | bytes 21758168 | solution.py:256
  165.9 7.5 %collective-permute-done.24 = bf16[128,2048]{1,0:T(8,128)(2,1)S(1)} collective-permute-done((bf16[128,2048]{1,0:T(8,128)(2,1)S(1)}, bf16[128,2048]{1,0:T(8,128)(2,1)S(1)}, u32[]{:S(2)}, u32[]{:S(2)}) %collective-permute-start.24) | collective-permute-done | bytes 524320 | tf_op jit(solution)/shard_map/cond/branch_1_fun/ppermute | solution.py:247
  189.2 30.9 %conditional.14 = (bf16[2048,2048]{1,0:T(8,128)(2,1)}) conditional(s32[]{:T(128)} %convert_element_type.295, () %tuple.148, (bf16[128,2048]{1,0:T(8,128)(2,1)S(1)}, bf16[512,2048]{1,0:T(8,128)(2,1)}, bf16[512,2048]{1,0:T(8,128)(2,1)}) %tuple.149), branch_computations={%region_10.11_spmd, %region_11.12_spmd} | conditional | flops 2097152 | bytes 37748944 | solution.py:256
  222.0 31.1 %conditional.15 = (bf16[2048,2048]{1,0:T(8,128)(2,1)}) conditional(s32[]{:T(128)} %convert_element_type.295, () %tuple.147, (bf16[128,2048]{1,0:T(8,128)(2,1)S(1)}, bf16[512,2048]{1,0:T(8,128)(2,1)}, bf16[512,2048]{1,0:T(8,128)(2,1)}) %tuple.151), branch_computations={%region_12.13_spmd, %region_13.14_spmd} | conditional | flops 2097152 | bytes 37748944 | solution.py:256
  255.7 8.7 %all-gather.9.cloned.1.call-done = bf16[2048,1024]{1,0:T(8,128)(2,1)} async-done(((bf16[1024,1024]{1,0:T(8,128)(2,1)}), bf16[2048,1024]{1,0:T(8,128)(2,1)}) %all-gather.9.cloned.1.call-update) | async-done | bytes 4194320 | tf_op jit(solution)/shard_map/all_gather | solution.py:378
  264.4 13.3 %fusion.38 = f32[2048,1024]{0,1:T(8,128)S(1)} fusion(bf16[2048,2048]{1,0:T(8,128)(2,1)} %get-tuple-element.703, bf16[2048,1024]{1,0:T(8,128)(2,1)} %all-gather.9.cloned.1.call-done), kind=kOutput, calls=%fused_computation.265 | convolution fusion | flops 8589934592 | bytes 20971520 | tf_op jit(solution)/shard_map/dot_general | solution.py:919
  282.4 9.2 %convolution_convert_fusion.16 = bf16[512,2048]{1,0:T(8,128)(2,1)} fusion(bf16[2048,512]{0,1:T(8,128)(2,1)S(1)} %multiply_convert_fusion.3, bf16[2048,2048]{1,0:T(8,128)(2,1)} %get-tuple-element.704), kind=kOutput, calls=%fused_computation.192 | convolution fusion | flops 4296015872 | bytes 12582912 | tf_op jit(solution)/shard_map/dot_general | solution.py:20
  291.9 8.2 %all-gather.11.cloned.1.call-done = bf16[512,2048]{1,0:T(8,128)(2,1)} async-done(((bf16[256,2048]{1,0:T(8,128)(2,1)}), bf16[512,2048]{1,0:T(8,128)(2,1)}) %all-gather.11.cloned.1.call-update) | async-done | bytes 2097168 | tf_op jit(solution)/shard_map/all_gather | solution.py:378
  300.1 12.1 %multiply_convert_fusion.1 = (bf16[2048,512]{0,1:T(8,128)(2,1)S(1)}, bf16[2048,512]{0,1:T(8,128)(2,1)S(1)}) fusion(f32[2048,1024]{0,1:T(8,128)} %copy-done.5, bf16[2048,2048]{1,0:T(8,128)(2,1)} %get-tuple-element.704, bf16[512,2048]{1,0:T(8,128)(2,1)} %all-gather.11.cloned.1.call-done), kind=kOutput, calls=%fused_computation.178 | convolution fusion | flops 4308598784 | bytes 23068672 | tf_op jit(solution)/shard_map/dot_general | solution.py:26
  322.3 12.8 %convolution_convert_fusion.7 = bf16[2048,1024]{1,0:T(8,128)(2,1)} fusion(bf16[2048,2048]{1,0:T(8,128)(2,1)} %get-tuple-element.703, bf16[2048,512]{0,1:T(8,128)(2,1)S(1)} %get-tuple-element.620, bf16[2048,512]{0,1:T(8,128)(2,1)S(1)} %get-tuple-element.621), kind=kOutput, calls=%fused_computation.183 | convolution fusion | flops 8600420352 | bytes 16777216 | tf_op jit(solution)/shard_map/dot_general | solution.py:20
  354.5 57.3 %conditional.16 = (f32[128,2048]{1,0:T(8,128)S(1)}, bf16[128,2048]{1,0:T(8,128)(2,1)}) conditional(s32[]{:T(128)} %convert_element_type.295, () %tuple.136, (bf16[128,2048]{1,0:T(8,128)(2,1)S(1)}, f32[128,1]{0,1:T(1,128)}, f32[128,1]{0,1:T(1,128)S(1)}, bf16[512,2048]{1,0:T(8,128)(2,1)S(1)}, bf16[128,2048]{1,0:T(8,128)(2,1)S(1)}, ...), branch_computations={%region_15.16_spmd, %region_16.18_spmd} | conditional | flops 21234176 | bytes 86513176 | solution.py:256
  374.3 16.0 %collective-permute-done.30 = bf16[128,2048]{1,0:T(8,128)(2,1)S(1)} collective-permute-done((bf16[128,2048]{1,0:T(8,128)(2,1)S(1)}, bf16[128,2048]{1,0:T(8,128)(2,1)S(1)}, u32[]{:S(2)}, u32[]{:S(2)}) %collective-permute-start.30) | collective-permute-done | bytes 524320 | tf_op jit(solution)/shard_map/cond/branch_1_fun/ppermute | solution.py:243
  417.1 48.4 %conditional.17 = (bf16[1024,2048]{1,0:T(8,128)(2,1)}, f32[128,2048]{1,0:T(8,128)S(1)}, f32[128,2048]{1,0:T(8,128)}) conditional(s32[]{:T(128)} %convert_element_type.295, () %tuple.135, (f32[128,2048]{1,0:T(8,128)S(1)}, bf16[512,2048]{1,0:T(8,128)(2,1)S(1)}, bf16[512,2048]{1,0:T(8,128)(2,1)}) %tuple.288), branch_computations={%region_19.20_spmd, %region_20.21_spmd} | conditional | flops 8126464 | bytes 64487796 | solution.py:256
  429.0 11.8 %collective-permute-done.42 = bf16[128,2048]{1,0:T(8,128)(2,1)S(1)} collective-permute-done((bf16[128,2048]{1,0:T(8,128)(2,1)S(1)}, bf16[128,2048]{1,0:T(8,128)(2,1)S(1)}, u32[]{:S(2)}, u32[]{:S(2)}) %collective-permute-start.42) | collective-permute-done | bytes 524320 | tf_op jit(solution)/shard_map/cond/branch_1_fun/ppermute | solution.py:247
  449.2 12.3 %collective-permute-done.45 = bf16[128,2048]{1,0:T(8,128)(2,1)S(1)} collective-permute-done((bf16[128,2048]{1,0:T(8,128)(2,1)S(1)}, bf16[128,2048]{1,0:T(8,128)(2,1)S(1)}, u32[]{:S(2)}, u32[]{:S(2)}) %collective-permute-start.45) | collective-permute-done | bytes 524320 | tf_op jit(solution)/shard_map/cond/branch_1_fun/ppermute | solution.py:247
  466.4 38.4 %conditional.18 = (bf16[1024,768]{1,0:T(8,128)(2,1)}, bf16[2,256,1024]{2,1,0:T(8,128)(2,1)}, bf16[2,256,1024]{2,1,0:T(8,128)(2,1)}, bf16[2048,768]{0,1:T(8,128)(...) conditional(s32[]{:T(128)} %convert_element_type.295, ...), branch_computations={%region_21.22_spmd, %region_22.23_spmd} | conditional | flops 6982467584 | bytes 49812020 | solution.py:256
  479.1 12.4 %attend_back.1 = bf16[1024,768]{1,0:T(8,128)(2,1)} custom-call(bf16[1024,512]{1,0:T(8,128)(2,1)} %get-tuple-element.236.turned_ref, bf16[1024,768]{1,0:T(8,128)(2,1)} %get-tuple-element.237.values_ref, bf16[1024,256]{1,0:T(8,128)(2,1)S(1)} %convolution_convert_fusion.4.grad_ref, f32[512,128]{1,0:T(8,128)S(1)} %copy.25.cosine_ref, ...), custom_call_target="tpu_custom_call" | custom-call | flops 2684354560 | bytes 4194304 | tf_op jit(solution)/shard_map/cond/branch_1_fun/attend_back/pallas_call | solution.py:714
  495.5 7.8 %fusion.8 = bf16[2048,768]{0,1:T(8,128)(2,1)} fusion(bf16[1024,768]{1,0:T(8,128)(2,1)} %attend_back.1, bf16[1024,2048]{1,0:T(8,128)(2,1)} %get-tuple-element.254), kind=kOutput, calls=%fused_computation.142 | convolution fusion | flops 3222798336 | bytes 8912896 | tf_op jit(solution)/shard_map/cond/branch_1_fun/dot_general | solution.py:20
  514.9 69.4 %conditional.19 = (f32[128,2048]{1,0:T(8,128)}) conditional(s32[]{:T(128)} %convert_element_type.295, () %tuple.162, (f32[128]{0:T(128)S(1)}, f32[128,1]{0,1:T(1,128)S(1)}, bf16[1024,768]{1,0:T(8,128)(2,1)}, bf16[2048,768]{1,0:T(8,128)(2,1)}, f32[128,2048]{1,0:T(8,128)S(1)}, /*index=5*/f32[128,2048]{1,0:T(8,128)}) %tuple.286), branch_computations={%region_24.25_spmd, %region_25.27_spmd} | conditional | flops 3231973888 | bytes 61871340 | solution.py:256
  526.4 46.0 %collective-permute-done.59 = bf16[128,2048]{1,0:T(8,128)(2,1)S(1)} collective-permute-done((bf16[128,2048]{1,0:T(8,128)(2,1)S(1)}, bf16[128,2048]{1,0:T(8,128)(2,1)S(1)}, u32[]{:S(2)}, u32[]{:S(2)}) %collective-permute-start.59) | collective-permute-done | bytes 524320 | tf_op jit(solution)/shard_map/cond/branch_1_fun/ppermute | solution.py:247
  599.5 15.8 %merge_wide.1 = (f32[256,16384]{1,0:T(8,128)}, f32[4,256,128]{2,1,0:T(8,128)S(1)}) custom-call(s32[3]{0:T(128)S(1)} %copy-done.33, bf16[4,256,1024]{2,1,0:T(8,128)(2,1)} %constant_dynamic-update-slice_fusion.68.refs_0_, bf16[4,256,1024]{2,1,0:T(8,128)(2,1)} %collective-permute-done.73.refs_1_, ...), custom_call_target="tpu_custom_call" | custom-call | tf_op jit(solution)/shard_map/merge_wide/pallas_call | solution.py:504
  627.6 11.7 %collective-permute-done.80.refs_3_ = bf16[2,256,768]{2,1,0:T(8,128)(2,1)S(1)} collective-permute-done((bf16[2,256,768]{2,1,0:T(8,128)(2,1)S(1)}, bf16[2,256,768]{2,1,0:T(8,128)(2,1)S(1)}, u32[]{:S(2)}, u32[]{:S(2)}) %collective-permute-start.80) | collective-permute-done | bytes 786464 | tf_op jit(solution)/shard_map/ppermute | solution.py:247
  648.1 9.0 %merge_heads.1 = (f32[256,6144]{1,0:T(8,128)}, f32[2,256,128]{2,1,0:T(8,128)}) custom-call(s32[3]{0:T(128)S(1)} %copy-done.33, bf16[2,256,768]{2,1,0:T(8,128)(2,1)} %copy-done.13, bf16[2,256,768]{2,1,0:T(8,128)(2,1)} %collective-permute-done.79.refs_1_, bf16[2,256,768]{2,1,0:T(8,128)(2,1)} %copy-done.23, bf16[2,256,768]{2,1,0:T(8,128)(2,1)} %copy-done.27, ...), custom_call_target="tpu_custom_call" | custom-call | tf_op jit(solution)/shard_map/merge_heads/pallas_call | solution.py:571
  (500 shorter events, 410.3 us)
Async XLA Ops:
  7.2 78.7 %all-gather.5.cloned.1.call-start = ((), (), s32[]{:S(2)}) async-start(), calls=%async_computation.4 | async-start | bytes 3932160 | tf_op jit(solution)/shard_map/all_gather | solution.py:378
  17.8 94.5 %all-gather.7.cloned.1.call-start = ((), (), s32[]{:S(2)}) async-start(), calls=%async_computation.5 | async-start | bytes 1310720 | tf_op jit(solution)/shard_map/all_gather | solution.py:378
  18.7 245.7 %all-gather.9.cloned.1.call-start = ((), (), s32[]{:S(2)}) async-start(), calls=%async_computation.6 | async-start | bytes 6291456 | tf_op jit(solution)/shard_map/all_gather | solution.py:378
  112.3 71.0 %collective-permute-start.64 = (bf16[512,1024]{1,0:T(8,128)(2,1)}, bf16[512,1024]{1,0:T(8,128)(2,1)}, u32[]{:S(2)}, u32[]{:S(2)}) collective-permute-start(bf16[512,1024]{1,0:T(8,128)(2,1)} %get-tuple-element.402), channel_id=1, source_target_pairs={{0,4},{1,5},{2,6},{3,7},{4,0},{5,1},{6,2},{7,3},{8,12},{9,13},{10,... | collective-permute-start | bytes 3145736 | tf_op jit(solution)/shard_map/ppermute | solution.py:243
  153.9 29.4 %collective-permute-start.65 = (bf16[128,2048]{1,0:T(8,128)(2,1)}, bf16[128,2048]{1,0:T(8,128)(2,1)S(1)}, u32[]{:S(2)}, u32[]{:S(2)}) collective-permute-start(bf16[128,2048]{1,0:T(8,128)(2,1)} %get-tuple-element.403), channel_id=1, source_target_pairs={{0,4},{1,5},{2,6},{3,7},{4,0},{5,1},{6,2},{7,3},{8,12},{9,13},{10,... | collective-permute-start | bytes 1572872 | tf_op jit(solution)/shard_map/ppermute | solution.py:243
  186.2 113.9 %all-gather.11.cloned.1.call-start = ((), (), s32[]{:S(2)}) async-start(), calls=%async_computation.7 | async-start | bytes 3145728 | tf_op jit(solution)/shard_map/all_gather | solution.py:378
  186.2 35.8 %collective-permute-start.67 = (bf16[128,2048]{1,0:T(8,128)(2,1)S(1)}, bf16[128,2048]{1,0:T(8,128)(2,1)S(1)}, u32[]{:S(2)}, u32[]{:S(2)}) collective-permute-start(bf16[128,2048]{1,0:T(8,128)(2,1)S(1)} %bitcast.82), channel_id=1, source_target_pairs={{0,4},{1,5},{2,6},{3,7},{4,0},{5,1},{6,2},{7,3},{8,12},{9,13},{10,... | collective-permute-start | bytes 1572872 | tf_op jit(solution)/shard_map/ppermute | solution.py:243
  188.0 65.1 %collective-permute-start.66 = (bf16[128,2048]{1,0:T(8,128)(2,1)S(1)}, bf16[128,2048]{1,0:T(8,128)(2,1)}, u32[]{:S(2)}, u32[]{:S(2)}) collective-permute-start(bf16[128,2048]{1,0:T(8,128)(2,1)S(1)} %constant_dynamic-slice_fusion.5), channel_id=1, source_target_pairs={{0,4},{1,5},{2,6},{3,7},{4,0},{5,1},{6,2},{7,3},{8,12},{9,13},{10,... | collective-permute-start | bytes 1572872 | tf_op jit(solution)/shard_map/ppermute | solution.py:243
  255.6 79.4 %reduce-scatter.5.cloned.1.call-start = ((), (), s32[]{:S(2)}) async-start(), calls=%async_computation.8 | async-start | bytes 3145728 | tf_op jit(solution)/shard_map/reduce_scatter | solution.py:382
  291.6 120.3 %reduce-scatter.7.cloned.1.call-start = ((), (), s32[]{:S(2)}) async-start(), calls=%async_computation.9 | async-start | bytes 6291456 | tf_op jit(solution)/shard_map/reduce_scatter | solution.py:382
  335.1 249.2 %reduce-scatter.9.cloned.1.call-start = ((), (), s32[]{:S(2)}) async-start(), calls=%async_computation.10 | async-start | bytes 3932160 | tf_op jit(solution)/shard_map/reduce_scatter | solution.py:382
  365.0 25.3 %collective-permute-start.30 = (bf16[128,2048]{1,0:T(8,128)(2,1)S(1)}, bf16[128,2048]{1,0:T(8,128)(2,1)S(1)}, u32[]{:S(2)}, u32[]{:S(2)}) collective-permute-start(bf16[128,2048]{1,0:T(8,128)(2,1)S(1)} %pad_maximum_fusion.14), channel_id=1, source_target_pairs={{0,4},{1,5},{2,6},{3,7},{4,0},{5,1},{6,2},{7,3},{8,12},{9,13},{10,... | collective-permute-start | bytes 1572872 | tf_op jit(solution)/shard_map/cond/branch_1_fun/ppermute | solution.py:243
  371.8 22.0 %collective-permute-start.33 = (bf16[128,2048]{1,0:T(8,128)(2,1)S(1)}, bf16[128,2048]{1,0:T(8,128)(2,1)S(1)}, u32[]{:S(2)}, u32[]{:S(2)}) collective-permute-start(bf16[128,2048]{1,0:T(8,128)(2,1)S(1)} %get-tuple-element.570), channel_id=1, source_target_pairs={{0,16},{8,24},{16,0},{24,8},{1,17},{9,25},{17,1},{25,9},{2,18},{10... | collective-permute-start | bytes 1572872 | tf_op jit(solution)/shard_map/cond/branch_1_fun/ppermute | solution.py:247
  373.1 22.0 %collective-permute-start.34 = (bf16[128,2048]{1,0:T(8,128)(2,1)S(1)}, bf16[128,2048]{1,0:T(8,128)(2,1)S(1)}, u32[]{:S(2)}, u32[]{:S(2)}) collective-permute-start(bf16[128,2048]{1,0:T(8,128)(2,1)S(1)} %get-tuple-element.569), channel_id=1, source_target_pairs={{0,8},{8,0},{16,24},{24,16},{1,9},{9,1},{17,25},{25,17},{2,10},{10... | collective-permute-start | bytes 1572872 | tf_op jit(solution)/shard_map/cond/branch_1_fun/ppermute | solution.py:247
  414.6 50.9 %collective-permute-start.71 = (bf16[512,1024]{1,0:T(8,128)(2,1)}, bf16[512,1024]{1,0:T(8,128)(2,1)}, u32[]{:S(2)}, u32[]{:S(2)}) collective-permute-start(bf16[512,1024]{1,0:T(8,128)(2,1)} %constant_dynamic-slice_fusion.4), channel_id=1, source_target_pairs={{0,4},{1,5},{2,6},{3,7},{4,0},{5,1},{6,2},{7,3},{8,12},{9,13},{10,... | collective-permute-start | bytes 3145736 | tf_op jit(solution)/shard_map/ppermute | solution.py:243
  473.0 31.8 %collective-permute-start.56 = (bf16[2,256,1024]{2,1,0:T(8,128)(2,1)}, bf16[2,256,1024]{2,1,0:T(8,128)(2,1)}, u32[]{:S(2)}, u32[]{:S(2)}) collective-permute-start(bf16[2,256,1024]{2,1,0:T(8,128)(2,1)} %pad_maximum_fusion.18), channel_id=1, source_target_pairs={{0,8},{8,0},{16,24},{24,16},{1,9},{9,1},{17,25},{25,17},{2,10},{10... | collective-permute-start | bytes 3145736 | tf_op jit(solution)/shard_map/cond/branch_1_fun/ppermute | solution.py:247
  473.6 31.1 %collective-permute-start.57 = (bf16[2,256,1024]{2,1,0:T(8,128)(2,1)}, bf16[2,256,1024]{2,1,0:T(8,128)(2,1)}, u32[]{:S(2)}, u32[]{:S(2)}) collective-permute-start(bf16[2,256,1024]{2,1,0:T(8,128)(2,1)} %collective-permute-done.52), channel_id=1, source_target_pairs={{0,16},{8,24},{16,0},{24,8},{1,17},{9,25},{17,1},{25,9},{2,18},{10... | collective-permute-start | bytes 3145736 | tf_op jit(solution)/shard_map/cond/branch_1_fun/ppermute | solution.py:247
  474.3 29.1 %collective-permute-start.53 = (bf16[128,2048]{1,0:T(8,128)(2,1)S(1)}, bf16[128,2048]{1,0:T(8,128)(2,1)}, u32[]{:S(2)}, u32[]{:S(2)}) collective-permute-start(bf16[128,2048]{1,0:T(8,128)(2,1)S(1)} %copy-done.28), channel_id=1, source_target_pairs={{0,4},{1,5},{2,6},{3,7},{4,0},{5,1},{6,2},{7,3},{8,12},{9,13},{10,... | collective-permute-start | bytes 1572872 | tf_op jit(solution)/shard_map/cond/branch_1_fun/ppermute | solution.py:243
  504.9 136.9 %reduce-scatter.11.cloned.1.call-start = ((), (), s32[]{:S(2)}) async-start(), calls=%async_computation.11 | async-start | bytes 1310720 | tf_op jit(solution)/shard_map/reduce_scatter | solution.py:382
  508.2 88.6 %collective-permute-start.74 = (bf16[4,256,1024]{2,1,0:T(8,128)(2,1)S(1)}, bf16[4,256,1024]{2,1,0:T(8,128)(2,1)}, u32[]{:S(2)}, u32[]{:S(2)}) collective-permute-start(bf16[4,256,1024]{2,1,0:T(8,128)(2,1)S(1)} %constant_dynamic-update-slice_fusion.70.refs_2_), channel_id=1, source_target_pairs={{0,8},{8,0},{16,24},{24,16},{1,9},{9,1},{17,25},{25,17},{2,10},{10... | collective-permute-start | bytes 6291464 | tf_op jit(solution)/shard_map/ppermute | solution.py:247
  514.6 84.9 %collective-permute-start.73 = (bf16[4,256,1024]{2,1,0:T(8,128)(2,1)}, bf16[4,256,1024]{2,1,0:T(8,128)(2,1)}, u32[]{:S(2)}, u32[]{:S(2)}) collective-permute-start(bf16[4,256,1024]{2,1,0:T(8,128)(2,1)} %constant_dynamic-update-slice_fusion.68.refs_0_), channel_id=1, source_target_pairs={{0,16},{8,24},{16,0},{24,8},{1,17},{9,25},{17,1},{25,9},{2,18},{10... | collective-permute-start | bytes 6291464 | tf_op jit(solution)/shard_map/ppermute | solution.py:247
  524.3 48.2 %collective-permute-start.59 = (bf16[128,2048]{1,0:T(8,128)(2,1)S(1)}, bf16[128,2048]{1,0:T(8,128)(2,1)S(1)}, u32[]{:S(2)}, u32[]{:S(2)}) collective-permute-start(bf16[128,2048]{1,0:T(8,128)(2,1)S(1)} %get-tuple-element.605), channel_id=1, source_target_pairs={{0,16},{8,24},{16,0},{24,8},{1,17},{9,25},{17,1},{25,9},{2,18},{10... | collective-permute-start | bytes 1572872 | tf_op jit(solution)/shard_map/cond/branch_1_fun/ppermute | solution.py:247
  526.0 46.4 %collective-permute-start.60 = (bf16[128,2048]{1,0:T(8,128)(2,1)S(1)}, bf16[128,2048]{1,0:T(8,128)(2,1)S(1)}, u32[]{:S(2)}, u32[]{:S(2)}) collective-permute-start(bf16[128,2048]{1,0:T(8,128)(2,1)S(1)} %get-tuple-element.604), channel_id=1, source_target_pairs={{0,8},{8,0},{16,24},{24,16},{1,9},{9,1},{17,25},{25,17},{2,10},{10... | collective-permute-start | bytes 1572872 | tf_op jit(solution)/shard_map/cond/branch_1_fun/ppermute | solution.py:247
  594.3 23.3 %collective-permute-start.75 = (bf16[1,256,768]{2,1,0:T(8,128)(2,1)}, bf16[1,256,768]{2,1,0:T(8,128)(2,1)S(1)}, u32[]{:S(2)}, u32[]{:S(2)}) collective-permute-start(bf16[1,256,768]{2,1,0:T(8,128)(2,1)} %bitcast.26), channel_id=1, source_target_pairs={{0,8},{8,0},{16,24},{24,16},{1,9},{9,1},{17,25},{25,17},{2,10},{10... | collective-permute-start | bytes 1179656 | tf_op jit(solution)/shard_map/ppermute | solution.py:247
  595.4 23.3 %collective-permute-start.77 = (bf16[128,2048]{1,0:T(8,128)(2,1)}, bf16[128,2048]{1,0:T(8,128)(2,1)S(1)}, u32[]{:S(2)}, u32[]{:S(2)}) collective-permute-start(bf16[128,2048]{1,0:T(8,128)(2,1)} %get-tuple-element.459), channel_id=1, source_target_pairs={{0,8},{8,0},{16,24},{24,16},{1,9},{9,1},{17,25},{25,17},{2,10},{10... | collective-permute-start | bytes 1572872 | tf_op jit(solution)/shard_map/ppermute | solution.py:247
  596.3 22.4 %collective-permute-start.78 = (bf16[128,2048]{1,0:T(8,128)(2,1)}, bf16[128,2048]{1,0:T(8,128)(2,1)S(1)}, u32[]{:S(2)}, u32[]{:S(2)}) collective-permute-start(bf16[128,2048]{1,0:T(8,128)(2,1)} %get-tuple-element.468), channel_id=1, source_target_pairs={{0,16},{8,24},{16,0},{24,8},{1,17},{9,25},{17,1},{25,9},{2,18},{10... | collective-permute-start | bytes 1572872 | tf_op jit(solution)/shard_map/ppermute | solution.py:247
  596.8 21.9 %collective-permute-start.76 = (bf16[1,256,768]{2,1,0:T(8,128)(2,1)}, bf16[1,256,768]{2,1,0:T(8,128)(2,1)S(1)}, u32[]{:S(2)}, u32[]{:S(2)}) collective-permute-start(bf16[1,256,768]{2,1,0:T(8,128)(2,1)} %collective-permute-done.72), channel_id=1, source_target_pairs={{0,16},{8,24},{16,0},{24,8},{1,17},{9,25},{17,1},{25,9},{2,18},{10... | collective-permute-start | bytes 1179656 | tf_op jit(solution)/shard_map/ppermute | solution.py:247
  622.1 39.2 %collective-permute-start.83 = (bf16[256,2048]{1,0:T(8,128)(2,1)S(1)}, bf16[256,2048]{1,0:T(8,128)(2,1)S(1)}, u32[]{:S(2)}, u32[]{:S(2)}) collective-permute-start(bf16[256,2048]{1,0:T(8,128)(2,1)S(1)} %constant_dynamic-update-slice_fusion.76.refs_2_), channel_id=1, source_target_pairs={{0,8},{8,0},{16,24},{24,16},{1,9},{9,1},{17,25},{25,17},{2,10},{10... | collective-permute-start | bytes 3145736 | tf_op jit(solution)/shard_map/ppermute | solution.py:247
  622.8 40.7 %collective-permute-start.82 = (bf16[256,2048]{1,0:T(8,128)(2,1)S(1)}, bf16[256,2048]{1,0:T(8,128)(2,1)}, u32[]{:S(2)}, u32[]{:S(2)}) collective-permute-start(bf16[256,2048]{1,0:T(8,128)(2,1)S(1)} %constant_dynamic-update-slice_fusion.72.refs_0_), channel_id=1, source_target_pairs={{0,16},{8,24},{16,0},{24,8},{1,17},{9,25},{17,1},{25,9},{2,18},{10... | collective-permute-start | bytes 3145736 | tf_op jit(solution)/shard_map/ppermute | solution.py:247
  625.2 31.9 %collective-permute-start.81 = (bf16[128,2048]{1,0:T(8,128)(2,1)}, bf16[128,2048]{1,0:T(8,128)(2,1)}, u32[]{:S(2)}, u32[]{:S(2)}) collective-permute-start(bf16[128,2048]{1,0:T(8,128)(2,1)} %get-tuple-element.477), channel_id=1, source_target_pairs={{0,4},{1,5},{2,6},{3,7},{4,0},{5,1},{6,2},{7,3},{8,12},{9,13},{10,... | collective-permute-start | bytes 1572872 | tf_op jit(solution)/shard_map/ppermute | solution.py:243
  642.8 20.8 %collective-permute-start.84 = (bf16[32,2048]{1,0:T(8,128)(2,1)S(1)}, bf16[32,2048]{1,0:T(8,128)(2,1)S(1)}, u32[]{:S(2)}, u32[]{:S(2)}) collective-permute-start(bf16[32,2048]{1,0:T(8,128)(2,1)S(1)} %get-tuple-element.639), channel_id=1, source_target_pairs={{0,8},{8,0},{16,24},{24,16},{1,9},{9,1},{17,25},{25,17},{2,10},{10... | collective-permute-start | bytes 393224 | tf_op jit(solution)/shard_map/ppermute | solution.py:247
  643.7 21.2 %collective-permute-start.85 = (bf16[32,2048]{1,0:T(8,128)(2,1)S(1)}, bf16[32,2048]{1,0:T(8,128)(2,1)}, u32[]{:S(2)}, u32[]{:S(2)}) collective-permute-start(bf16[32,2048]{1,0:T(8,128)(2,1)S(1)} %get-tuple-element.638), channel_id=1, source_target_pairs={{0,16},{8,24},{16,0},{24,8},{1,17},{9,25},{17,1},{25,9},{2,18},{10... | collective-permute-start | bytes 393224 | tf_op jit(solution)/shard_map/ppermute | solution.py:247
  (114 other events, 1142.4 us)
Sparse Core Ops, SparseCore 0:
  18.0 66.1 all-gather.4
  85.7 26.5 all-gather.6
  186.3 78.0 all-gather.8
  266.4 33.6 all-gather.10
  302.1 31.8 reduce-scatter.4
  336.3 65.5 reduce-scatter.6
  505.0 59.3 reduce-scatter.8
  593.3 26.3 reduce-scatter.10
